TPU v7x, 256 devices: a whole 4x4x8 slice. The times are simulated.
256 devices in a mesh: seq: 32 (over y, z), head: 8 (over x, core).
Axes of the slice: x: 4, y: 4, z: 8, core: 2. Of those that a mesh axis runs over, the one named last changes fastest.
Arguments:
- query: bfloat16 [16384, 8192], P('seq', 'head'), may hold values from -1.5 to 1.5
- key_in: bfloat16 [16384, 8192], P('seq', 'head'), may hold values from -0.5 to 0.5
- value: bfloat16 [16384, 8192], P('seq', 'head'), may hold values from -6 to 6
- gate: bfloat16 [16384, 8192], P(('seq', 'head')), may hold values from -6 to 6
- gain: float32 [8192], replicated, may hold values from 0.5 to 1.5
- grad_out: bfloat16 [16384, 8192], P(('seq', 'head')), may hold values from -6 to 6
Outputs:
- grad_query: bfloat16 [16384, 8192], P('seq', 'head')
- grad_key: bfloat16 [16384, 8192], P('seq', 'head')
- grad_value: bfloat16 [16384, 8192], P('seq', 'head')
- grad_gate: bfloat16 [16384, 8192], P(('seq', 'head'))
All inputs are finite; a program needn't handle non-finite values.
Results may differ from a plain program's by a relative error of at most 0.012.
Values may be sent and summed in bfloat16 or wider, within the bound.
No kernel may reach another device: no remote copies, remote signals or barrier semaphores. Data moves between devices by JAX's collectives and lax.ppermute only.
A program may use at most 128 MiB of HBM per device.

v0:
```python
import jax
import jax.numpy as jnp
from jax import lax
from jax.sharding import PartitionSpec as P

HEAD_DIM = 128


def carried_in(value, axis, combine, identity, reverse):
    peers, place = (lax.axis_size(axis), lax.axis_index(axis))
    everything = lax.all_gather(value.astype(jnp.bfloat16), axis)
    start = jnp.broadcast_to(jnp.asarray(identity, value.dtype), value.shape)

    def step(k, before):
        at = peers - 1 - k if reverse else k
        reached = at > place if reverse else at < place
        new = combine(before, everything[at].astype(value.dtype))
        return jnp.where(reached, new, before)

    return lax.fori_loop(0, peers, step, start)


def add_states(earlier, later_part):
    return earlier + later_part


def split_heads(matrix, head_dim):
    return matrix.reshape(matrix.shape[0], matrix.shape[1] // head_dim, head_dim)


def on_device(query, key_in, value, gate, gain, grad_out):
    head_dim = HEAD_DIM
    tok_here = query.shape[0]
    queries = split_heads(query, head_dim)
    keys_here = split_heads(key_in, head_dim)
    values_here = split_heads(value, head_dim)
    local_state = jnp.einsum(
        "thd,the->hde", keys_here, values_here, preferred_element_type=jnp.float32
    )
    zero_state = jnp.zeros_like(local_state)
    prefix = carried_in(local_state, "seq", add_states, zero_state, False)
    causal = jnp.tril(jnp.ones((tok_here, tok_here), dtype=bool))
    scores = jnp.einsum("thd,shd->hts", queries, keys_here, preferred_element_type=jnp.float32)
    masked_scores = jnp.where(causal[None], scores, 0.0).astype(jnp.bfloat16)
    prefix_low = prefix.astype(jnp.bfloat16)
    attn_out = jnp.einsum(
        "hts,she->the", masked_scores, values_here, preferred_element_type=jnp.float32
    )
    attn_out = attn_out + jnp.einsum(
        "thd,hde->the", queries, prefix_low, preferred_element_type=jnp.float32
    )
    attn_out = attn_out.astype(jnp.bfloat16).reshape(tok_here, -1)
    token_rows = lax.all_to_all(attn_out, "head", split_axis=0, concat_axis=1, tiled=True)
    rows_wide = token_rows.astype(jnp.float32)
    inv_rms = lax.rsqrt(jnp.mean(rows_wide * rows_wide, axis=1, keepdims=True) + 1e-06)
    normed = rows_wide * inv_rms
    gate_wide = gate.astype(jnp.float32)
    sigmoid_gate = jax.nn.sigmoid(gate_wide)
    scaled = grad_out.astype(jnp.float32) * gain[None, :]
    grad_gate = (scaled * normed * sigmoid_gate * (1.0 + gate_wide * (1.0 - sigmoid_gate))).astype(
        jnp.bfloat16
    )
    weighted = scaled * gate_wide * sigmoid_gate
    grad_rows = inv_rms * (weighted - normed * jnp.mean(weighted * normed, axis=1, keepdims=True))
    grad_rows = grad_rows.astype(jnp.bfloat16)
    grad_heads = lax.all_to_all(grad_rows, "head", split_axis=1, concat_axis=0, tiled=True)
    grad_attn = split_heads(grad_heads, head_dim)
    local_grad = jnp.einsum("thd,the->hde", queries, grad_attn, preferred_element_type=jnp.float32)
    suffix = carried_in(local_grad, "seq", add_states, zero_state, True)
    suffix_low = suffix.astype(jnp.bfloat16)
    grad_scores = jnp.einsum(
        "the,she->hts", grad_attn, values_here, preferred_element_type=jnp.float32
    )
    grad_scores = jnp.where(causal[None], grad_scores, 0.0).astype(jnp.bfloat16)
    grad_query = jnp.einsum(
        "hts,shd->thd", grad_scores, keys_here, preferred_element_type=jnp.float32
    )
    grad_query = grad_query + jnp.einsum(
        "the,hde->thd", grad_attn, prefix_low, preferred_element_type=jnp.float32
    )
    grad_key = jnp.einsum("hts,thd->shd", grad_scores, queries, preferred_element_type=jnp.float32)
    grad_key = grad_key + jnp.einsum(
        "she,hde->shd", values_here, suffix_low, preferred_element_type=jnp.float32
    )
    grad_value = jnp.einsum(
        "hts,the->she", masked_scores, grad_attn, preferred_element_type=jnp.float32
    )
    grad_value = grad_value + jnp.einsum(
        "shd,hde->she", keys_here, suffix_low, preferred_element_type=jnp.float32
    )
    return (
        grad_query.astype(jnp.bfloat16).reshape(tok_here, -1),
        grad_key.astype(jnp.bfloat16).reshape(tok_here, -1),
        grad_value.astype(jnp.bfloat16).reshape(tok_here, -1),
        grad_gate,
    )


def solution(mesh):
    in_specs = (
        P("seq", "head"),
        P("seq", "head"),
        P("seq", "head"),
        P(("seq", "head"), None),
        P(),
        P(("seq", "head"), None),
    )
    out_specs = (P("seq", "head"), P("seq", "head"), P("seq", "head"), P(("seq", "head"), None))
    return jax.shard_map(
        on_device, mesh=mesh, in_specs=in_specs, out_specs=out_specs, check_vma=False
    )
```

profile of v0, /device:TPU:32, one launch (start us, length us, event | category | flops | bytes accessed | tf_op | source)
XLA Modules:
  0.0 358.9 jit_solution(4173324930574338439)
XLA Ops:
  7.2 1.6 copy.116
  11.2 2.5 select_convert_fusion.1
  13.8 1.9 copy-done.1
  15.7 2.6 fusion.16
  18.3 92.3 %all-gather.5.cloned.1.call-done = bf16[256,128,128]{2,1,0:T(8,128)(2,1)} async-done(((bf16[8,128,128]{2,1,0:T(8,128)(2,1)}), bf16[256,128,128]{2,1,0:T(8,128)(2,1)}) %all-gather.5.cloned.1.call-update) | async-done | bytes 8388624 | tf_op jit(solution)/shard_map/all_gather | solution.py:11
  110.6 40.3 %while.30 = (s32[]{:T(128)}, f32[8,128,128]{2,1,0:T(8,128)S(1)}, s32[]{:T(128)}, bf16[32,8,128,128]{3,2,1,0:T(8,128)(2,1)}, s32[]{:T(128)}, /*index=5*/s32[]{:T(128)}) while((s32[]{:T(128)}, f32[8,128,128]{2,1,0:T(8,128)S(1)}, s32[]{:T(128)}, bf16[32,8,128,128]{3,2,1,0:T(8,128)(2,1)}, s32[]{:T(128)}, /*index=5*/s32[]{:T(128)}) %tuple.90), condition=%wide.region_1.2_spmd.clone, body=%wide.region_0.1_spmd.clone.sunk | while | flops 524292 | bytes 1310821 | solution.py:20
  110.6 1.3 add_select_fusion.4
  113.2 1.2 add_select_fusion.4
  114.4 1.2 add_select_fusion.4
  115.7 1.2 add_select_fusion.4
  116.9 1.2 add_select_fusion.4
  118.2 1.2 add_select_fusion.4
  119.5 1.2 add_select_fusion.4
  122.0 1.2 add_select_fusion.4
  123.2 1.2 add_select_fusion.4
  124.5 1.2 add_select_fusion.4
  125.7 1.2 add_select_fusion.4
  128.3 1.2 add_select_fusion.4
  129.5 1.2 add_select_fusion.4
  130.8 1.2 add_select_fusion.4
  132.0 1.2 add_select_fusion.4
  133.3 1.2 add_select_fusion.4
  134.5 1.2 add_select_fusion.4
  137.1 1.2 add_select_fusion.4
  138.3 1.2 add_select_fusion.4
  139.6 1.2 add_select_fusion.4
  140.8 1.2 add_select_fusion.4
  142.1 1.2 add_select_fusion.4
  143.4 1.2 add_select_fusion.4
  145.9 1.2 add_select_fusion.4
  147.1 1.2 add_select_fusion.4
  148.4 1.2 add_select_fusion.4
  149.6 1.2 add_select_fusion.4
  150.9 2.0 fusion.10
  153.6 1.3 all_to_all.22
  154.9 20.4 %all_to_all.29 = bf16[8,64,1024]{2,1,0:T(8,128)(2,1)S(1)} all-to-all(bf16[8,64,1024]{2,1,0:T(8,128)(2,1)} %all_to_all.22), channel_id=1, replica_groups=mesh['seq'=32,'head'=8] {'head'}, dimensions={0} | all-to-all | bytes 2097152 | tf_op jit(solution)/shard_map/all_to_all | solution.py:53
  178.3 2.4 fusion.7
  180.8 18.5 %all_to_all.30 = bf16[64,8,1024]{2,0,1:T(8,128)(2,1)S(1)} all-to-all(bf16[64,8,1024]{2,0,1:T(8,128)(2,1)S(1)} %bitcast.119), channel_id=1, replica_groups=mesh['seq'=32,'head'=8] {'head'}, dimensions={1} | all-to-all | bytes 2097152 | tf_op jit(solution)/shard_map/all_to_all | solution.py:66
  199.3 1.2 copy.117
  200.5 1.6 copy.98
  202.2 1.7 fusion.11
  204.8 1.4 select_convert_fusion
  206.2 1.5 fusion.38
  208.2 1.4 fusion.9
  209.6 2.3 copy.105
  211.8 4.3 %fusion.39 = f32[8,128,512]{2,1,0:T(8,128)} fusion(bf16[512,8,128]{0,2,1:T(8,128)(2,1)S(1)} %copy.98, bf16[8,512,512]{2,1,0:T(8,128)(2,1)} %copy-done.1), kind=kOutput, calls=%fused_computation.61 | convolution fusion | flops 536870912 | bytes 7340032 | tf_op jit(solution)/shard_map/hts,the->she/dot_general | solution.py:85
  216.1 82.5 %all-gather.7.cloned.1.call-done = bf16[256,128,128]{2,1,0:T(8,128)(2,1)} async-done(((bf16[8,128,128]{2,1,0:T(8,128)(2,1)}), bf16[256,128,128]{2,1,0:T(8,128)(2,1)}) %all-gather.7.cloned.1.call-update) | async-done | bytes 8388624 | tf_op jit(solution)/shard_map/all_gather | solution.py:11
  298.7 40.4 %while.31 = (s32[]{:T(128)}, f32[8,128,128]{2,1,0:T(8,128)S(1)}, s32[]{:T(128)}, bf16[32,8,128,128]{3,2,1,0:T(8,128)(2,1)}, s32[]{:T(128)}, /*index=5*/s32[]{:T(128)}, s32[]{:T(128)}, s32[]{:T(128)}) while((s32[]{:T(128)}, f32[8,128,128]{2,1,0:T(8,128)S(1)}, s32[]{:T(128)}, bf16[32,8,128,128]{3,2,1,0:T(8,128)(2,1)}, s32[]{:T(128)}, ...), condition=%wide.region_5.6_spmd.clone, body=%wide.region_4.5_spmd.clone.sunk | while | flops 524296 | bytes 1310883 | solution.py:20
  301.2 1.2 add_select_fusion.5
  302.4 1.2 add_select_fusion.5
  303.7 1.2 add_select_fusion.5
  305.0 1.2 add_select_fusion.5
  306.2 1.2 add_select_fusion.5
  307.5 1.2 add_select_fusion.5
  308.7 1.2 add_select_fusion.5
  310.0 1.2 add_select_fusion.5
  311.3 1.2 add_select_fusion.5
  312.5 1.2 add_select_fusion.5
  315.1 1.2 add_select_fusion.5
  339.0 1.8 fusion.12
  341.6 1.5 add_convert_fusion
  343.1 2.4 copy.107
  345.5 4.3 %fusion.8 = bf16[512,8,128]{0,2,1:T(8,128)(2,1)} fusion(f32[8,128,512]{2,1,0:T(8,128)S(1)} %copy-done.4, bf16[8,512,512]{2,1,0:T(8,128)(2,1)} %copy-done.2, bf16[512,1024]{1,0:T(8,128)(2,1)} %param.10), kind=kOutput, calls=%fused_computation.18 | convolution fusion | flops 537919488 | bytes 8388608 | tf_op jit(solution)/shard_map/hts,thd->shd/dot_general | solution.py:81
  349.8 2.3 copy.106
  (69 shorter events, 40.5 us)
Async XLA Ops:
  7.2 2.3 copy-start
  7.2 103.4 %all-gather.5.cloned.1.call-start = ((), (), s32[]{:S(2)}) async-start(), calls=%async_computation.2 | async-start | bytes 8650752 | tf_op jit(solution)/shard_map/all_gather | solution.py:11
  9.5 1.3 copy-start.5
  9.5 1.7 copy-start.9
  10.7 288.0 %all-gather.7.cloned.1.call-start = ((), (), s32[]{:S(2)}) async-start(), calls=%async_computation.3 | async-start | bytes 8650752 | tf_op jit(solution)/shard_map/all_gather | solution.py:11
  13.7 1.9 copy-start.1
  110.6 40.3 %copy-start.11 = (bf16[512,1024]{1,0:T(8,128)(2,1)S(1)}, bf16[512,1024]{1,0:T(8,128)(2,1)}, u32[]{:S(2)}) copy-start(bf16[512,1024]{1,0:T(8,128)(2,1)} %param.10) | copy-start | bytes 3145732
  175.8 1.2 copy-start.7
  175.8 1.5 copy-start.8
  175.8 1.5 copy-start.12
  204.7 1.4 copy-start.6
  206.2 2.0 copy-start.2
  339.0 1.9 copy-start.3
  339.0 2.6 copy-start.10
  343.1 2.4 copy-start.4
Sparse Core Ops, SparseCore 0:
  11.2 99.3 all-gather.4
  204.9 93.7 all-gather.6
where the time goes:
time: 364 us; the launch traced here: 359 us
  waiting for transfers between devices  175 us (48%)
  other arithmetic  83.1 us (23%)
  blocking collectives  38.9 us (11%)
  matrix products  26.1 us (7%)
  local copies, waits for them, and re-layouts  20.1 us (6%)
  between operations  14.3 us (4%)
    all_gather x2, waiting for transfers between devices, carried_in(): everything = lax.all_gather(value.astype(jnp.bfloat16), axis)  175 us
    select_n x64, other arithmetic, step(): return jnp.where(reached, new, before)  79.1 us
    all_to_all x1, blocking collectives, on_device(): lax.all_to_all(attn_out, 'head', split_axis=0, concat_axis=1, tiled=True)  20.4 us
    all_to_all x1, blocking collectives, on_device(): lax.all_to_all(grad_rows, 'head', split_axis=1, concat_axis=0, tiled=True)  18.5 us
    unnamed x31, local copies, waits for them, and re-layouts  14.7 us
  transfers between devices with their start and end apart: 2, of which 2 were waited for; matrix products, arithmetic and copies ran while one was open for 4% of the time, Pallas kernels for 0%

commit v1 on v0

v1 whole, which is shorter than its diff:
```python
import functools

import jax
import jax.numpy as jnp
from jax import lax
from jax.experimental import pallas as pl
from jax.experimental.pallas import tpu as pltpu
from jax.sharding import PartitionSpec as P

HEAD_DIM = 128
EPS = 1e-06
F32 = jnp.float32
BF16 = jnp.bfloat16


def mm(a, b):
    return lax.dot_general(a, b, (((1,), (0,)), ((), ())), preferred_element_type=F32)


def mm_bt(a, b):
    return lax.dot_general(a, b, (((1,), (1,)), ((), ())), preferred_element_type=F32)


def mm_at(a, b):
    return lax.dot_general(a, b, (((0,), (0,)), ((), ())), preferred_element_type=F32)


def call(kernel, out_shape, grid, in_specs, out_specs, flops, nbytes, name):
    specs = dict(grid=grid, in_specs=in_specs, out_specs=out_specs) if grid else {}
    return pl.pallas_call(
        kernel,
        out_shape=out_shape,
        **specs,
        compiler_params=pltpu.CompilerParams(vmem_limit_bytes=24 * 2**20),
        cost_estimate=pl.CostEstimate(flops=flops, bytes_accessed=nbytes, transcendentals=0),
        name=name,
    )


def state_kernel(a_ref, b_ref, s_ref):
    both = mm_at(a_ref[...], b_ref[...])
    d = HEAD_DIM
    for h in range(2):
        s_ref[h] = both[h * d : (h + 1) * d, h * d : (h + 1) * d].astype(s_ref.dtype)


def running_kernel(reverse, x_ref, o_ref):
    n = x_ref.shape[0]
    total = jnp.zeros(x_ref.shape[1:], F32)
    for k in range(n):
        at = n - 1 - k if reverse else k
        o_ref[at] = total.astype(o_ref.dtype)
        total = total + x_ref[at].astype(F32)


def weigh_kernel(gate_ref, grad_ref, gain_ref, w_ref):
    g = gate_ref[...].astype(F32)
    w = grad_ref[...].astype(F32) * gain_ref[...] * g * jax.nn.sigmoid(g)
    w_ref[0] = w.astype(w_ref.dtype)


def lower(n):
    return lax.broadcasted_iota(jnp.int32, (n, n), 0) >= lax.broadcasted_iota(jnp.int32, (n, n), 1)


def upper(n):
    return lax.broadcasted_iota(jnp.int32, (n, n), 0) <= lax.broadcasted_iota(jnp.int32, (n, n), 1)


def intra_kernel(q_ref, k_ref, v_ref, i_ref):
    d = HEAD_DIM
    t = q_ref.shape[0]
    half = t // 2
    keep = lower(half)
    for h in range(2):
        cols = slice(h * d, (h + 1) * d)
        q, k, v = q_ref[:, cols], k_ref[:, cols], v_ref[:, cols]
        for r in range(2):
            rows = slice(r * half, (r + 1) * half)
            s = mm_bt(q[rows], k[rows])
            s = jnp.where(keep, s, 0.0).astype(BF16)
            acc = mm(s, v[rows])
            if r:
                s = mm_bt(q[rows], k[:half]).astype(BF16)
                acc = acc + mm(s, v[:half])
            i_ref[rows, cols] = acc


def out_kernel(i_ref, q_ref, p_ref, w_ref, o_ref, sums_ref, sq_ref, cross_ref):
    d = HEAD_DIM
    step = pl.program_id(0)
    sq, cross = None, None
    for h in range(2):
        cols = slice(h * d, (h + 1) * d)
        o = (i_ref[:, cols] + mm(q_ref[:, cols], p_ref[h])).astype(BF16)
        o_ref[:, cols] = o
        o = o.astype(F32)
        a, b = o * o, o * w_ref[:, cols].astype(F32)
        sq, cross = (a, b) if sq is None else (sq + a, cross + b)

    @pl.when(step == 0)
    def _():
        sq_ref[...] = sq
        cross_ref[...] = cross

    @pl.when(step > 0)
    def _():
        sq_ref[...] += sq
        cross_ref[...] += cross

    @pl.when(step == pl.num_programs(0) - 1)
    def _():
        blocks = sq_ref.shape[0] // 128
        rows = []
        for ref in (sq_ref, cross_ref):
            for r in range(blocks):
                piece = jnp.transpose(ref[r * 128 : (r + 1) * 128, :])
                rows.append(jnp.sum(piece, axis=0, keepdims=True))
        tile = jnp.concatenate(rows, axis=0)
        for k in range(sums_ref.shape[0]):
            sums_ref[k] = tile


def grad_kernel(width, sums_ref, w_ref, o_ref, q_ref, do_ref, z_ref):
    d = HEAD_DIM
    tile = jnp.sum(sums_ref[...], axis=0)
    turned = jnp.transpose(jnp.broadcast_to(tile[None], (16,) + tile.shape).reshape(128, 128))
    blocks = tile.shape[0] // 2
    inv = lax.rsqrt(turned[:, :blocks] / width + EPS)
    fall = inv * inv * inv * (turned[:, blocks : 2 * blocks] / width)
    inv = jnp.concatenate([inv[:, r : r + 1] for r in range(blocks)], axis=0)
    fall = jnp.concatenate([fall[:, r : r + 1] for r in range(blocks)], axis=0)
    do = (inv * w_ref[...].astype(F32) - fall * o_ref[...].astype(F32)).astype(BF16)
    do_ref[...] = do
    both = mm_at(q_ref[...], do)
    for h in range(2):
        z_ref[h] = both[h * d : (h + 1) * d, h * d : (h + 1) * d].astype(z_ref.dtype)


def back_kernel(q_ref, k_ref, v_ref, do_ref, p_ref, gq_ref, gk_ref, gv_ref):
    d = HEAD_DIM
    t = q_ref.shape[0]
    half = t // 2
    low, up = lower(half), upper(half)
    one, two = slice(0, half), slice(half, t)
    for h in range(2):
        cols = slice(h * d, (h + 1) * d)
        q, k, v, do = q_ref[:, cols], k_ref[:, cols], v_ref[:, cols], do_ref[:, cols]
        for r in (one, two):
            g = jnp.where(low, mm_bt(do[r], v[r]), 0.0).astype(BF16)
            acc = mm(g, k[r]) + mm_bt(do[r], p_ref[h])
            if r is two:
                acc = acc + mm(mm_bt(do[r], v[one]).astype(BF16), k[one])
            gq_ref[r, cols] = acc.astype(BF16)
            gt = jnp.where(up, mm_bt(v[r], do[r]), 0.0).astype(BF16)
            st = jnp.where(up, mm_bt(k[r], q[r]), 0.0).astype(BF16)
            ak, av = mm(gt, q[r]), mm(st, do[r])
            if r is one:
                ak = ak + mm(mm_bt(v[r], do[two]).astype(BF16), q[two])
                av = av + mm(mm_bt(k[r], q[two]).astype(BF16), do[two])
            gk_ref[r, cols] = ak
            gv_ref[r, cols] = av


def last_kernel(ak_ref, av_ref, k_ref, v_ref, s_ref, gk_ref, gv_ref):
    d = HEAD_DIM
    for h in range(2):
        cols = slice(h * d, (h + 1) * d)
        gk_ref[:, cols] = (ak_ref[:, cols] + mm_bt(v_ref[:, cols], s_ref[h])).astype(BF16)
        gv_ref[:, cols] = (av_ref[:, cols] + mm(k_ref[:, cols], s_ref[h])).astype(BF16)


def gate_kernel(rows_ref, gate_ref, grad_ref, gain_ref, gg_ref):
    parts, _, wide = rows_ref.shape
    total = None
    for p in range(parts):
        o = rows_ref[p].astype(F32)
        s = jnp.sum(o * o, axis=1, keepdims=True)
        total = s if total is None else total + s
    inv = lax.rsqrt(total / (parts * wide) + EPS)
    for p in range(parts):
        cols = slice(p * wide, (p + 1) * wide)
        g = gate_ref[:, cols].astype(F32)
        s = jax.nn.sigmoid(g)
        scaled = grad_ref[:, cols].astype(F32) * gain_ref[:, cols]
        normed = rows_ref[p].astype(F32) * inv
        gg_ref[:, cols] = (scaled * normed * s * (1.0 + g * (1.0 - s))).astype(BF16)


def on_device(query, key_in, value, gate, gain, grad_out):
    d = HEAD_DIM
    t, own = query.shape
    heads = own // d
    rows, width = gate.shape
    n_seq, n_head = lax.axis_size("seq"), lax.axis_size("head")
    pairs = heads // 2
    gain = gain.reshape(1, width)

    def sds(shape, dtype):
        return jax.ShapeDtypeStruct(shape, dtype)

    wide = pl.BlockSpec((t, 2 * d), lambda i: (0, i))
    square = pl.BlockSpec((2, d, d), lambda i: (i, 0, 0))
    small = 2 * t * d * d * heads
    large = 2 * t * t * d * heads

    def exchange(states, reverse):
        piece = (n_seq, heads * d // n_seq, d)
        states = lax.all_to_all(states.reshape(piece), "seq", 0, 0, tiled=True)
        summed = call(
            functools.partial(running_kernel, reverse), sds(piece, BF16), (), None, None,
            heads * d * d, 4 * heads * d * d, "running",
        )(states)
        return lax.all_to_all(summed, "seq", 0, 0, tiled=True).reshape(heads, d, d)

    states = call(
        state_kernel, sds((heads, d, d), BF16), (pairs,), [wide, wide], square,
        2 * small, 4 * t * own, "states",
    )(key_in, value)
    prefix = exchange(states, False)

    part = pl.BlockSpec((rows, own), lambda i: (0, i))
    weighted = call(
        weigh_kernel, sds((n_head, rows, own), BF16), (n_head,),
        [part, part, pl.BlockSpec((1, own), lambda i: (0, i))],
        pl.BlockSpec((1, rows, own), lambda i: (i, 0, 0)),
        20 * rows * width, 6 * rows * width, "weigh",
    )(gate, grad_out, gain)
    weighted = lax.all_to_all(weighted, "head", 0, 0, tiled=True).reshape(t, own)

    intra = call(
        intra_kernel, sds((t, own), F32), (pairs,), [wide, wide, wide], wide,
        2 * large, 10 * t * own, "intra",
    )(query, key_in, value)

    tile = (n_head, 2 * t // 128, 128)
    out, sums = pl.pallas_call(
        out_kernel,
        out_shape=(sds((t, own), BF16), sds(tile, F32)),
        grid=(pairs,),
        in_specs=[wide, wide, square, wide],
        out_specs=(wide, pl.BlockSpec(tile, lambda i: (0, 0, 0))),
        scratch_shapes=[pltpu.VMEM((t, d), F32), pltpu.VMEM((t, d), F32)],
        compiler_params=pltpu.CompilerParams(vmem_limit_bytes=24 * 2**20),
        cost_estimate=pl.CostEstimate(flops=small, bytes_accessed=10 * t * own, transcendentals=0),
        name="outs",
    )(intra, query, prefix, weighted)
    sums = lax.all_to_all(sums, "head", 0, 0, tiled=True)

    grad_attn, states = call(
        functools.partial(grad_kernel, float(width)),
        (sds((t, own), BF16), sds((heads, d, d), BF16)), (pairs,),
        [pl.BlockSpec(tile, lambda i: (0, 0, 0)), wide, wide, wide], (wide, square),
        small, 8 * t * own, "grads",
    )(sums, weighted, out, query)
    suffix = exchange(states, True)

    token_rows = lax.all_to_all(out.reshape(n_head, rows, own), "head", 0, 0, tiled=True)
    grad_gate = call(
        gate_kernel, sds((rows, width), BF16), (), None, None,
        20 * rows * width, 8 * rows * width, "gates",
    )(token_rows, gate, grad_out, gain)

    grad_query, part_key, part_value = call(
        back_kernel,
        (sds((t, own), BF16), sds((t, own), F32), sds((t, own), F32)), (pairs,),
        [wide, wide, wide, wide, square], (wide, wide, wide),
        4 * large, 18 * t * own, "backs",
    )(query, key_in, value, grad_attn, prefix)

    grad_key, grad_value = call(
        last_kernel, (sds((t, own), BF16), sds((t, own), BF16)), (pairs,),
        [wide, wide, wide, wide, square], (wide, wide),
        2 * small, 16 * t * own, "last",
    )(part_key, part_value, key_in, value, suffix)
    return grad_query, grad_key, grad_value, grad_gate


def solution(mesh):
    in_specs = (
        P("seq", "head"),
        P("seq", "head"),
        P("seq", "head"),
        P(("seq", "head"), None),
        P(),
        P(("seq", "head"), None),
    )
    out_specs = (P("seq", "head"), P("seq", "head"), P("seq", "head"), P(("seq", "head"), None))
    return jax.shard_map(
        on_device, mesh=mesh, in_specs=in_specs, out_specs=out_specs, check_vma=False
    )
```

time: 364 us -> 152 us (0.42)
  waiting for transfers between devices: 175 us -> 46.6 us
  other arithmetic: 83.1 us -> 0 us
  Pallas kernels: 0 us -> 32.1 us
  starting transfers between devices: 0.08 us -> 29.1 us
  matrix products: 26.1 us -> 0 us
  blocking collectives: 38.9 us -> 24.5 us
  between operations: 14.3 us -> 0.84 us
    all_gather x2 -> x0, waiting for transfers between devices: 175 us -> none  [carried_in(): everything = lax.all_gather(value.astype(jnp.bfloat16), axis)]
    select_n x64 -> x0, other arithmetic: 79.1 us -> none  [step(): return jnp.where(reached, new, before)]
    all_to_all x0 -> x5, waiting for transfers between devices: none -> 46.6 us  [the longest x1 15.3 us: on_device(): lax.all_to_all(weighted, 'head', 0, 0, tiled=True).reshape(t, own)]
    pallas_call x0 -> x10, Pallas kernels: none -> 32.1 us  [the longest x1 9.48 us: on_device(): call(back_kernel, (sds((t, own), BF16), sds((t, own), F32), sds((t, own),...]
    all_to_all x0 -> x5, starting transfers between devices: none -> 29.1 us  [the longest x1 11.4 us: exchange(): states = lax.all_to_all(states.reshape(piece), 'seq', 0, 0, tiled=True)]
    dot_general x12 -> x0, matrix products: 26.1 us -> none  [the longest x1 4.3 us: on_device(): jnp.einsum('hts,thd->shd', grad_scores, queries, preferred_element_type=j...]
    all_to_all x2, blocking collectives: 38.9 us -> 24.5 us  [the longest x1 16.7 us: exchange(): states = lax.all_to_all(states.reshape(piece), 'seq', 0, 0, tiled=True)]
    unnamed x31 -> x46, local copies, waits for them, and re-layouts: 14.7 us -> 16.7 us
  transfers between devices with their start and end apart: 2 -> 5, of which waited for: 2 -> 4; matrix products, arithmetic and copies ran while one was open for 4% -> 0% of each run, Pallas kernels for 0% -> 12%
where the time goes in v1:
time: 152 us; the launch traced here: 150 us
  waiting for transfers between devices  46.6 us (31%)
  Pallas kernels  32.1 us (21%)
  starting transfers between devices  29.1 us (19%)
  blocking collectives  24.5 us (16%)
  local copies, waits for them, and re-layouts  16.7 us (11%)
    unnamed x46, local copies, waits for them, and re-layouts  16.7 us
    all_to_all x1, blocking collectives, exchange(): states = lax.all_to_all(states.reshape(piece), 'seq', 0, 0, tiled=True)  16.7 us
    all_to_all x1, waiting for transfers between devices, on_device(): lax.all_to_all(weighted, 'head', 0, 0, tiled=True).reshape(t, own)  15.3 us
    all_to_all x1, waiting for transfers between devices, on_device(): lax.all_to_all(out.reshape(n_head, rows, own), 'head', 0, 0, tiled=True)  14.3 us
    all_to_all x1, starting transfers between devices, exchange(): states = lax.all_to_all(states.reshape(piece), 'seq', 0, 0, tiled=True)  11.4 us
    all_to_all x1, waiting for transfers between devices, exchange(): states = lax.all_to_all(states.reshape(piece), 'seq', 0, 0, tiled=True)  10.4 us
    pallas_call x1, Pallas kernels, on_device(): call(back_kernel, (sds((t, own), BF16), sds((t, own), F32), sds((t, own),...  9.48 us
    all_to_all x2, starting transfers between devices, exchange(): return lax.all_to_all(summed, 'seq', 0, 0, tiled=True).reshape(heads, d, d)  9.18 us
  transfers between devices with their start and end apart: 5, of which 4 were waited for; matrix products, arithmetic and copies ran while one was open for 0% of the time, Pallas kernels for 12%

profile of v1, /device:TPU:32, one launch (start us, length us, event | category | flops | bytes accessed | tf_op | source)
XLA Modules:
  0.0 149.9 jit_solution(6438871106237950454)
XLA Ops:
  0.6 0.0 copy-start.1
  0.6 1.2 copy-done.1
  1.9 0.0 copy-start.3
  1.9 1.2 copy-done.3
  3.1 0.0 copy-start.9
  3.1 0.0 copy-start.11
  3.1 0.0 copy-start.20
  3.1 2.3 %states.1 = bf16[8,128,128]{2,1,0:T(8,128)(2,1)} custom-call(bf16[512,1024]{1,0:T(8,128)(2,1)S(1)} %copy-done.1, bf16[512,1024]{1,0:T(8,128)(2,1)S(1)} %copy-done.3), custom_call_target="tpu_custom_call" | custom-call | flops 268435456 | bytes 2097152 | tf_op jit(solution)/shard_map/states/pallas_call | solution.py:216
  5.4 11.4 %all-to-all-start = ((bf16[32,32,128]{2,1,0:T(8,128)(2,1)}), bf16[32,32,128]{2,1,0:T(8,128)(2,1)S(1)}, u32[]{:S(2)}, u32[]{:S(2)}) async-start(bf16[32,32,128]{2,1,0:T(8,128)(2,1)} %bitcast), calls=%async_computation | async-start | bytes 524288 | tf_op jit(solution)/shard_map/all_to_all | solution.py:209
  16.8 0.0 copy-done.9
  16.8 0.0 copy-done.11
  16.8 0.0 copy-done.20
  16.8 0.8 weigh.1
  17.7 0.0 copy-start.8
  17.7 1.0 copy-done.8
  18.6 0.0 copy-start
  18.6 0.0 copy-start.2
  18.6 0.0 copy-start.4
  18.6 10.4 %all-to-all-done.x_ref = bf16[32,32,128]{2,1,0:T(8,128)(2,1)S(1)} async-done(((bf16[32,32,128]{2,1,0:T(8,128)(2,1)}), bf16[32,32,128]{2,1,0:T(8,128)(2,1)S(1)}, u32[]{:S(2)}, u32[]{:S(2)}) %all-to-all-start) | async-done | bytes 262176 | tf_op jit(solution)/shard_map/all_to_all | solution.py:209
  29.1 4.3 %all-to-all-start.2 = ((bf16[8,64,1024]{2,1,0:T(8,128)(2,1)}), bf16[8,64,1024]{2,1,0:T(8,128)(2,1)}, u32[]{:S(2)}, u32[]{:S(2)}) async-start(bf16[8,64,1024]{2,1,0:T(8,128)(2,1)} %copy-done.8), calls=%async_computation.2 | async-start | bytes 2097152 | tf_op jit(solution)/shard_map/all_to_all | solution.py:229
  33.4 0.0 copy-start.18
  33.4 0.7 copy-done.18
  34.1 15.3 %all-to-all-done.2 = bf16[8,64,1024]{2,1,0:T(8,128)(2,1)} async-done(((bf16[8,64,1024]{2,1,0:T(8,128)(2,1)}), bf16[8,64,1024]{2,1,0:T(8,128)(2,1)}, u32[]{:S(2)}, u32[]{:S(2)}) %all-to-all-start.2) | async-done | bytes 1048608 | tf_op jit(solution)/shard_map/all_to_all | solution.py:229
  49.4 4.6 %all-to-all-start.1 = ((bf16[32,32,128]{2,1,0:T(8,128)(2,1)}), bf16[32,32,128]{2,1,0:T(8,128)(2,1)S(1)}, u32[]{:S(2)}, u32[]{:S(2)}) async-start(bf16[32,32,128]{2,1,0:T(8,128)(2,1)} %copy-done.18), calls=%async_computation.1 | async-start | bytes 524288 | tf_op jit(solution)/shard_map/all_to_all | solution.py:214
  54.0 0.0 copy-done
  54.0 0.0 copy-done.2
  54.0 0.0 copy-done.4
  54.0 4.1 %intra.1.i_ref = f32[512,1024]{1,0:T(8,128)S(1)} custom-call(bf16[512,1024]{1,0:T(8,128)(2,1)S(1)} %copy-done, bf16[512,1024]{1,0:T(8,128)(2,1)S(1)} %copy-done.2, bf16[512,1024]{1,0:T(8,128)(2,1)S(1)} %copy-done.4), custom_call_target="tpu_custom_call" | custom-call | flops 1073741824 | bytes 5242880 | tf_op jit(solution)/shard_map/intra/pallas_call | solution.py:231
  58.1 0.0 copy-start.5
  58.1 1.3 copy-done.5
  59.5 6.6 %all-to-all-done.1 = bf16[32,32,128]{2,1,0:T(8,128)(2,1)S(1)} async-done(((bf16[32,32,128]{2,1,0:T(8,128)(2,1)}), bf16[32,32,128]{2,1,0:T(8,128)(2,1)S(1)}, u32[]{:S(2)}, u32[]{:S(2)}) %all-to-all-start.1) | async-done | bytes 262176 | tf_op jit(solution)/shard_map/all_to_all | solution.py:214
  66.1 0.0 copy-start.6
  66.1 1.6 %copy-done.6 = f32[512,1024]{1,0:T(8,128)S(1)} copy-done((f32[512,1024]{1,0:T(8,128)S(1)}, f32[512,1024]{1,0:T(8,128)}, u32[]{:S(2)}) %copy-start.6) | copy-done | bytes 2097176
  67.7 3.4 %outs.1 = (bf16[512,1024]{1,0:T(8,128)(2,1)S(1)}, f32[8,8,128]{2,1,0:T(8,128)S(1)}) custom-call(f32[512,1024]{1,0:T(8,128)S(1)} %copy-done.6, bf16[512,1024]{1,0:T(8,128)(2,1)S(1)} %copy-done, bf16[8,128,128]{2,1,0:T(8,128)(2,1)S(1)} %bitcast.8, bf16[512,1024]{1,0:T(8,128)(2,1)} %bitcast.3.w_ref), custom_call_target="tpu_custom_call" | custom-call | flops 134217728 | bytes 5242880 | tf_op jit(solution)/shard_map/outs/pallas_call | solution.py:237
  71.1 0.0 copy-start.7
  71.1 7.8 %all_to_all.35.sums_ref = f32[8,8,128]{2,1,0:T(8,128)S(1)} all-to-all(f32[8,8,128]{2,1,0:T(8,128)S(1)} %get-tuple-element.13), channel_id=1, replica_groups=mesh['seq'=32,'head'=8] {'head'}, dimensions={0} | all-to-all | bytes 65536 | tf_op jit(solution)/shard_map/all_to_all | solution.py:248
  79.0 4.0 %grads.1 = (bf16[512,1024]{1,0:T(8,128)(2,1)S(1)}, bf16[8,128,128]{2,1,0:T(8,128)(2,1)S(1)}) custom-call(f32[8,8,128]{2,1,0:T(8,128)S(1)} %all_to_all.35.sums_ref, bf16[512,1024]{1,0:T(8,128)(2,1)} %bitcast.3.w_ref, bf16[512,1024]{1,0:T(8,128)(2,1)S(1)} %get-tuple-element.14.o_ref, bf16[512,1024]{1,0:T(8,128)(2,1)S(1)} %copy-done), custom_call_target="tpu_custom_call" | custom-call | flops 134217728 | bytes 4194304 | tf_op jit(solution)/shard_map/grads/pallas_call | solution.py:250
  83.0 0.0 copy-start.21
  83.0 1.0 copy-done.21
  83.9 16.7 %all_to_all.36.x_ref = bf16[32,32,128]{2,1,0:T(8,128)(2,1)} all-to-all(bf16[32,32,128]{2,1,0:T(8,128)(2,1)S(1)} %bitcast.10), channel_id=1, replica_groups=mesh['seq'=32,'head'=8] {'seq'}, dimensions={0} | all-to-all | bytes 524288 | tf_op jit(solution)/shard_map/all_to_all | solution.py:209
  100.6 0.0 copy-done.7
  100.6 4.2 %all-to-all-start.6 = ((bf16[8,64,1024]{2,1,0:T(8,128)(2,1)}), bf16[8,64,1024]{2,1,0:T(8,128)(2,1)}, u32[]{:S(2)}, u32[]{:S(2)}) async-start(bf16[8,64,1024]{2,1,0:T(8,128)(2,1)} %bitcast.7), calls=%async_computation.6 | async-start | bytes 2097152 | tf_op jit(solution)/shard_map/all_to_all | solution.py:258
  104.9 0.0 copy-start.19
  104.9 0.9 copy-done.19
  105.9 0.0 copy-start.17
  105.9 0.7 copy-done.17
  106.6 14.3 %all-to-all-done.6.rows_ref = bf16[8,64,1024]{2,1,0:T(8,128)(2,1)} async-done(((bf16[8,64,1024]{2,1,0:T(8,128)(2,1)}), bf16[8,64,1024]{2,1,0:T(8,128)(2,1)}, u32[]{:S(2)}, u32[]{:S(2)}) %all-to-all-start.6) | async-done | bytes 1048608 | tf_op jit(solution)/shard_map/all_to_all | solution.py:258
  120.8 4.6 %all-to-all-start.5 = ((bf16[32,32,128]{2,1,0:T(8,128)(2,1)}), bf16[32,32,128]{2,1,0:T(8,128)(2,1)}, u32[]{:S(2)}, u32[]{:S(2)}) async-start(bf16[32,32,128]{2,1,0:T(8,128)(2,1)} %copy-done.17), calls=%async_computation.5 | async-start | bytes 524288 | tf_op jit(solution)/shard_map/all_to_all | solution.py:214
  125.4 0.0 copy-start.22
  125.5 1.2 copy-done.22
  126.7 0.0 copy-start.10
  126.7 0.0 copy-start.12
  126.7 9.5 %backs.1 = (bf16[512,1024]{1,0:T(8,128)(2,1)}, f32[512,1024]{1,0:T(8,128)S(1)}, f32[512,1024]{1,0:T(8,128)S(1)}) custom-call(bf16[512,1024]{1,0:T(8,128)(2,1)S(1)} %copy-done, bf16[512,1024]{1,0:T(8,128)(2,1)S(1)} %copy-done.2, bf16[512,1024]{1,0:T(8,128)(2,1)S(1)} %copy-done.4, bf16[512,1024]{1,0:T(8,128)(2,1)S(1)} %copy-done.22, ...), custom_call_target="tpu_custom_call" | custom-call | flops 2147483648 | bytes 9437184 | tf_op jit(solution)/shard_map/backs/pallas_call | solution.py:264
  136.2 0.0 copy-start.13
  136.2 1.3 copy-done.13
  137.5 0.0 copy-start.15
  137.5 1.3 copy-done.15
  138.8 0.0 copy-done.10
  138.8 0.0 copy-done.12
  138.8 3.8 %gates.1 = bf16[64,8192]{1,0:T(8,128)(2,1)} custom-call(bf16[8,64,1024]{2,1,0:T(8,128)(2,1)} %all-to-all-done.6.rows_ref, bf16[64,8192]{1,0:T(8,128)(2,1)S(1)} %copy-done.10, bf16[64,8192]{1,0:T(8,128)(2,1)S(1)} %copy-done.12, f32[1,8192]{1,0:T(1,128)S(1)} %bitcast.12), custom_call_target="tpu_custom_call" | custom-call | flops 10485760 | bytes 4194304 | tf_op jit(solution)/shard_map/gates/pallas_call | solution.py:259
  142.6 0.0 all-to-all-done.5
  142.6 1.6 %copy-done.14 = f32[512,1024]{1,0:T(8,128)S(1)} copy-done((f32[512,1024]{1,0:T(8,128)S(1)}, f32[512,1024]{1,0:T(8,128)}, u32[]{:S(2)}) %copy-start.14) | copy-done | bytes 2097176
  144.2 1.6 %copy-done.16 = f32[512,1024]{1,0:T(8,128)S(1)} copy-done((f32[512,1024]{1,0:T(8,128)S(1)}, f32[512,1024]{1,0:T(8,128)}, u32[]{:S(2)}) %copy-start.16) | copy-done | bytes 2097176
  145.8 4.1 %last.1 = (bf16[512,1024]{1,0:T(8,128)(2,1)}, bf16[512,1024]{1,0:T(8,128)(2,1)}) custom-call(f32[512,1024]{1,0:T(8,128)S(1)} %copy-done.14, f32[512,1024]{1,0:T(8,128)S(1)} %copy-done.16, bf16[512,1024]{1,0:T(8,128)(2,1)S(1)} %copy-done.2, bf16[512,1024]{1,0:T(8,128)(2,1)S(1)} %copy-done.4, bf16[8,128,128]{2,1,0:T(8,128)(2,1)} %bitcast.5.s_ref), custom_call_target="tpu_custom_call" | custom-call | flops 268435456 | bytes 8388608 | tf_op jit(solution)/shard_map/last/pallas_call | solution.py:271
  (4 shorter events, 0.1 us)
Async XLA Ops:
  0.6 1.2 copy-start.1
  1.9 1.2 copy-start.3
  3.1 13.7 %copy-start.9 = (bf16[64,8192]{1,0:T(8,128)(2,1)S(1)}, bf16[64,8192]{1,0:T(8,128)(2,1)}, u32[]{:S(2)}) copy-start(bf16[64,8192]{1,0:T(8,128)(2,1)} %gate_ref.3) | copy-start | bytes 3145732
  3.1 13.7 %copy-start.11 = (bf16[64,8192]{1,0:T(8,128)(2,1)S(1)}, bf16[64,8192]{1,0:T(8,128)(2,1)}, u32[]{:S(2)}) copy-start(bf16[64,8192]{1,0:T(8,128)(2,1)} %grad_ref.3) | copy-start | bytes 3145732
  3.1 13.7 %copy-start.20 = (f32[8192]{0:T(1024)S(1)}, f32[8192]{0:T(1024)}, u32[]{:S(2)}) copy-start(f32[8192]{0:T(1024)} %param.10) | copy-start | bytes 98308
  5.4 23.7 %all-to-all-start = ((bf16[32,32,128]{2,1,0:T(8,128)(2,1)}), bf16[32,32,128]{2,1,0:T(8,128)(2,1)S(1)}, u32[]{:S(2)}, u32[]{:S(2)}) async-start(bf16[32,32,128]{2,1,0:T(8,128)(2,1)} %bitcast), calls=%async_computation | async-start | bytes 524288 | tf_op jit(solution)/shard_map/all_to_all | solution.py:209
  17.7 1.0 copy-start.8
  18.6 35.4 %copy-start = (bf16[512,1024]{1,0:T(8,128)(2,1)S(1)}, bf16[512,1024]{1,0:T(8,128)(2,1)}, u32[]{:S(2)}) copy-start(bf16[512,1024]{1,0:T(8,128)(2,1)} %q_ref.7) | copy-start | bytes 3145732
  18.6 35.4 %copy-start.2 = (bf16[512,1024]{1,0:T(8,128)(2,1)S(1)}, bf16[512,1024]{1,0:T(8,128)(2,1)}, u32[]{:S(2)}) copy-start(bf16[512,1024]{1,0:T(8,128)(2,1)} %k_ref.5) | copy-start | bytes 3145732
  18.6 35.4 %copy-start.4 = (bf16[512,1024]{1,0:T(8,128)(2,1)S(1)}, bf16[512,1024]{1,0:T(8,128)(2,1)}, u32[]{:S(2)}) copy-start(bf16[512,1024]{1,0:T(8,128)(2,1)} %v_ref.5) | copy-start | bytes 3145732
  29.1 20.4 %all-to-all-start.2 = ((bf16[8,64,1024]{2,1,0:T(8,128)(2,1)}), bf16[8,64,1024]{2,1,0:T(8,128)(2,1)}, u32[]{:S(2)}, u32[]{:S(2)}) async-start(bf16[8,64,1024]{2,1,0:T(8,128)(2,1)} %copy-done.8), calls=%async_computation.2 | async-start | bytes 2097152 | tf_op jit(solution)/shard_map/all_to_all | solution.py:229
  33.4 0.7 copy-start.18
  49.4 16.7 %all-to-all-start.1 = ((bf16[32,32,128]{2,1,0:T(8,128)(2,1)}), bf16[32,32,128]{2,1,0:T(8,128)(2,1)S(1)}, u32[]{:S(2)}, u32[]{:S(2)}) async-start(bf16[32,32,128]{2,1,0:T(8,128)(2,1)} %copy-done.18), calls=%async_computation.1 | async-start | bytes 524288 | tf_op jit(solution)/shard_map/all_to_all | solution.py:214
  58.1 1.3 copy-start.5
  66.1 1.6 %copy-start.6 = (f32[512,1024]{1,0:T(8,128)S(1)}, f32[512,1024]{1,0:T(8,128)}, u32[]{:S(2)}) copy-start(f32[512,1024]{1,0:T(8,128)} %copy-done.5) | copy-start | bytes 6291460
  71.1 29.5 %copy-start.7 = (bf16[512,1024]{1,0:T(8,128)(2,1)}, bf16[512,1024]{1,0:T(8,128)(2,1)S(1)}, u32[]{:S(2)}) copy-start(bf16[512,1024]{1,0:T(8,128)(2,1)S(1)} %get-tuple-element.14.o_ref) | copy-start | bytes 3145732
  83.0 1.0 copy-start.21
  100.6 20.2 %all-to-all-start.6 = ((bf16[8,64,1024]{2,1,0:T(8,128)(2,1)}), bf16[8,64,1024]{2,1,0:T(8,128)(2,1)}, u32[]{:S(2)}, u32[]{:S(2)}) async-start(bf16[8,64,1024]{2,1,0:T(8,128)(2,1)} %bitcast.7), calls=%async_computation.6 | async-start | bytes 2097152 | tf_op jit(solution)/shard_map/all_to_all | solution.py:258
  104.9 1.0 copy-start.19
  105.9 0.7 copy-start.17
  120.8 21.8 %all-to-all-start.5 = ((bf16[32,32,128]{2,1,0:T(8,128)(2,1)}), bf16[32,32,128]{2,1,0:T(8,128)(2,1)}, u32[]{:S(2)}, u32[]{:S(2)}) async-start(bf16[32,32,128]{2,1,0:T(8,128)(2,1)} %copy-done.17), calls=%async_computation.5 | async-start | bytes 524288 | tf_op jit(solution)/shard_map/all_to_all | solution.py:214
  125.4 1.2 copy-start.22
  126.7 12.1 %copy-start.10 = (bf16[64,8192]{1,0:T(8,128)(2,1)S(1)}, bf16[64,8192]{1,0:T(8,128)(2,1)}, u32[]{:S(2)}) copy-start(bf16[64,8192]{1,0:T(8,128)(2,1)} %gate_ref.3) | copy-start | bytes 3145732
  126.7 12.1 %copy-start.12 = (bf16[64,8192]{1,0:T(8,128)(2,1)S(1)}, bf16[64,8192]{1,0:T(8,128)(2,1)}, u32[]{:S(2)}) copy-start(bf16[64,8192]{1,0:T(8,128)(2,1)} %grad_ref.3) | copy-start | bytes 3145732
  136.2 1.3 copy-start.13
  137.5 1.3 copy-start.15
  142.6 1.6 %copy-start.14 = (f32[512,1024]{1,0:T(8,128)S(1)}, f32[512,1024]{1,0:T(8,128)}, u32[]{:S(2)}) copy-start(f32[512,1024]{1,0:T(8,128)} %copy-done.13) | copy-start | bytes 6291460
  144.2 1.6 %copy-start.16 = (f32[512,1024]{1,0:T(8,128)S(1)}, f32[512,1024]{1,0:T(8,128)}, u32[]{:S(2)}) copy-start(f32[512,1024]{1,0:T(8,128)} %copy-done.15) | copy-start | bytes 6291460

commit v2 on v1

v2 whole, which is shorter than its diff:
```python
import functools

import jax
import jax.numpy as jnp
from jax import lax
from jax.experimental import pallas as pl
from jax.experimental.pallas import tpu as pltpu
from jax.sharding import PartitionSpec as P

HEAD_DIM = 128
EPS = 1e-06
F32 = jnp.float32
BF16 = jnp.bfloat16


def mm(a, b):
    return lax.dot_general(a, b, (((1,), (0,)), ((), ())), preferred_element_type=F32)


def mm_bt(a, b):
    return lax.dot_general(a, b, (((1,), (1,)), ((), ())), preferred_element_type=F32)


def mm_at(a, b):
    return lax.dot_general(a, b, (((0,), (0,)), ((), ())), preferred_element_type=F32)


def params():
    return pltpu.CompilerParams(vmem_limit_bytes=24 * 2**20)


def cost(flops, nbytes):
    return pl.CostEstimate(flops=int(flops), bytes_accessed=int(nbytes), transcendentals=0)


def in_hbm(x):
    return pltpu.with_memory_space_constraint(x, pltpu.HBM)


def partner(n, d, sign):
    me = lax.axis_index("head")
    chip, core = me // 2, me % 2
    flip = core + d % 2 - 2 * core * (d % 2)
    return lax.rem(chip + sign * (d // 2) + n // 2, n // 2) * 2 + flip


def send_all(pieces):
    n = len(pieces)
    got = [pieces[0]]
    for d in range(1, n):
        pairs = [(i, ((i // 2 + d // 2) % (n // 2)) * 2 + ((i % 2) ^ (d % 2))) for i in range(n)]
        got.append(lax.ppermute(pieces[d], "head", pairs))
    return got


def start_all(copies):
    for c in copies:
        c.start()
    return copies


def wait_all(copies):
    for c in copies:
        c.wait()


def columns(i):
    return pl.ds(2 * HEAD_DIM * i, 2 * HEAD_DIM)


def by_pairs(src, dst, sems, at):
    n = src.shape[1] // (2 * HEAD_DIM)
    return [
        pltpu.make_async_copy(src.at[:, columns(i)], dst.at[:, columns(i)], sems.at[at + i])
        for i in range(n)
    ]


def rows_of(n, d, sign, rows):
    return pl.ds(pl.multiple_of(partner(n, d, sign) * rows, rows), rows)


def assemble(pieces, dst, sems, at):
    n, rows = len(pieces), pieces[0].shape[0]
    return [
        pltpu.make_async_copy(pieces[d], dst.at[rows_of(n, d, -1, rows), :], sems.at[at + d])
        for d in range(n)
    ]


def state_kernel(a_hbm, b_hbm, s_ref, a_ref, b_ref, sems):
    d = HEAD_DIM
    n = s_ref.shape[0] // 2
    ca, cb = by_pairs(a_hbm, a_ref, sems, 0), by_pairs(b_hbm, b_ref, sems, n)
    for i in range(n):
        ca[i].start()
        cb[i].start()
    for i in range(n):
        ca[i].wait()
        cb[i].wait()
        both = mm_at(a_ref[:, columns(i)], b_ref[:, columns(i)])
        for h in range(2):
            s_ref[2 * i + h] = both[h * d : (h + 1) * d, h * d : (h + 1) * d].astype(s_ref.dtype)


def running_kernel(reverse, x_ref, o_ref):
    n = x_ref.shape[0]
    total = jnp.zeros(x_ref.shape[1:], F32)
    for k in range(n):
        at = n - 1 - k if reverse else k
        o_ref[at] = total.astype(o_ref.dtype)
        total = total + x_ref[at].astype(F32)


def weigh_kernel(gate_ref, grad_ref, gain_ref, *w_refs):
    n = len(w_refs)
    own = gate_ref.shape[1] // n
    for d in range(n):
        cols = pl.ds(pl.multiple_of(partner(n, d, 1) * own, own), own)
        g = gate_ref[:, cols].astype(F32)
        w = grad_ref[:, cols].astype(F32) * gain_ref[:, cols] * g * jax.nn.sigmoid(g)
        w_refs[d][...] = w.astype(BF16)


def lower(n):
    return lax.broadcasted_iota(jnp.int32, (n, n), 0) >= lax.broadcasted_iota(jnp.int32, (n, n), 1)


def upper(n):
    return lax.broadcasted_iota(jnp.int32, (n, n), 0) <= lax.broadcasted_iota(jnp.int32, (n, n), 1)


def intra_kernel(q_ref, k_ref, v_ref, i_ref):
    d = HEAD_DIM
    t = q_ref.shape[0]
    half = t // 2
    keep = lower(half)
    for h in range(2):
        cols = slice(h * d, (h + 1) * d)
        q, k, v = q_ref[:, cols], k_ref[:, cols], v_ref[:, cols]
        for r in range(2):
            rows = slice(r * half, (r + 1) * half)
            s = mm_bt(q[rows], k[rows])
            s = jnp.where(keep, s, 0.0).astype(BF16)
            acc = mm(s, v[rows])
            if r:
                s = mm_bt(q[rows], k[:half]).astype(BF16)
                acc = acc + mm(s, v[:half])
            i_ref[rows, cols] = acc


def out_kernel(n_head, *refs):
    i_hbm, q_hbm, p_ref = refs[:3]
    w_hbm = refs[3 : 3 + n_head]
    sums_ref = refs[3 + n_head]
    o_hbm = refs[4 + n_head : 4 + 2 * n_head]
    i_ref, q_ref, w_ref, o_ref, sq_ref, cross_ref, sems, out_sems = refs[4 + 2 * n_head :]
    d = HEAD_DIM
    t, own = q_ref.shape
    n = own // (2 * d)
    ci, cq = by_pairs(i_hbm, i_ref, sems, 0), by_pairs(q_hbm, q_ref, sems, n)
    for i in range(n):
        cq[i].start()
        ci[i].start()
    cw = start_all(assemble(w_hbm, w_ref, sems, 2 * n))
    for i in range(n):
        cq[i].wait()
        ci[i].wait()
        for h in range(2 * i, 2 * i + 2):
            cols = slice(h * d, (h + 1) * d)
            for r in range(0, t, 256):
                rows = slice(r, r + 256)
                o = i_ref[rows, cols] + mm(q_ref[rows, cols], p_ref[h])
                o_ref[rows, cols] = o.astype(BF16)
    rows = t // n_head
    co = start_all(
        [
            pltpu.make_async_copy(o_ref.at[rows_of(n_head, k, 1, rows), :], o_hbm[k], out_sems.at[k])
            for k in range(n_head)
        ]
    )
    wait_all(cw)
    blocks = t // d
    lines = [None] * (2 * blocks)
    for r in range(blocks):
        rows = slice(r * d, (r + 1) * d)
        sq, cross = None, None
        for h in range(2 * n):
            cols = slice(h * d, (h + 1) * d)
            o = o_ref[rows, cols].astype(F32)
            a, b = o * o, o * w_ref[rows, cols].astype(F32)
            sq, cross = (a, b) if sq is None else (sq + a, cross + b)
        lines[r] = jnp.sum(jnp.transpose(sq), axis=0, keepdims=True)
        lines[blocks + r] = jnp.sum(jnp.transpose(cross), axis=0, keepdims=True)
    tile = jnp.concatenate(lines, axis=0)
    for k in range(n_head):
        sums_ref[k] = tile
    wait_all(co)


def grad_kernel(n_head, width, *refs):
    sums_ref, q_hbm = refs[:2]
    w_hbm = refs[2 : 2 + n_head]
    o_hbm = refs[2 + n_head : 2 + 2 * n_head]
    z_ref, do_hbm, q_ref, w_ref, o_ref, do_ref, sems, out_sems = refs[2 + 2 * n_head :]
    d = HEAD_DIM
    t, own = q_ref.shape
    n = own // (2 * d)
    rows = t // n_head
    cw = start_all(assemble(w_hbm, w_ref, sems, 0))
    co = start_all(
        [
            pltpu.make_async_copy(
                o_hbm[k], o_ref.at[rows_of(n_head, k, 1, rows), :], sems.at[n_head + k]
            )
            for k in range(n_head)
        ]
    )
    cq = start_all(by_pairs(q_hbm, q_ref, sems, 2 * n_head))
    tile = jnp.sum(sums_ref[...], axis=0)
    blocks = t // d
    turned = jnp.transpose(jnp.concatenate([tile] * (d // tile.shape[0]), axis=0))
    inv = lax.rsqrt(turned[:, :blocks] / width + EPS)
    fall = inv * inv * inv * (turned[:, blocks : 2 * blocks] / width)
    inv = [jnp.broadcast_to(inv[:, r : r + 1], (d, d)) for r in range(blocks)]
    fall = [jnp.broadcast_to(fall[:, r : r + 1], (d, d)) for r in range(blocks)]
    wait_all(cw)
    wait_all(co)
    cd = by_pairs(do_ref, do_hbm, out_sems, 0)
    for i in range(n):
        for h in range(2 * i, 2 * i + 2):
            cols = slice(h * d, (h + 1) * d)
            for r in range(blocks):
                rows = slice(r * d, (r + 1) * d)
                w, o = w_ref[rows, cols].astype(F32), o_ref[rows, cols].astype(F32)
                do_ref[rows, cols] = (inv[r] * w - fall[r] * o).astype(BF16)
        cd[i].start()
        cq[i].wait()
        both = mm_at(q_ref[:, columns(i)], do_ref[:, columns(i)])
        for h in range(2):
            z_ref[2 * i + h] = both[h * d : (h + 1) * d, h * d : (h + 1) * d].astype(z_ref.dtype)
    wait_all(cd)


def back_kernel(q_ref, k_ref, v_ref, do_ref, p_ref, gq_ref, gk_ref, gv_ref):
    d = HEAD_DIM
    t = q_ref.shape[0]
    half = t // 2
    low, up = lower(half), upper(half)
    one, two = slice(0, half), slice(half, t)
    for h in range(2):
        cols = slice(h * d, (h + 1) * d)
        q, k, v, do = q_ref[:, cols], k_ref[:, cols], v_ref[:, cols], do_ref[:, cols]
        for r in (one, two):
            g = jnp.where(low, mm_bt(do[r], v[r]), 0.0).astype(BF16)
            acc = mm(g, k[r]) + mm_bt(do[r], p_ref[h])
            if r is two:
                acc = acc + mm(mm_bt(do[r], v[one]).astype(BF16), k[one])
            gq_ref[r, cols] = acc.astype(BF16)
            gt = jnp.where(up, mm_bt(v[r], do[r]), 0.0).astype(BF16)
            st = jnp.where(up, mm_bt(k[r], q[r]), 0.0).astype(BF16)
            ak, av = mm(gt, q[r]), mm(st, do[r])
            if r is one:
                ak = ak + mm(mm_bt(v[r], do[two]).astype(BF16), q[two])
                av = av + mm(mm_bt(k[r], q[two]).astype(BF16), do[two])
            gk_ref[r, cols] = ak
            gv_ref[r, cols] = av


def last_kernel(ak_hbm, av_hbm, k_hbm, v_hbm, s_ref, gk_hbm, gv_hbm, ak_ref, av_ref, k_ref, v_ref, gk_ref, gv_ref, sems, out_sems):
    d = HEAD_DIM
    t, own = k_ref.shape
    n = own // (2 * d)
    ins = [
        by_pairs(src, dst, sems, n * k)
        for k, (src, dst) in enumerate(
            ((v_hbm, v_ref), (ak_hbm, ak_ref), (k_hbm, k_ref), (av_hbm, av_ref))
        )
    ]
    for i in range(n):
        for c in ins:
            c[i].start()
    ck, cv = by_pairs(gk_ref, gk_hbm, out_sems, 0), by_pairs(gv_ref, gv_hbm, out_sems, n)
    for i in range(n):
        for c in ins:
            c[i].wait()
        for h in range(2 * i, 2 * i + 2):
            cols = slice(h * d, (h + 1) * d)
            for r in range(0, t, 256):
                rows = slice(r, r + 256)
                gk = ak_ref[rows, cols] + mm_bt(v_ref[rows, cols], s_ref[h])
                gk_ref[rows, cols] = gk.astype(BF16)
                gv = av_ref[rows, cols] + mm(k_ref[rows, cols], s_ref[h])
                gv_ref[rows, cols] = gv.astype(BF16)
        ck[i].start()
        cv[i].start()
    wait_all(ck + cv)


def gate_kernel(n, *refs):
    o_refs = refs[:n]
    gate_ref, grad_ref, gain_ref, gg_ref = refs[n:]
    wide = o_refs[0].shape[1]
    total = None
    for r in o_refs:
        o = r[...].astype(F32)
        s = jnp.sum(o * o, axis=1, keepdims=True)
        total = s if total is None else total + s
    inv = lax.rsqrt(total / (n * wide) + EPS)
    for k in range(n):
        cols = pl.ds(pl.multiple_of(partner(n, k, -1) * wide, wide), wide)
        g = gate_ref[:, cols].astype(F32)
        s = jax.nn.sigmoid(g)
        scaled = grad_ref[:, cols].astype(F32) * gain_ref[:, cols]
        normed = o_refs[k][...].astype(F32) * inv
        gg_ref[:, cols] = (scaled * normed * s * (1.0 + g * (1.0 - s))).astype(BF16)


def on_device(query, key_in, value, gate, gain, grad_out):
    d = HEAD_DIM
    t, own = query.shape
    heads = own // d
    rows, width = gate.shape
    n_seq, n_head = lax.axis_size("seq"), lax.axis_size("head")
    pairs = heads // 2
    gain = gain.reshape(1, width)

    def sds(shape, dtype):
        return jax.ShapeDtypeStruct(shape, dtype)

    def dma(n):
        return pltpu.SemaphoreType.DMA((n,))

    anywhere = pl.BlockSpec(memory_space=pl.ANY)
    whole = pl.BlockSpec(memory_space=pltpu.VMEM)
    wide = pl.BlockSpec((t, 2 * d), lambda i: (0, i))
    square = pl.BlockSpec((2, d, d), lambda i: (i, 0, 0))
    small = 2 * t * d * d * heads
    large = 2 * t * t * d * heads
    query, key_in, value = in_hbm(query), in_hbm(key_in), in_hbm(value)
    full = pltpu.VMEM((t, own), BF16)
    full32 = pltpu.VMEM((t, own), F32)

    def exchange(states, reverse):
        piece = (n_seq, heads * d // n_seq, d)
        states = lax.all_to_all(states.reshape(piece), "seq", 0, 0, tiled=True)
        summed = pl.pallas_call(
            functools.partial(running_kernel, reverse),
            out_shape=sds(piece, BF16),
            compiler_params=params(),
            cost_estimate=cost(heads * d * d, 4 * heads * d * d),
            name="running",
        )(states)
        return lax.all_to_all(summed, "seq", 0, 0, tiled=True).reshape(heads, d, d)

    states = pl.pallas_call(
        state_kernel,
        out_shape=sds((heads, d, d), BF16),
        in_specs=[anywhere, anywhere],
        out_specs=whole,
        scratch_shapes=[full, full, dma(2 * pairs)],
        compiler_params=params(),
        cost_estimate=cost(2 * small, 4 * t * own),
        name="states",
    )(key_in, value)
    prefix = exchange(states, False)

    weighted = pl.pallas_call(
        weigh_kernel,
        out_shape=[sds((rows, own), BF16)] * n_head,
        compiler_params=params(),
        cost_estimate=cost(20 * rows * width, 6 * rows * width),
        name="weigh",
    )(gate, grad_out, gain)
    weighted = [in_hbm(w) for w in send_all(weighted)]

    intra = pl.pallas_call(
        intra_kernel,
        out_shape=pltpu.HBM((t, own), F32),
        grid=(pairs,),
        in_specs=[wide, wide, wide],
        out_specs=wide,
        compiler_params=params(),
        cost_estimate=cost(2 * large, 10 * t * own),
        name="intra",
    )(query, key_in, value)

    tile = (n_head, 2 * t // d, d)
    sums, *out = pl.pallas_call(
        functools.partial(out_kernel, n_head),
        out_shape=[sds(tile, F32)] + [pltpu.HBM((rows, own), BF16)] * n_head,
        in_specs=[anywhere, anywhere, whole] + [anywhere] * n_head,
        out_specs=[whole] + [anywhere] * n_head,
        scratch_shapes=[
            full32, full, full, full, pltpu.VMEM((t, d), F32), pltpu.VMEM((t, d), F32),
            dma(2 * pairs + n_head), dma(n_head),
        ],
        compiler_params=params(),
        cost_estimate=cost(small, 10 * t * own),
        name="outs",
    )(in_hbm(intra), query, prefix, *weighted)
    sums = lax.all_to_all(sums, "head", 0, 0, tiled=True)

    states, grad_attn = pl.pallas_call(
        functools.partial(grad_kernel, n_head, float(width)),
        out_shape=[sds((heads, d, d), BF16), pltpu.HBM((t, own), BF16)],
        in_specs=[whole, anywhere] + [anywhere] * (2 * n_head),
        out_specs=[whole, anywhere],
        scratch_shapes=[full, full, full, full, dma(2 * n_head + pairs), dma(pairs)],
        compiler_params=params(),
        cost_estimate=cost(small, 8 * t * own),
        name="grads",
    )(sums, query, *weighted, *[in_hbm(o) for o in out])
    suffix = exchange(states, True)

    token_rows = send_all(out)
    grad_gate = pl.pallas_call(
        functools.partial(gate_kernel, n_head),
        out_shape=sds((rows, width), BF16),
        compiler_params=params(),
        cost_estimate=cost(20 * rows * width, 8 * rows * width),
        name="gates",
    )(*token_rows, gate, grad_out, gain)

    grad_query, part_key, part_value = pl.pallas_call(
        back_kernel,
        out_shape=[sds((t, own), BF16), pltpu.HBM((t, own), F32), pltpu.HBM((t, own), F32)],
        grid=(pairs,),
        in_specs=[wide, wide, wide, wide, square],
        out_specs=[wide, wide, wide],
        compiler_params=params(),
        cost_estimate=cost(4 * large, 18 * t * own),
        name="backs",
    )(query, key_in, value, in_hbm(grad_attn), prefix)

    grad_key, grad_value = pl.pallas_call(
        last_kernel,
        out_shape=[sds((t, own), BF16), sds((t, own), BF16)],
        in_specs=[anywhere] * 4 + [whole],
        out_specs=[anywhere] * 2,
        scratch_shapes=[full32, full32, full, full, full, full, dma(4 * pairs), dma(2 * pairs)],
        compiler_params=params(),
        cost_estimate=cost(2 * small, 16 * t * own),
        name="last",
    )(in_hbm(part_key), in_hbm(part_value), key_in, value, suffix)
    return grad_query, grad_key, grad_value, grad_gate


def solution(mesh):
    in_specs = (
        P("seq", "head"),
        P("seq", "head"),
        P("seq", "head"),
        P(("seq", "head"), None),
        P(),
        P(("seq", "head"), None),
    )
    out_specs = (P("seq", "head"), P("seq", "head"), P("seq", "head"), P(("seq", "head"), None))
    return jax.shard_map(
        on_device, mesh=mesh, in_specs=in_specs, out_specs=out_specs, check_vma=False
    )
```

time: 152 us -> 122 us (0.80)
  waiting for transfers between devices: 46.6 us -> 3.77 us
  blocking collectives: 24.5 us -> 54.9 us
  local copies, waits for them, and re-layouts: 16.7 us -> 0.07 us
  starting transfers between devices: 29.1 us -> 24.9 us
  Pallas kernels: 32.1 us -> 35.4 us
    all_to_all x3 -> x0, waiting for transfers between devices: 40 us -> none  [the longest x1 15.3 us: on_device(): lax.all_to_all(weighted, 'head', 0, 0, tiled=True).reshape(t, own)]
    all_to_all x1 -> x2, blocking collectives: 16.7 us -> 45.3 us  [exchange(): states = lax.all_to_all(states.reshape(piece), 'seq', 0, 0, tiled=True)]
    all_to_all x3 -> x0, starting transfers between devices: 19.9 us -> none  [the longest x1 11.4 us: exchange(): states = lax.all_to_all(states.reshape(piece), 'seq', 0, 0, tiled=True)]
    unnamed x46 -> x34, local copies, waits for them, and re-layouts: 16.7 us -> 0.07 us
    ppermute x0 -> x14, starting transfers between devices: none -> 15.8 us  [send_all(): got.append(lax.ppermute(pieces[d], 'head', pairs))]
    all_to_all x2, waiting for transfers between devices: 6.64 us -> 0.01 us  [exchange(): return lax.all_to_all(summed, 'seq', 0, 0, tiled=True).reshape(heads, d, d)]
    ppermute x0 -> x14, waiting for transfers between devices: none -> 3.77 us  [send_all(): got.append(lax.ppermute(pieces[d], 'head', pairs))]
    pallas_call x10, Pallas kernels: 32.1 us -> 35.4 us  [the longest x1 10.5 us: on_device(): pl.pallas_call(back_kernel, out_shape=[sds((t, own), BF16), pltpu.HBM((t,...]
  transfers between devices with their start and end apart: 5 -> 16, of which waited for: 4 -> 4; matrix products, arithmetic and copies ran while one was open for 0% -> 0% of each run, Pallas kernels for 12% -> 16%
where the time goes in v2:
time: 122 us; the launch traced here: 120 us
  blocking collectives  54.9 us (45%)
  Pallas kernels  35.4 us (29%)
  starting transfers between devices  24.9 us (20%)
  waiting for transfers between devices  3.77 us (3%)
    all_to_all x2, blocking collectives, exchange(): states = lax.all_to_all(states.reshape(piece), 'seq', 0, 0, tiled=True)  45.3 us
    ppermute x14, starting transfers between devices, send_all(): got.append(lax.ppermute(pieces[d], 'head', pairs))  15.8 us
    pallas_call x1, Pallas kernels, on_device(): pl.pallas_call(back_kernel, out_shape=[sds((t, own), BF16), pltpu.HBM((t,...  10.5 us
    all_to_all x1, blocking collectives, on_device(): sums = lax.all_to_all(sums, 'head', 0, 0, tiled=True)  9.68 us
    all_to_all x2, starting transfers between devices, exchange(): return lax.all_to_all(summed, 'seq', 0, 0, tiled=True).reshape(heads, d, d)  9.12 us
    pallas_call x1, Pallas kernels, on_device(): pl.pallas_call(intra_kernel, out_shape=pltpu.HBM((t, own), F32), grid=(pa...  6 us
    pallas_call x1, Pallas kernels, on_device(): pl.pallas_call(last_kernel, out_shape=[sds((t, own), BF16), sds((t, own),...  4.37 us
    pallas_call x1, Pallas kernels, on_device(): pl.pallas_call(functools.partial(grad_kernel, n_head, float(width)), out_...  4.19 us
  transfers between devices with their start and end apart: 16, of which 4 were waited for; matrix products, arithmetic and copies ran while one was open for 0% of the time, Pallas kernels for 16%

profile of v2, /device:TPU:32, one launch (start us, length us, event | category | flops | bytes accessed | tf_op | source)
XLA Modules:
  0.0 120.2 jit_solution(14020332802786835517)
XLA Ops:
  0.6 0.0 copy-start.1
  0.6 0.0 copy-start
  0.7 0.0 copy-start.4
  0.7 2.5 %states.1 = bf16[8,128,128]{2,1,0:T(8,128)(2,1)S(1)} custom-call(bf16[512,1024]{1,0:T(8,128)(2,1)} %k_hbm.1, bf16[512,1024]{1,0:T(8,128)(2,1)} %v_hbm.1), custom_call_target="tpu_custom_call" | custom-call | flops 268435456 | bytes 2097152 | tf_op jit(solution)/shard_map/states/pallas_call | solution.py:356
  3.2 23.4 %all_to_all.25.x_ref = bf16[32,32,128]{2,1,0:T(8,128)(2,1)S(1)} all-to-all(bf16[32,32,128]{2,1,0:T(8,128)(2,1)S(1)} %bitcast.8), channel_id=1, replica_groups=mesh['seq'=32,'head'=8] {'seq'}, dimensions={0} | all-to-all | bytes 524288 | tf_op jit(solution)/shard_map/all_to_all | solution.py:346
  26.6 0.7 running.2
  27.4 4.6 %all-to-all-start.1 = ((bf16[32,32,128]{2,1,0:T(8,128)(2,1)}), bf16[32,32,128]{2,1,0:T(8,128)(2,1)S(1)}, u32[]{:S(2)}, u32[]{:S(2)}) async-start(bf16[32,32,128]{2,1,0:T(8,128)(2,1)} %running.2), calls=%async_computation.1 | async-start | bytes 524288 | tf_op jit(solution)/shard_map/all_to_all | solution.py:354
  31.9 0.0 copy-done.1
  32.0 0.0 copy-done
  32.0 0.0 copy-done.4
  32.0 0.5 weigh.1
  32.5 0.0 copy-start.3
  32.5 0.1 collective-permute-start
  32.6 1.6 %collective-permute-start.1 = (bf16[64,1024]{1,0:T(8,128)(2,1)S(1)}, bf16[64,1024]{1,0:T(8,128)(2,1)S(1)}, u32[]{:S(2)}, u32[]{:S(2)}) collective-permute-start(bf16[64,1024]{1,0:T(8,128)(2,1)S(1)} %get-tuple-element.30), channel_id=1, source_target_pairs={{0,2},{1,3},{2,4},{3,5},{4,6},{5,7},{6,0},{7,1},{8,10},{9,11},{10,... | collective-permute-start | bytes 393224 | tf_op jit(solution)/shard_map/ppermute | solution.py:52
  34.2 1.2 %collective-permute-start.2 = (bf16[64,1024]{1,0:T(8,128)(2,1)S(1)}, bf16[64,1024]{1,0:T(8,128)(2,1)S(1)}, u32[]{:S(2)}, u32[]{:S(2)}) collective-permute-start(bf16[64,1024]{1,0:T(8,128)(2,1)S(1)} %get-tuple-element.31), channel_id=1, source_target_pairs={{0,3},{1,2},{2,5},{3,4},{4,7},{5,6},{6,1},{7,0},{8,11},{9,10},{10,... | collective-permute-start | bytes 393224 | tf_op jit(solution)/shard_map/ppermute | solution.py:52
  35.5 1.7 %collective-permute-start.3 = (bf16[64,1024]{1,0:T(8,128)(2,1)S(1)}, bf16[64,1024]{1,0:T(8,128)(2,1)S(1)}, u32[]{:S(2)}, u32[]{:S(2)}) collective-permute-start(bf16[64,1024]{1,0:T(8,128)(2,1)S(1)} %get-tuple-element.32), channel_id=1, source_target_pairs={{0,4},{1,5},{2,6},{3,7},{4,0},{5,1},{6,2},{7,3},{8,12},{9,13},{10,... | collective-permute-start | bytes 393224 | tf_op jit(solution)/shard_map/ppermute | solution.py:52
  37.2 1.5 %collective-permute-start.4 = (bf16[64,1024]{1,0:T(8,128)(2,1)S(1)}, bf16[64,1024]{1,0:T(8,128)(2,1)S(1)}, u32[]{:S(2)}, u32[]{:S(2)}) collective-permute-start(bf16[64,1024]{1,0:T(8,128)(2,1)S(1)} %get-tuple-element.33), channel_id=1, source_target_pairs={{0,5},{1,4},{2,7},{3,6},{4,1},{5,0},{6,3},{7,2},{8,13},{9,12},{10,... | collective-permute-start | bytes 393224 | tf_op jit(solution)/shard_map/ppermute | solution.py:52
  38.7 0.0 collective-permute-done.refs_4_.refs_3_
  38.7 1.7 %collective-permute-start.5 = (bf16[64,1024]{1,0:T(8,128)(2,1)S(1)}, bf16[64,1024]{1,0:T(8,128)(2,1)S(1)}, u32[]{:S(2)}, u32[]{:S(2)}) collective-permute-start(bf16[64,1024]{1,0:T(8,128)(2,1)S(1)} %get-tuple-element.34), channel_id=1, source_target_pairs={{0,6},{1,7},{2,0},{3,1},{4,2},{5,3},{6,4},{7,5},{8,14},{9,15},{10,... | collective-permute-start | bytes 393224 | tf_op jit(solution)/shard_map/ppermute | solution.py:52
  40.4 0.0 collective-permute-done.1.refs_5_.refs_4_
  40.4 0.3 collective-permute-start.6
  40.7 6.0 %intra.1.refs_0_ = f32[512,1024]{1,0:T(8,128)} custom-call(bf16[512,1024]{1,0:T(8,128)(2,1)} %q_ref.3, bf16[512,1024]{1,0:T(8,128)(2,1)} %k_hbm.1, bf16[512,1024]{1,0:T(8,128)(2,1)} %v_hbm.1), custom_call_target="tpu_custom_call" | custom-call | flops 1073741824 | bytes 5242880 | tf_op jit(solution)/shard_map/intra/pallas_call | solution.py:377
  46.7 0.0 copy-done.3
  46.7 0.0 copy-done.5
  46.7 0.0 copy-done.6
  46.7 0.0 collective-permute-done.2.refs_6_.refs_5_
  46.8 0.0 copy-start.7
  46.8 0.1 collective-permute-done.3.refs_7_.refs_6_
  46.8 1.9 %collective-permute-done.4.refs_8_.refs_7_ = bf16[64,1024]{1,0:T(8,128)(2,1)S(1)} collective-permute-done((bf16[64,1024]{1,0:T(8,128)(2,1)S(1)}, bf16[64,1024]{1,0:T(8,128)(2,1)S(1)}, u32[]{:S(2)}, u32[]{:S(2)}) %collective-permute-start.4) | collective-permute-done | bytes 131104 | tf_op jit(solution)/shard_map/ppermute | solution.py:52
  48.7 0.0 collective-permute-done.5.refs_9_.refs_8_
  48.7 1.1 collective-permute-done.6.refs_10_.refs_9_
  49.8 0.0 all-to-all-done.1
  49.8 0.0 copy-done.7
  49.8 0.0 copy-done.8
  49.8 0.0 copy-done.9
  49.8 0.0 copy-done.10
  49.8 3.3 %outs.1 = (f32[8,8,128]{2,1,0:T(8,128)S(1)}, bf16[64,1024]{1,0:T(8,128)(2,1)}, bf16[64,1024]{1,0:T(8,128)(2,1)}, bf16[64,1024]{1,0:T(8,128)(2,1)}, bf16[64,1024]...) custom-call(f32[512,1024]{1,0:T(8,128)} %intra.1.refs_0_, ...), custom_call_target="tpu_custom_call" | custom-call | flops 134217728 | bytes 5242880 | tf_op jit(solution)/shard_map/outs/pallas_call | solution.py:389
  53.1 9.7 %all_to_all.26.refs_0_ = f32[8,8,128]{2,1,0:T(8,128)S(1)} all-to-all(f32[8,8,128]{2,1,0:T(8,128)S(1)} %get-tuple-element.36), channel_id=1, replica_groups=mesh['seq'=32,'head'=8] {'head'}, dimensions={0} | all-to-all | bytes 65536 | tf_op jit(solution)/shard_map/all_to_all | solution.py:402
  62.8 0.0 copy-start.12
  62.8 0.0 copy-start.11
  62.8 4.2 %grads.1 = (bf16[8,128,128]{2,1,0:T(8,128)(2,1)S(1)}, bf16[512,1024]{1,0:T(8,128)(2,1)}) custom-call(f32[8,8,128]{2,1,0:T(8,128)S(1)} %all_to_all.26.refs_0_, bf16[512,1024]{1,0:T(8,128)(2,1)} %q_ref.3, bf16[64,1024]{1,0:T(8,128)(2,1)} %copy-done.3, bf16[64,1024]{1,0:T(8,128)(2,1)} %copy-done.5, bf16[64,1024]{1,0:T(8,128)(2,1)} %copy-done.6, ...), custom_call_target="tpu_custom_call" | custom-call | flops 134217728 | bytes 4194304 | tf_op jit(solution)/shard_map/grads/pallas_call | solution.py:404
  67.0 21.8 %all_to_all.27.x_ref = bf16[32,32,128]{2,1,0:T(8,128)(2,1)S(1)} all-to-all(bf16[32,32,128]{2,1,0:T(8,128)(2,1)S(1)} %bitcast.9), channel_id=1, replica_groups=mesh['seq'=32,'head'=8] {'seq'}, dimensions={0} | all-to-all | bytes 524288 | tf_op jit(solution)/shard_map/all_to_all | solution.py:346
  88.9 0.7 running.3
  89.6 4.6 %all-to-all-start.4 = ((bf16[32,32,128]{2,1,0:T(8,128)(2,1)}), bf16[32,32,128]{2,1,0:T(8,128)(2,1)S(1)}, u32[]{:S(2)}, u32[]{:S(2)}) async-start(bf16[32,32,128]{2,1,0:T(8,128)(2,1)} %running.3), calls=%async_computation.4 | async-start | bytes 524288 | tf_op jit(solution)/shard_map/all_to_all | solution.py:354
  94.2 0.3 collective-permute-start.7
  94.5 0.0 copy-done.16
  94.5 0.6 collective-permute-start.8
  95.1 0.2 collective-permute-start.9
  95.3 3.7 %collective-permute-start.10 = (bf16[64,1024]{1,0:T(8,128)(2,1)S(1)}, bf16[64,1024]{1,0:T(8,128)(2,1)S(1)}, u32[]{:S(2)}, u32[]{:S(2)}) collective-permute-start(bf16[64,1024]{1,0:T(8,128)(2,1)S(1)} %copy-done.14), channel_id=1, source_target_pairs={{0,4},{1,5},{2,6},{3,7},{4,0},{5,1},{6,2},{7,3},{8,12},{9,13},{10,... | collective-permute-start | bytes 393224 | tf_op jit(solution)/shard_map/ppermute | solution.py:52
  99.0 0.0 copy-done.13
  99.0 0.0 collective-permute-start.11
  99.1 0.0 collective-permute-done.7.refs_1_
  99.1 2.3 %collective-permute-start.12 = (bf16[64,1024]{1,0:T(8,128)(2,1)S(1)}, bf16[64,1024]{1,0:T(8,128)(2,1)S(1)}, u32[]{:S(2)}, u32[]{:S(2)}) collective-permute-start(bf16[64,1024]{1,0:T(8,128)(2,1)S(1)} %copy-done.12), channel_id=1, source_target_pairs={{0,6},{1,7},{2,0},{3,1},{4,2},{5,3},{6,4},{7,5},{8,14},{9,15},{10,... | collective-permute-start | bytes 393224 | tf_op jit(solution)/shard_map/ppermute | solution.py:52
  101.3 0.7 collective-permute-done.8.refs_2_
  102.1 0.5 collective-permute-start.13
  102.6 10.5 %backs.1 = (bf16[512,1024]{1,0:T(8,128)(2,1)}, f32[512,1024]{1,0:T(8,128)}, f32[512,1024]{1,0:T(8,128)}) custom-call(bf16[512,1024]{1,0:T(8,128)(2,1)} %q_ref.3, bf16[512,1024]{1,0:T(8,128)(2,1)} %k_hbm.1, bf16[512,1024]{1,0:T(8,128)(2,1)} %v_hbm.1, bf16[512,1024]{1,0:T(8,128)(2,1)} %get-tuple-element.45.do_ref, bf16[8,128,128]{2,1,0:T(8,128)(2,1)S(1)} %bitcast.6), custom_call_target="tpu_custom_call" | custom-call | flops 2147483648 | bytes 9437184 | tf_op jit(solution)/shard_map/backs/pallas_call | solution.py:425
  113.0 0.0 collective-permute-done.9.refs_3_
  113.0 0.0 collective-permute-done.10.refs_4_
  113.0 0.0 collective-permute-done.11.refs_5_
  113.0 0.0 collective-permute-done.12.refs_6_
  113.0 0.0 collective-permute-done.13.refs_7_
  113.1 2.6 %gates.1 = bf16[64,8192]{1,0:T(8,128)(2,1)} custom-call(bf16[64,1024]{1,0:T(8,128)(2,1)S(1)} %copy-done.2, bf16[64,1024]{1,0:T(8,128)(2,1)S(1)} %collective-permute-done.7.refs_1_, bf16[64,1024]{1,0:T(8,128)(2,1)S(1)} %collective-permute-done.8.refs_2_, bf16[64,1024]{1,0:T(8,128)(2,1)S(1)} %collective-permute-done.9.refs_3_, ...), custom_call_target="tpu_custom_call" | custom-call | flops 10485760 | bytes 4194304 | tf_op jit(solution)/shard_map/gates/pallas_call | solution.py:417
  115.6 0.0 all-to-all-done.4
  115.6 4.4 %last.1 = (bf16[512,1024]{1,0:T(8,128)(2,1)}, bf16[512,1024]{1,0:T(8,128)(2,1)}) custom-call(f32[512,1024]{1,0:T(8,128)} %get-tuple-element.47.ak_hbm, f32[512,1024]{1,0:T(8,128)} %get-tuple-element.48.av_hbm, bf16[512,1024]{1,0:T(8,128)(2,1)} %k_hbm.1, bf16[512,1024]{1,0:T(8,128)(2,1)} %v_hbm.1, bf16[8,128,128]{2,1,0:T(8,128)(2,1)S(1)} %bitcast.7), custom_call_target="tpu_custom_call" | custom-call | flops 268435456 | bytes 8388608 | tf_op jit(solution)/shard_map/last/pallas_call | solution.py:436
  (15 shorter events, 0.0 us)
Async XLA Ops:
  0.6 31.3 %copy-start.1 = (bf16[64,8192]{1,0:T(8,128)(2,1)S(1)}, bf16[64,8192]{1,0:T(8,128)(2,1)}, u32[]{:S(2)}) copy-start(bf16[64,8192]{1,0:T(8,128)(2,1)} %refs_9_.1) | copy-start | bytes 3145732
  0.6 31.3 %copy-start = (bf16[64,8192]{1,0:T(8,128)(2,1)S(1)}, bf16[64,8192]{1,0:T(8,128)(2,1)}, u32[]{:S(2)}) copy-start(bf16[64,8192]{1,0:T(8,128)(2,1)} %refs_8_.1) | copy-start | bytes 3145732
  0.7 31.3 %copy-start.4 = (f32[8192]{0:T(1024)S(1)}, f32[8192]{0:T(1024)}, u32[]{:S(2)}) copy-start(f32[8192]{0:T(1024)} %param.10) | copy-start | bytes 98308
  27.4 22.4 %all-to-all-start.1 = ((bf16[32,32,128]{2,1,0:T(8,128)(2,1)}), bf16[32,32,128]{2,1,0:T(8,128)(2,1)S(1)}, u32[]{:S(2)}, u32[]{:S(2)}) async-start(bf16[32,32,128]{2,1,0:T(8,128)(2,1)} %running.2), calls=%async_computation.1 | async-start | bytes 524288 | tf_op jit(solution)/shard_map/all_to_all | solution.py:354
  32.5 14.2 %copy-start.3 = (bf16[64,1024]{1,0:T(8,128)(2,1)}, bf16[64,1024]{1,0:T(8,128)(2,1)S(1)}, u32[]{:S(2)}) copy-start(bf16[64,1024]{1,0:T(8,128)(2,1)S(1)} %get-tuple-element.28.refs_3_.refs_2_) | copy-start | bytes 393220
  32.5 6.1 %collective-permute-start = (bf16[64,1024]{1,0:T(8,128)(2,1)S(1)}, bf16[64,1024]{1,0:T(8,128)(2,1)S(1)}, u32[]{:S(2)}, u32[]{:S(2)}) collective-permute-start(bf16[64,1024]{1,0:T(8,128)(2,1)S(1)} %get-tuple-element.29), channel_id=1, source_target_pairs={{0,1},{1,0},{2,3},{3,2},{4,5},{5,4},{6,7},{7,6},{8,9},{9,8},{10,11... | collective-permute-start | bytes 393224 | tf_op jit(solution)/shard_map/ppermute | solution.py:52
  32.6 7.8 %collective-permute-start.1 = (bf16[64,1024]{1,0:T(8,128)(2,1)S(1)}, bf16[64,1024]{1,0:T(8,128)(2,1)S(1)}, u32[]{:S(2)}, u32[]{:S(2)}) collective-permute-start(bf16[64,1024]{1,0:T(8,128)(2,1)S(1)} %get-tuple-element.30), channel_id=1, source_target_pairs={{0,2},{1,3},{2,4},{3,5},{4,6},{5,7},{6,0},{7,1},{8,10},{9,11},{10,... | collective-permute-start | bytes 393224 | tf_op jit(solution)/shard_map/ppermute | solution.py:52
  34.2 12.5 %collective-permute-start.2 = (bf16[64,1024]{1,0:T(8,128)(2,1)S(1)}, bf16[64,1024]{1,0:T(8,128)(2,1)S(1)}, u32[]{:S(2)}, u32[]{:S(2)}) collective-permute-start(bf16[64,1024]{1,0:T(8,128)(2,1)S(1)} %get-tuple-element.31), channel_id=1, source_target_pairs={{0,3},{1,2},{2,5},{3,4},{4,7},{5,6},{6,1},{7,0},{8,11},{9,10},{10,... | collective-permute-start | bytes 393224 | tf_op jit(solution)/shard_map/ppermute | solution.py:52
  35.5 11.4 %collective-permute-start.3 = (bf16[64,1024]{1,0:T(8,128)(2,1)S(1)}, bf16[64,1024]{1,0:T(8,128)(2,1)S(1)}, u32[]{:S(2)}, u32[]{:S(2)}) collective-permute-start(bf16[64,1024]{1,0:T(8,128)(2,1)S(1)} %get-tuple-element.32), channel_id=1, source_target_pairs={{0,4},{1,5},{2,6},{3,7},{4,0},{5,1},{6,2},{7,3},{8,12},{9,13},{10,... | collective-permute-start | bytes 393224 | tf_op jit(solution)/shard_map/ppermute | solution.py:52
  37.2 11.5 %collective-permute-start.4 = (bf16[64,1024]{1,0:T(8,128)(2,1)S(1)}, bf16[64,1024]{1,0:T(8,128)(2,1)S(1)}, u32[]{:S(2)}, u32[]{:S(2)}) collective-permute-start(bf16[64,1024]{1,0:T(8,128)(2,1)S(1)} %get-tuple-element.33), channel_id=1, source_target_pairs={{0,5},{1,4},{2,7},{3,6},{4,1},{5,0},{6,3},{7,2},{8,13},{9,12},{10,... | collective-permute-start | bytes 393224 | tf_op jit(solution)/shard_map/ppermute | solution.py:52
  38.7 8.1 %copy-start.5 = (bf16[64,1024]{1,0:T(8,128)(2,1)}, bf16[64,1024]{1,0:T(8,128)(2,1)S(1)}, u32[]{:S(2)}) copy-start(bf16[64,1024]{1,0:T(8,128)(2,1)S(1)} %collective-permute-done.refs_4_.refs_3_) | copy-start | bytes 393220
  38.7 10.0 %collective-permute-start.5 = (bf16[64,1024]{1,0:T(8,128)(2,1)S(1)}, bf16[64,1024]{1,0:T(8,128)(2,1)S(1)}, u32[]{:S(2)}, u32[]{:S(2)}) collective-permute-start(bf16[64,1024]{1,0:T(8,128)(2,1)S(1)} %get-tuple-element.34), channel_id=1, source_target_pairs={{0,6},{1,7},{2,0},{3,1},{4,2},{5,3},{6,4},{7,5},{8,14},{9,15},{10,... | collective-permute-start | bytes 393224 | tf_op jit(solution)/shard_map/ppermute | solution.py:52
  40.4 6.3 %copy-start.6 = (bf16[64,1024]{1,0:T(8,128)(2,1)}, bf16[64,1024]{1,0:T(8,128)(2,1)S(1)}, u32[]{:S(2)}) copy-start(bf16[64,1024]{1,0:T(8,128)(2,1)S(1)} %collective-permute-done.1.refs_5_.refs_4_) | copy-start | bytes 393220
  40.4 9.4 %collective-permute-start.6 = (bf16[64,1024]{1,0:T(8,128)(2,1)S(1)}, bf16[64,1024]{1,0:T(8,128)(2,1)}, u32[]{:S(2)}, u32[]{:S(2)}) collective-permute-start(bf16[64,1024]{1,0:T(8,128)(2,1)S(1)} %get-tuple-element.35), channel_id=1, source_target_pairs={{0,7},{1,6},{2,1},{3,0},{4,3},{5,2},{6,5},{7,4},{8,15},{9,14},{10,... | collective-permute-start | bytes 393224 | tf_op jit(solution)/shard_map/ppermute | solution.py:52
  46.8 3.0 %copy-start.7 = (bf16[64,1024]{1,0:T(8,128)(2,1)}, bf16[64,1024]{1,0:T(8,128)(2,1)S(1)}, u32[]{:S(2)}) copy-start(bf16[64,1024]{1,0:T(8,128)(2,1)S(1)} %collective-permute-done.2.refs_6_.refs_5_) | copy-start | bytes 393220
  46.8 3.0 %copy-start.8 = (bf16[64,1024]{1,0:T(8,128)(2,1)}, bf16[64,1024]{1,0:T(8,128)(2,1)S(1)}, u32[]{:S(2)}) copy-start(bf16[64,1024]{1,0:T(8,128)(2,1)S(1)} %collective-permute-done.3.refs_7_.refs_6_) | copy-start | bytes 393220
  48.7 1.1 copy-start.9
  48.7 1.1 copy-start.10
  62.8 31.6 %copy-start.16 = (bf16[64,1024]{1,0:T(8,128)(2,1)S(1)}, bf16[64,1024]{1,0:T(8,128)(2,1)}, u32[]{:S(2)}) copy-start(bf16[64,1024]{1,0:T(8,128)(2,1)} %get-tuple-element.39.refs_12_) | copy-start | bytes 393220
  62.8 32.3 %copy-start.15 = (bf16[64,1024]{1,0:T(8,128)(2,1)S(1)}, bf16[64,1024]{1,0:T(8,128)(2,1)}, u32[]{:S(2)}) copy-start(bf16[64,1024]{1,0:T(8,128)(2,1)} %get-tuple-element.40.refs_13_) | copy-start | bytes 393220
  62.8 32.5 %copy-start.14 = (bf16[64,1024]{1,0:T(8,128)(2,1)S(1)}, bf16[64,1024]{1,0:T(8,128)(2,1)}, u32[]{:S(2)}) copy-start(bf16[64,1024]{1,0:T(8,128)(2,1)} %get-tuple-element.41.refs_14_) | copy-start | bytes 393220
  62.8 36.2 %copy-start.13 = (bf16[64,1024]{1,0:T(8,128)(2,1)S(1)}, bf16[64,1024]{1,0:T(8,128)(2,1)}, u32[]{:S(2)}) copy-start(bf16[64,1024]{1,0:T(8,128)(2,1)} %get-tuple-element.42.refs_15_) | copy-start | bytes 393220
  62.8 36.2 %copy-start.12 = (bf16[64,1024]{1,0:T(8,128)(2,1)S(1)}, bf16[64,1024]{1,0:T(8,128)(2,1)}, u32[]{:S(2)}) copy-start(bf16[64,1024]{1,0:T(8,128)(2,1)} %get-tuple-element.43.refs_16_) | copy-start | bytes 393220
  62.8 39.2 %copy-start.11 = (bf16[64,1024]{1,0:T(8,128)(2,1)S(1)}, bf16[64,1024]{1,0:T(8,128)(2,1)}, u32[]{:S(2)}) copy-start(bf16[64,1024]{1,0:T(8,128)(2,1)} %get-tuple-element.44.refs_17_) | copy-start | bytes 393220
  89.6 26.0 %all-to-all-start.4 = ((bf16[32,32,128]{2,1,0:T(8,128)(2,1)}), bf16[32,32,128]{2,1,0:T(8,128)(2,1)S(1)}, u32[]{:S(2)}, u32[]{:S(2)}) async-start(bf16[32,32,128]{2,1,0:T(8,128)(2,1)} %running.3), calls=%async_computation.4 | async-start | bytes 524288 | tf_op jit(solution)/shard_map/all_to_all | solution.py:354
  94.2 4.9 %collective-permute-start.7 = (bf16[64,1024]{1,0:T(8,128)(2,1)}, bf16[64,1024]{1,0:T(8,128)(2,1)S(1)}, u32[]{:S(2)}, u32[]{:S(2)}) collective-permute-start(bf16[64,1024]{1,0:T(8,128)(2,1)} %get-tuple-element.38.refs_11_), channel_id=1, source_target_pairs={{0,1},{1,0},{2,3},{3,2},{4,5},{5,4},{6,7},{7,6},{8,9},{9,8},{10,11... | collective-permute-start | bytes 393224 | tf_op jit(solution)/shard_map/ppermute | solution.py:52
  94.5 7.6 %collective-permute-start.8 = (bf16[64,1024]{1,0:T(8,128)(2,1)S(1)}, bf16[64,1024]{1,0:T(8,128)(2,1)S(1)}, u32[]{:S(2)}, u32[]{:S(2)}) collective-permute-start(bf16[64,1024]{1,0:T(8,128)(2,1)S(1)} %copy-done.16), channel_id=1, source_target_pairs={{0,2},{1,3},{2,4},{3,5},{4,6},{5,7},{6,0},{7,1},{8,10},{9,11},{10,... | collective-permute-start | bytes 393224 | tf_op jit(solution)/shard_map/ppermute | solution.py:52
  95.1 17.9 %collective-permute-start.9 = (bf16[64,1024]{1,0:T(8,128)(2,1)S(1)}, bf16[64,1024]{1,0:T(8,128)(2,1)S(1)}, u32[]{:S(2)}, u32[]{:S(2)}) collective-permute-start(bf16[64,1024]{1,0:T(8,128)(2,1)S(1)} %copy-done.15), channel_id=1, source_target_pairs={{0,3},{1,2},{2,5},{3,4},{4,7},{5,6},{6,1},{7,0},{8,11},{9,10},{10,... | collective-permute-start | bytes 393224 | tf_op jit(solution)/shard_map/ppermute | solution.py:52
  95.3 17.7 %collective-permute-start.10 = (bf16[64,1024]{1,0:T(8,128)(2,1)S(1)}, bf16[64,1024]{1,0:T(8,128)(2,1)S(1)}, u32[]{:S(2)}, u32[]{:S(2)}) collective-permute-start(bf16[64,1024]{1,0:T(8,128)(2,1)S(1)} %copy-done.14), channel_id=1, source_target_pairs={{0,4},{1,5},{2,6},{3,7},{4,0},{5,1},{6,2},{7,3},{8,12},{9,13},{10,... | collective-permute-start | bytes 393224 | tf_op jit(solution)/shard_map/ppermute | solution.py:52
  99.0 14.0 %collective-permute-start.11 = (bf16[64,1024]{1,0:T(8,128)(2,1)S(1)}, bf16[64,1024]{1,0:T(8,128)(2,1)S(1)}, u32[]{:S(2)}, u32[]{:S(2)}) collective-permute-start(bf16[64,1024]{1,0:T(8,128)(2,1)S(1)} %copy-done.13), channel_id=1, source_target_pairs={{0,5},{1,4},{2,7},{3,6},{4,1},{5,0},{6,3},{7,2},{8,13},{9,12},{10,... | collective-permute-start | bytes 393224 | tf_op jit(solution)/shard_map/ppermute | solution.py:52
  99.1 14.0 %collective-permute-start.12 = (bf16[64,1024]{1,0:T(8,128)(2,1)S(1)}, bf16[64,1024]{1,0:T(8,128)(2,1)S(1)}, u32[]{:S(2)}, u32[]{:S(2)}) collective-permute-start(bf16[64,1024]{1,0:T(8,128)(2,1)S(1)} %copy-done.12), channel_id=1, source_target_pairs={{0,6},{1,7},{2,0},{3,1},{4,2},{5,3},{6,4},{7,5},{8,14},{9,15},{10,... | collective-permute-start | bytes 393224 | tf_op jit(solution)/shard_map/ppermute | solution.py:52
  102.1 11.0 %collective-permute-start.13 = (bf16[64,1024]{1,0:T(8,128)(2,1)S(1)}, bf16[64,1024]{1,0:T(8,128)(2,1)S(1)}, u32[]{:S(2)}, u32[]{:S(2)}) collective-permute-start(bf16[64,1024]{1,0:T(8,128)(2,1)S(1)} %copy-done.11), channel_id=1, source_target_pairs={{0,7},{1,6},{2,1},{3,0},{4,3},{5,2},{6,5},{7,4},{8,15},{9,14},{10,... | collective-permute-start | bytes 393224 | tf_op jit(solution)/shard_map/ppermute | solution.py:52
  102.6 10.5 %copy-start.2 = (bf16[64,1024]{1,0:T(8,128)(2,1)S(1)}, bf16[64,1024]{1,0:T(8,128)(2,1)}, u32[]{:S(2)}) copy-start(bf16[64,1024]{1,0:T(8,128)(2,1)} %get-tuple-element.37.refs_10_.refs_0_) | copy-start | bytes 393220

commit v3 on v2

v3 whole, which is shorter than its diff:
```python
import functools

import jax
import jax.numpy as jnp
from jax import lax
from jax.experimental import pallas as pl
from jax.experimental.pallas import tpu as pltpu
from jax.sharding import PartitionSpec as P

HEAD_DIM = 128
EPS = 1e-06
F32 = jnp.float32
BF16 = jnp.bfloat16


def mm(a, b):
    return lax.dot_general(a, b, (((1,), (0,)), ((), ())), preferred_element_type=F32)


def mm_bt(a, b):
    return lax.dot_general(a, b, (((1,), (1,)), ((), ())), preferred_element_type=F32)


def mm_at(a, b):
    return lax.dot_general(a, b, (((0,), (0,)), ((), ())), preferred_element_type=F32)


def params():
    return pltpu.CompilerParams(vmem_limit_bytes=24 * 2**20)


def cost(flops, nbytes):
    return pl.CostEstimate(flops=int(flops), bytes_accessed=int(nbytes), transcendentals=0)


def in_hbm(x):
    return pltpu.with_memory_space_constraint(x, pltpu.HBM)


def in_vmem(x):
    return pltpu.with_memory_space_constraint(x, pltpu.VMEM)


def place(n, dx, dc, sign):
    me = lax.axis_index("head")
    chip, core = me // 2, me % 2
    flip = core + dc - 2 * core * dc
    return lax.rem(chip + sign * dx + n // 2, n // 2) * 2 + flip


def send_all(bundles):
    n = 2 * len(bundles)
    same = [bundles[0]]
    for dx in range(1, n // 2):
        pairs = [(i, (i + 2 * dx) % n) for i in range(n)]
        same.append(lax.ppermute(bundles[dx], "head", pairs))
    other = [lax.ppermute(b, "head", [(i, i ^ 1) for i in range(n)]) for b in same]
    return same + other


def parts(n):
    return [(dx + dc * (n // 2), dx, dc) for dx in range(n // 2) for dc in range(2)]


def start_all(copies):
    for c in copies:
        c.start()
    return copies


def wait_all(copies):
    for c in copies:
        c.wait()


def columns(i):
    return pl.ds(2 * HEAD_DIM * i, 2 * HEAD_DIM)


def by_pairs(src, dst, sems, at):
    n = src.shape[1] // (2 * HEAD_DIM)
    return [
        pltpu.make_async_copy(src.at[:, columns(i)], dst.at[:, columns(i)], sems.at[at + i])
        for i in range(n)
    ]


def rows_of(n, dx, dc, sign, rows):
    return pl.ds(pl.multiple_of(place(n, dx, dc, sign) * rows, rows), rows)


def assemble(n, bundles, dst, sems, at):
    rows = bundles[0].shape[1]
    return [
        pltpu.make_async_copy(
            bundles[k].at[dc], dst.at[rows_of(n, dx, dc, -1, rows), :], sems.at[at + i]
        )
        for i, (k, dx, dc) in enumerate(parts(n))
    ]


def state_kernel(a_hbm, b_hbm, s_ref, a_ref, b_ref, sems):
    d = HEAD_DIM
    n = s_ref.shape[0] // 2
    ca, cb = by_pairs(a_hbm, a_ref, sems, 0), by_pairs(b_hbm, b_ref, sems, n)
    for i in range(n):
        ca[i].start()
        cb[i].start()
    for i in range(n):
        ca[i].wait()
        cb[i].wait()
        for h in range(2 * i, 2 * i + 2):
            cols = slice(h * d, (h + 1) * d)
            s_ref[h] = mm_at(a_ref[:, cols], b_ref[:, cols]).astype(s_ref.dtype)


def running_kernel(reverse, x_ref, *refs):
    o_ref = refs[-1]
    n = x_ref.shape[0]
    total = jnp.zeros(x_ref.shape[1:], F32)
    for k in range(n):
        at = n - 1 - k if reverse else k
        o_ref[at] = total.astype(o_ref.dtype)
        total = total + x_ref[at].astype(F32)


def weigh_kernel(n, gate_ref, grad_ref, gain_ref, *w_refs):
    own = gate_ref.shape[1] // n
    for dx in range(n // 2):
        for dc in range(2):
            cols = pl.ds(pl.multiple_of(place(n, dx, dc, 1) * own, own), own)
            g = gate_ref[:, cols].astype(F32)
            w = grad_ref[:, cols].astype(F32) * gain_ref[:, cols] * g * jax.nn.sigmoid(g)
            w_refs[dx][dc] = w.astype(BF16)


def lower(n):
    return lax.broadcasted_iota(jnp.int32, (n, n), 0) >= lax.broadcasted_iota(jnp.int32, (n, n), 1)


def upper(n):
    return lax.broadcasted_iota(jnp.int32, (n, n), 0) <= lax.broadcasted_iota(jnp.int32, (n, n), 1)


def intra_kernel(q_hbm, k_hbm, v_hbm, _, i_hbm, s_hbm, *refs):
    q_ref, k_ref, v_ref, i_ref, s_ref, sems, out_sems = refs
    t, own = q_ref.shape
    half = t // 2
    n = own // (2 * HEAD_DIM)
    ins = [
        by_pairs(src, dst, sems, n * j)
        for j, (src, dst) in enumerate(((q_hbm, q_ref), (k_hbm, k_ref), (v_hbm, v_ref)))
    ]
    for i in range(n):
        for c in ins:
            c[i].start()
    outs = [
        pltpu.make_async_copy(s_ref.at[pl.ds(2 * i, 2)], s_hbm.at[pl.ds(2 * i, 2)], out_sems.at[i])
        for i in range(n)
    ]
    more = by_pairs(i_ref, i_hbm, out_sems, n)
    keep = lower(half)
    one, two = slice(0, half), slice(half, t)
    for i in range(n):
        for c in ins:
            c[i].wait()
        for h in range(2 * i, 2 * i + 2):
            cols = slice(h * HEAD_DIM, (h + 1) * HEAD_DIM)
            q, k, v = q_ref[:, cols], k_ref[:, cols], v_ref[:, cols]
            s0 = jnp.where(keep, mm_bt(q[one], k[one]), 0.0).astype(BF16)
            i_ref[one, cols] = mm(s0, v[one])
            s2 = mm_bt(q[two], k[one]).astype(BF16)
            s1 = jnp.where(keep, mm_bt(q[two], k[two]), 0.0).astype(BF16)
            i_ref[two, cols] = mm(s2, v[one]) + mm(s1, v[two])
            s_ref[h, 0], s_ref[h, 1], s_ref[h, 2] = s0, s1, s2
        outs[i].start()
        more[i].start()
    wait_all(outs + more)


def out_kernel(n_head, *refs):
    i_hbm, q_hbm, p_ref = refs[:3]
    w_any = refs[3 : 3 + n_head]
    sums_ref, o_ref, w_ref, q_ref = refs[3 + n_head : 7 + n_head]
    *bundles, i_ref, sems, out_sems = refs[7 + n_head :]
    d = HEAD_DIM
    t, own = q_ref.shape
    rows = t // n_head
    blocks = t // d
    cq = [
        pltpu.make_async_copy(q_hbm.at[pl.ds(r * d, d), :], q_ref.at[pl.ds(r * d, d), :], sems.at[r])
        for r in range(blocks)
    ]
    ci = [
        pltpu.make_async_copy(
            i_hbm.at[pl.ds(r * d, d), :], i_ref.at[pl.ds(r * d, d), :], sems.at[blocks + r]
        )
        for r in range(blocks)
    ]
    for r in range(blocks):
        cq[r].start()
        ci[r].start()
    cw = start_all(assemble(n_head, w_any, w_ref, sems, 2 * blocks))
    for r in range(blocks):
        at = slice(r * d, (r + 1) * d)
        cq[r].wait()
        ci[r].wait()
        for h in range(own // d):
            cols = slice(h * d, (h + 1) * d)
            o_ref[at, cols] = (i_ref[at, cols] + mm(q_ref[at, cols], p_ref[h])).astype(BF16)
    co = start_all(
        [
            pltpu.make_async_copy(
                o_ref.at[rows_of(n_head, dx, dc, 1, rows), :],
                bundles[dx].at[dc],
                out_sems.at[2 * dx + dc],
            )
            for dx in range(n_head // 2)
            for dc in range(2)
        ]
    )
    wait_all(cw)
    lines = [None] * (2 * blocks)
    for r in range(blocks):
        at = slice(r * d, (r + 1) * d)
        sq, cross = None, None
        for h in range(own // d):
            cols = slice(h * d, (h + 1) * d)
            o = o_ref[at, cols].astype(F32)
            a, b = o * o, o * w_ref[at, cols].astype(F32)
            sq, cross = (a, b) if sq is None else (sq + a, cross + b)
        lines[r] = jnp.sum(jnp.transpose(sq), axis=0, keepdims=True)
        lines[blocks + r] = jnp.sum(jnp.transpose(cross), axis=0, keepdims=True)
    tile = jnp.concatenate(lines, axis=0)
    for k in range(n_head):
        sums_ref[k] = tile
    wait_all(co)


def grad_kernel(width, sums_ref, q_ref, w_ref, o_ref, z_ref, do_hbm, do_ref, sems):
    d = HEAD_DIM
    t, own = q_ref.shape
    tile = jnp.sum(sums_ref[...], axis=0)
    blocks = t // d
    turned = jnp.transpose(jnp.concatenate([tile] * (d // tile.shape[0]), axis=0))
    inv = lax.rsqrt(turned[:, :blocks] / width + EPS)
    fall = inv * inv * inv * (turned[:, blocks : 2 * blocks] / width)
    copies = []
    for r in range(blocks):
        at = slice(r * d, (r + 1) * d)
        a = jnp.broadcast_to(inv[:, r : r + 1], (d, d))
        b = jnp.broadcast_to(fall[:, r : r + 1], (d, d))
        for h in range(own // d):
            cols = slice(h * d, (h + 1) * d)
            do = a * w_ref[at, cols].astype(F32) - b * o_ref[at, cols].astype(F32)
            do_ref[at, cols] = do.astype(BF16)
        copies.append(
            pltpu.make_async_copy(
                do_ref.at[pl.ds(r * d, d), :], do_hbm.at[pl.ds(r * d, d), :], sems.at[r]
            )
        )
        copies[r].start()
    for h in range(own // d):
        cols = slice(h * d, (h + 1) * d)
        z_ref[h] = mm_at(q_ref[:, cols], do_ref[:, cols]).astype(z_ref.dtype)
    wait_all(copies)


def back_kernel(
    q_hbm, k_hbm, v_hbm, do_hbm, t_hbm, p_ref, ak_hbm, av_hbm, gq_hbm,
    q_ref, k_ref, v_ref, do_ref, t_ref, ak_ref, av_ref, gq_ref, sems, out_sems,
):
    t, own = q_ref.shape
    half = t // 2
    n = own // (2 * HEAD_DIM)
    ins = [
        by_pairs(src, dst, sems, n * j)
        for j, (src, dst) in enumerate(
            ((do_hbm, do_ref), (v_hbm, v_ref), (k_hbm, k_ref), (q_hbm, q_ref))
        )
    ]
    ins.append(
        [
            pltpu.make_async_copy(
                t_hbm.at[pl.ds(2 * i, 2)], t_ref.at[pl.ds(2 * i, 2)], sems.at[4 * n + i]
            )
            for i in range(n)
        ]
    )
    for i in range(n):
        for c in ins:
            c[i].start()
    outs = [
        by_pairs(src, dst, out_sems, n * j)
        for j, (src, dst) in enumerate(((gq_ref, gq_hbm), (ak_ref, ak_hbm), (av_ref, av_hbm)))
    ]
    low = lower(half)
    one, two = slice(0, half), slice(half, t)
    for i in range(n):
        for c in ins:
            c[i].wait()
        for h in range(2 * i, 2 * i + 2):
            cols = slice(h * HEAD_DIM, (h + 1) * HEAD_DIM)
            q, k, v, do = q_ref[:, cols], k_ref[:, cols], v_ref[:, cols], do_ref[:, cols]
            qt, dot = q.T, do.T
            base = mm_bt(do, p_ref[h])
            g0 = jnp.where(low, mm_bt(do[one], v[one]), 0.0).astype(BF16)
            gq_ref[one, cols] = (mm(g0, k[one]) + base[one]).astype(BF16)
            g2 = mm_bt(do[two], v[one]).astype(BF16)
            g1 = jnp.where(low, mm_bt(do[two], v[two]), 0.0).astype(BF16)
            gq_ref[two, cols] = (mm(g2, k[one]) + mm(g1, k[two]) + base[two]).astype(BF16)
            ak_ref[one, cols] = (mm(qt[:, one], g0) + mm(qt[:, two], g2)).astype(BF16).T
            ak_ref[two, cols] = mm(qt[:, two], g1).astype(BF16).T
            s0, s1, s2 = t_ref[h, 0], t_ref[h, 1], t_ref[h, 2]
            av_ref[one, cols] = (mm(dot[:, one], s0) + mm(dot[:, two], s2)).astype(BF16).T
            av_ref[two, cols] = mm(dot[:, two], s1).astype(BF16).T
        for c in outs:
            c[i].start()
    for c in outs:
        wait_all(c)


def last_kernel(
    ak_hbm, av_hbm, k_hbm, v_hbm, s_ref, gk_hbm, gv_hbm,
    ak_ref, av_ref, k_ref, v_ref, gk_ref, gv_ref, sems, out_sems,
):
    d = HEAD_DIM
    t, own = k_ref.shape
    n = own // (2 * d)
    ins = [
        by_pairs(src, dst, sems, n * j)
        for j, (src, dst) in enumerate(
            ((k_hbm, k_ref), (av_hbm, av_ref), (v_hbm, v_ref), (ak_hbm, ak_ref))
        )
    ]
    for i in range(n):
        for c in ins:
            c[i].start()
    ck, cv = by_pairs(gk_ref, gk_hbm, out_sems, 0), by_pairs(gv_ref, gv_hbm, out_sems, n)
    for i in range(n):
        for c in ins:
            c[i].wait()
        for h in range(2 * i, 2 * i + 2):
            cols = slice(h * d, (h + 1) * d)
            for r in range(0, t, 256):
                rows = slice(r, r + 256)
                gv = av_ref[rows, cols].astype(F32) + mm(k_ref[rows, cols], s_ref[h])
                gv_ref[rows, cols] = gv.astype(BF16)
                gk = ak_ref[rows, cols].astype(F32) + mm_bt(v_ref[rows, cols], s_ref[h])
                gk_ref[rows, cols] = gk.astype(BF16)
        cv[i].start()
        ck[i].start()
    wait_all(ck + cv)


def gate_kernel(n, *refs):
    *o_refs, gate_ref, grad_ref, gain_ref, gg_ref = refs
    wide = o_refs[0].shape[2]
    total = None
    for k, _, dc in parts(n):
        o = o_refs[k][dc].astype(F32)
        s = o * o
        total = s if total is None else total + s
    inv = lax.rsqrt(jnp.sum(total, axis=1, keepdims=True) / (n * wide) + EPS)
    for k, dx, dc in parts(n):
        cols = pl.ds(pl.multiple_of(place(n, dx, dc, -1) * wide, wide), wide)
        g = gate_ref[:, cols].astype(F32)
        s = jax.nn.sigmoid(g)
        scaled = grad_ref[:, cols].astype(F32) * gain_ref[:, cols]
        normed = o_refs[k][dc].astype(F32) * inv
        gg_ref[:, cols] = (scaled * normed * s * (1.0 + g * (1.0 - s))).astype(BF16)


def on_device(query, key_in, value, gate, gain, grad_out):
    d = HEAD_DIM
    t, own = query.shape
    heads = own // d
    rows, width = gate.shape
    n_seq, n_head = lax.axis_size("seq"), lax.axis_size("head")
    pairs, chips = heads // 2, n_head // 2
    gain = gain.reshape(1, width)

    def sds(shape, dtype):
        return jax.ShapeDtypeStruct(shape, dtype)

    def dma(n):
        return pltpu.SemaphoreType.DMA((n,))

    anywhere = pl.BlockSpec(memory_space=pl.ANY)
    whole = pl.BlockSpec(memory_space=pltpu.VMEM)
    small = 2 * t * d * d * heads
    large = 2 * t * t * d * heads
    full = pltpu.VMEM((t, own), BF16)
    full32 = pltpu.VMEM((t, own), F32)
    piece = (n_seq, heads * d // n_seq, d)

    def exchange(states):
        return lax.all_to_all(states.reshape(piece), "seq", 0, 0, tiled=True)

    def running(states, reverse, *after):
        return pl.pallas_call(
            functools.partial(running_kernel, reverse),
            out_shape=pltpu.HBM(piece, BF16),
            in_specs=[whole] + [anywhere] * len(after),
            out_specs=whole,
            compiler_params=params(),
            cost_estimate=cost(heads * d * d, 4 * heads * d * d),
            name="running",
        )(states, *after)

    query, key_in, value = in_hbm(query), in_hbm(key_in), in_hbm(value)
    states = pl.pallas_call(
        state_kernel,
        out_shape=sds((heads, d, d), BF16),
        in_specs=[anywhere, anywhere],
        out_specs=whole,
        scratch_shapes=[full, full, dma(2 * pairs)],
        compiler_params=params(),
        cost_estimate=cost(2 * small, 4 * t * own),
        name="states",
    )(key_in, value)
    received = exchange(states)

    bundle = (2, rows, own)
    weighted = pl.pallas_call(
        functools.partial(weigh_kernel, n_head),
        out_shape=[sds(bundle, BF16)] * chips,
        compiler_params=params(),
        cost_estimate=cost(20 * rows * width, 6 * rows * width),
        name="weigh",
    )(gate, grad_out, gain)
    weighted = [in_hbm(w) for w in send_all(weighted)]

    tiles = (heads, 3, t // 2, t // 2)
    intra, scores = pl.pallas_call(
        intra_kernel,
        out_shape=[pltpu.HBM((t, own), F32), pltpu.HBM(tiles, BF16)],
        in_specs=[anywhere] * 4,
        out_specs=[anywhere, anywhere],
        scratch_shapes=[full] * 3
        + [full32, pltpu.VMEM(tiles, BF16), dma(3 * pairs), dma(2 * pairs)],
        compiler_params=params(),
        cost_estimate=cost(2 * large, 16 * t * own),
        name="intra",
    )(query, key_in, value, states)
    intra, scores = in_hbm(intra), in_hbm(scores)

    prefix = exchange(running(received, False, intra)).reshape(heads, d, d)

    tile = (n_head, 2 * t // d, d)
    sums, out, weighted, queries, *bundles = pl.pallas_call(
        functools.partial(out_kernel, n_head),
        out_shape=[sds(tile, F32), full, full, full] + [pltpu.HBM(bundle, BF16)] * chips,
        in_specs=[anywhere, anywhere, whole] + [anywhere] * n_head,
        out_specs=[whole] * 4 + [anywhere] * chips,
        scratch_shapes=[full32, dma(2 * t // d + n_head), dma(n_head)],
        compiler_params=params(),
        cost_estimate=cost(small, 10 * t * own),
        name="outs",
    )(intra, query, prefix, *weighted)
    sums = lax.all_to_all(sums, "head", 0, 0, tiled=True)

    states, grad_attn = pl.pallas_call(
        functools.partial(grad_kernel, float(width)),
        out_shape=[sds((heads, d, d), BF16), pltpu.HBM((t, own), BF16)],
        in_specs=[whole] * 4,
        out_specs=[whole, anywhere],
        scratch_shapes=[full, dma(t // d)],
        compiler_params=params(),
        cost_estimate=cost(small, 8 * t * own),
        name="grads",
    )(sums, in_vmem(queries), in_vmem(weighted), in_vmem(out))
    received = exchange(states)

    part_key, part_value, grad_query = pl.pallas_call(
        back_kernel,
        out_shape=[pltpu.HBM((t, own), BF16)] * 2 + [sds((t, own), BF16)],
        in_specs=[anywhere] * 5 + [whole],
        out_specs=[anywhere] * 3,
        scratch_shapes=[full] * 4 + [pltpu.VMEM(tiles, BF16)] + [full] * 3
        + [dma(5 * pairs), dma(3 * pairs)],
        compiler_params=params(),
        cost_estimate=cost(3 * large, 20 * t * own),
        name="backs",
    )(query, key_in, value, in_hbm(grad_attn), scores, prefix)
    part_key, part_value = in_hbm(part_key), in_hbm(part_value)
    suffix = exchange(running(received, True, part_key)).reshape(heads, d, d)

    token_rows = send_all(bundles)
    grad_gate = pl.pallas_call(
        functools.partial(gate_kernel, n_head),
        out_shape=sds((rows, width), BF16),
        compiler_params=params(),
        cost_estimate=cost(20 * rows * width, 8 * rows * width),
        name="gates",
    )(*token_rows, gate, grad_out, gain)

    grad_key, grad_value = pl.pallas_call(
        last_kernel,
        out_shape=[sds((t, own), BF16), sds((t, own), BF16)],
        in_specs=[anywhere] * 4 + [whole],
        out_specs=[anywhere] * 2,
        scratch_shapes=[full] * 6 + [dma(4 * pairs), dma(2 * pairs)],
        compiler_params=params(),
        cost_estimate=cost(2 * small, 16 * t * own),
        name="last",
    )(part_key, part_value, key_in, value, suffix)
    return grad_query, grad_key, grad_value, grad_gate


def solution(mesh):
    in_specs = (
        P("seq", "head"),
        P("seq", "head"),
        P("seq", "head"),
        P(("seq", "head"), None),
        P(),
        P(("seq", "head"), None),
    )
    out_specs = (P("seq", "head"), P("seq", "head"), P("seq", "head"), P(("seq", "head"), None))
    return jax.shard_map(
        on_device, mesh=mesh, in_specs=in_specs, out_specs=out_specs, check_vma=False
    )
```

time: 122 us -> 105 us (0.86); the launches traced: 120 us -> 105 us
  blocking collectives: 54.9 us -> 7.82 us
  starting transfers between devices: 24.9 us -> 46.2 us
  waiting for transfers between devices: 3.77 us -> 17.2 us
  Pallas kernels: 35.4 us -> 31.5 us
    all_to_all x2 -> x0, blocking collectives: 45.3 us -> none  [exchange(): states = lax.all_to_all(states.reshape(piece), 'seq', 0, 0, tiled=True)]
    all_to_all x2 -> x4, starting transfers between devices: 9.12 us -> 34.5 us  [exchange(): return lax.all_to_all(states.reshape(piece), 'seq', 0, 0, tiled=True)]
    all_to_all x2 -> x4, waiting for transfers between devices: 0.01 us -> 13.6 us  [exchange(): return lax.all_to_all(states.reshape(piece), 'seq', 0, 0, tiled=True)]
    pallas_call x6, Pallas kernels: 22.7 us -> 18 us  [the longest x1 7.71 us: on_device(): pl.pallas_call(back_kernel, out_shape=[pltpu.HBM((t, own), BF16)] * 2 + [...]
    ppermute x14, starting transfers between devices: 15.8 us -> 11.7 us  [the longest x6 9.53 us: send_all(): same.append(lax.ppermute(bundles[dx], 'head', pairs))]
    all_to_all x1, blocking collectives: 9.68 us -> 7.82 us  [on_device(): sums = lax.all_to_all(sums, 'head', 0, 0, tiled=True)]
  transfers between devices with their start and end apart: 16 -> 18, of which waited for: 4 -> 11; matrix products, arithmetic and copies ran while one was open for 0% -> 0% of each run, Pallas kernels for 16% -> 18%
where the time goes in v3:
time: 105 us
  starting transfers between devices  46.2 us (44%)
  Pallas kernels  31.5 us (30%)
  waiting for transfers between devices  17.2 us (16%)
  blocking collectives  7.82 us (7%)
    all_to_all x4, starting transfers between devices, exchange(): return lax.all_to_all(states.reshape(piece), 'seq', 0, 0, tiled=True)  34.5 us
    all_to_all x4, waiting for transfers between devices, exchange(): return lax.all_to_all(states.reshape(piece), 'seq', 0, 0, tiled=True)  13.6 us
    ppermute x6, starting transfers between devices, send_all(): same.append(lax.ppermute(bundles[dx], 'head', pairs))  9.53 us
    all_to_all x1, blocking collectives, on_device(): sums = lax.all_to_all(sums, 'head', 0, 0, tiled=True)  7.82 us
    pallas_call x1, Pallas kernels, on_device(): pl.pallas_call(back_kernel, out_shape=[pltpu.HBM((t, own), BF16)] * 2 + [...  7.71 us
    pallas_call x1, Pallas kernels, on_device(): pl.pallas_call(intra_kernel, out_shape=[pltpu.HBM((t, own), F32), pltpu.H...  5.97 us
    ppermute x8, waiting for transfers between devices, send_all(): lax.ppermute(b, 'head', [(i, i ^ 1) for i in range(n)])  3.66 us
    pallas_call x1, Pallas kernels, on_device(): pl.pallas_call(last_kernel, out_shape=[sds((t, own), BF16), sds((t, own),...  3.6 us
  transfers between devices with their start and end apart: 18, of which 11 were waited for; matrix products, arithmetic and copies ran while one was open for 0% of the time, Pallas kernels for 18%

profile of v3, /device:TPU:32, one launch (start us, length us, event | category | flops | bytes accessed | tf_op | source)
XLA Modules:
  0.0 104.6 jit_solution(14809491236492568379)
XLA Ops:
  0.6 0.0 copy-start.1
  0.6 0.0 copy-start
  0.7 3.2 %states.1._ = bf16[8,128,128]{2,1,0:T(8,128)(2,1)} custom-call(bf16[512,1024]{1,0:T(8,128)(2,1)} %k_hbm.5, bf16[512,1024]{1,0:T(8,128)(2,1)} %v_hbm.5), custom_call_target="tpu_custom_call" | custom-call | flops 268435456 | bytes 2097152 | tf_op jit(solution)/shard_map/states/pallas_call | solution.py:412
  3.8 11.4 %all-to-all-start = ((bf16[32,32,128]{2,1,0:T(8,128)(2,1)}), bf16[32,32,128]{2,1,0:T(8,128)(2,1)S(1)}, u32[]{:S(2)}, u32[]{:S(2)}) async-start(bf16[32,32,128]{2,1,0:T(8,128)(2,1)} %bitcast), calls=%async_computation | async-start | bytes 524288 | tf_op jit(solution)/shard_map/all_to_all | solution.py:398
  15.2 0.0 copy-done.1
  15.2 0.0 copy-done
  15.2 0.0 copy-start.4
  15.2 0.7 copy-done.4
  16.0 0.5 weigh.1
  16.5 0.0 copy-start.3
  16.5 1.6 %collective-permute-start = (bf16[2,64,1024]{2,1,0:T(8,128)(2,1)S(1)}, bf16[2,64,1024]{2,1,0:T(8,128)(2,1)}, u32[]{:S(2)}, u32[]{:S(2)}) collective-permute-start(bf16[2,64,1024]{2,1,0:T(8,128)(2,1)S(1)} %get-tuple-element.27), channel_id=1, source_target_pairs={{0,2},{1,3},{2,4},{3,5},{4,6},{5,7},{6,0},{7,1},{8,10},{9,11},{10,... | collective-permute-start | bytes 786440 | tf_op jit(solution)/shard_map/ppermute | solution.py:56
  18.1 2.7 %collective-permute-start.1 = (bf16[2,64,1024]{2,1,0:T(8,128)(2,1)S(1)}, bf16[2,64,1024]{2,1,0:T(8,128)(2,1)}, u32[]{:S(2)}, u32[]{:S(2)}) collective-permute-start(bf16[2,64,1024]{2,1,0:T(8,128)(2,1)S(1)} %get-tuple-element.28), channel_id=1, source_target_pairs={{0,4},{1,5},{2,6},{3,7},{4,0},{5,1},{6,2},{7,3},{8,12},{9,13},{10,... | collective-permute-start | bytes 786440 | tf_op jit(solution)/shard_map/ppermute | solution.py:56
  20.8 1.4 %collective-permute-start.2 = (bf16[2,64,1024]{2,1,0:T(8,128)(2,1)S(1)}, bf16[2,64,1024]{2,1,0:T(8,128)(2,1)}, u32[]{:S(2)}, u32[]{:S(2)}) collective-permute-start(bf16[2,64,1024]{2,1,0:T(8,128)(2,1)S(1)} %get-tuple-element.29), channel_id=1, source_target_pairs={{0,6},{1,7},{2,0},{3,1},{4,2},{5,3},{6,4},{7,5},{8,14},{9,15},{10,... | collective-permute-start | bytes 786440 | tf_op jit(solution)/shard_map/ppermute | solution.py:56
  22.3 6.0 %intra.1 = (f32[512,1024]{1,0:T(8,128)}, bf16[8,3,256,256]{3,2,1,0:T(8,128)(2,1)}) custom-call(bf16[512,1024]{1,0:T(8,128)(2,1)} %q_hbm.3, bf16[512,1024]{1,0:T(8,128)(2,1)} %k_hbm.5, bf16[512,1024]{1,0:T(8,128)(2,1)} %v_hbm.5, bf16[8,128,128]{2,1,0:T(8,128)(2,1)} %states.1._), custom_call_target="tpu_custom_call" | custom-call | flops 1073741824 | bytes 8388608 | tf_op jit(solution)/shard_map/intra/pallas_call | solution.py:435
  28.2 0.0 all-to-all-done.x_ref
  28.3 0.7 running.2
  29.0 9.8 %all-to-all-start.1 = ((bf16[32,32,128]{2,1,0:T(8,128)(2,1)}), bf16[32,32,128]{2,1,0:T(8,128)(2,1)S(1)}, u32[]{:S(2)}, u32[]{:S(2)}) async-start(bf16[32,32,128]{2,1,0:T(8,128)(2,1)} %running.2), calls=%async_computation.1 | async-start | bytes 524288 | tf_op jit(solution)/shard_map/all_to_all | solution.py:398
  38.8 0.0 copy-done.3
  38.8 0.1 collective-permute-start.3
  38.9 0.0 collective-permute-done.refs_4_
  38.9 0.5 collective-permute-start.4
  39.4 0.0 collective-permute-done.1.refs_5_
  39.4 0.1 collective-permute-start.5
  39.5 0.0 collective-permute-done.2.refs_6_
  39.5 0.4 collective-permute-start.6
  39.9 0.5 collective-permute-done.3.refs_7_
  40.4 0.0 copy-start.6
  40.4 0.6 collective-permute-done.4.refs_8_
  41.0 0.0 copy-start.7
  41.0 0.4 collective-permute-done.5.refs_9_
  41.4 0.0 copy-done.6
  41.4 0.0 copy-start.8
  41.4 0.4 collective-permute-done.6.refs_10_
  41.8 8.2 %all-to-all-done.1 = bf16[32,32,128]{2,1,0:T(8,128)(2,1)S(1)} async-done(((bf16[32,32,128]{2,1,0:T(8,128)(2,1)}), bf16[32,32,128]{2,1,0:T(8,128)(2,1)S(1)}, u32[]{:S(2)}, u32[]{:S(2)}) %all-to-all-start.1) | async-done | bytes 262176 | tf_op jit(solution)/shard_map/all_to_all | solution.py:398
  49.9 0.0 copy-done.7
  49.9 0.0 copy-done.8
  49.9 0.0 copy-done.9
  49.9 3.3 %outs.1 = (f32[8,8,128]{2,1,0:T(8,128)S(1)}, bf16[512,1024]{1,0:T(8,128)(2,1)S(1)}, bf16[512,1024]{1,0:T(8,128)(2,1)S(1)}, bf16[512,1024]{1,0:T(8,128)(2,1)S(1)}...) custom-call(f32[512,1024]{1,0:T(8,128)} %get-tuple-element.25.refs_0, ...), custom_call_target="tpu_custom_call" | custom-call | flops 134217728 | bytes 5242880 | tf_op jit(solution)/shard_map/outs/pallas_call | solution.py:451
  53.2 7.8 %all_to_all.25.sums_ref = f32[8,8,128]{2,1,0:T(8,128)S(1)} all-to-all(f32[8,8,128]{2,1,0:T(8,128)S(1)} %get-tuple-element.30), channel_id=1, replica_groups=mesh['seq'=32,'head'=8] {'head'}, dimensions={0} | all-to-all | bytes 65536 | tf_op jit(solution)/shard_map/all_to_all | solution.py:461
  61.0 2.3 %grads.1 = (bf16[8,128,128]{2,1,0:T(8,128)(2,1)}, bf16[512,1024]{1,0:T(8,128)(2,1)}) custom-call(f32[8,8,128]{2,1,0:T(8,128)S(1)} %all_to_all.25.sums_ref, bf16[512,1024]{1,0:T(8,128)(2,1)S(1)} %get-tuple-element.31.q_ref, bf16[512,1024]{1,0:T(8,128)(2,1)S(1)} %get-tuple-element.32.w_ref, bf16[512,1024]{1,0:T(8,128)(2,1)S(1)} %get-tuple-element.33.o_ref), custom_call_target="tpu_custom_call" | custom-call | flops 134217728 | bytes 4194304 | tf_op jit(solution)/shard_map/grads/pallas_call | solution.py:463
  63.3 4.3 %all-to-all-start.3 = ((bf16[32,32,128]{2,1,0:T(8,128)(2,1)}), bf16[32,32,128]{2,1,0:T(8,128)(2,1)S(1)}, u32[]{:S(2)}, u32[]{:S(2)}) async-start(bf16[32,32,128]{2,1,0:T(8,128)(2,1)} %bitcast.3), calls=%async_computation.3 | async-start | bytes 524288 | tf_op jit(solution)/shard_map/all_to_all | solution.py:398
  67.7 0.6 collective-permute-start.7
  68.3 2.1 %collective-permute-start.8 = (bf16[2,64,1024]{2,1,0:T(8,128)(2,1)}, bf16[2,64,1024]{2,1,0:T(8,128)(2,1)S(1)}, u32[]{:S(2)}, u32[]{:S(2)}) collective-permute-start(bf16[2,64,1024]{2,1,0:T(8,128)(2,1)} %get-tuple-element.44), channel_id=1, source_target_pairs={{0,4},{1,5},{2,6},{3,7},{4,0},{5,1},{6,2},{7,3},{8,12},{9,13},{10,... | collective-permute-start | bytes 786440 | tf_op jit(solution)/shard_map/ppermute | solution.py:56
  70.4 1.1 %collective-permute-start.9 = (bf16[2,64,1024]{2,1,0:T(8,128)(2,1)}, bf16[2,64,1024]{2,1,0:T(8,128)(2,1)}, u32[]{:S(2)}, u32[]{:S(2)}) collective-permute-start(bf16[2,64,1024]{2,1,0:T(8,128)(2,1)} %get-tuple-element.45), channel_id=1, source_target_pairs={{0,6},{1,7},{2,0},{3,1},{4,2},{5,3},{6,4},{7,5},{8,14},{9,15},{10,... | collective-permute-start | bytes 786440 | tf_op jit(solution)/shard_map/ppermute | solution.py:56
  71.5 7.7 %backs.1 = (bf16[512,1024]{1,0:T(8,128)(2,1)}, bf16[512,1024]{1,0:T(8,128)(2,1)}, bf16[512,1024]{1,0:T(8,128)(2,1)}) custom-call(bf16[512,1024]{1,0:T(8,128)(2,1)} %q_hbm.3, bf16[512,1024]{1,0:T(8,128)(2,1)} %k_hbm.5, bf16[512,1024]{1,0:T(8,128)(2,1)} %v_hbm.5, bf16[512,1024]{1,0:T(8,128)(2,1)} %get-tuple-element.34.do_hbm, ...), custom_call_target="tpu_custom_call" | custom-call | flops 1610612736 | bytes 10485760 | tf_op jit(solution)/shard_map/backs/pallas_call | solution.py:475
  79.2 0.8 all-to-all-done.3.x_ref
  79.9 0.7 running.3
  80.7 9.0 %all-to-all-start.4 = ((bf16[32,32,128]{2,1,0:T(8,128)(2,1)}), bf16[32,32,128]{2,1,0:T(8,128)(2,1)S(1)}, u32[]{:S(2)}, u32[]{:S(2)}) async-start(bf16[32,32,128]{2,1,0:T(8,128)(2,1)} %running.3), calls=%async_computation.4 | async-start | bytes 524288 | tf_op jit(solution)/shard_map/all_to_all | solution.py:398
  89.7 0.0 copy-done.2
  89.7 0.1 collective-permute-start.10
  89.8 0.0 collective-permute-done.7.refs_1_
  89.9 0.5 collective-permute-start.11
  90.3 0.0 collective-permute-done.8.refs_2_
  90.3 0.1 collective-permute-start.12
  90.5 0.0 collective-permute-done.9.refs_3_
  90.5 0.4 collective-permute-start.13
  90.9 0.5 collective-permute-done.10.refs_4_
  91.4 0.4 collective-permute-done.11.refs_5_
  91.7 0.4 collective-permute-done.12.refs_6_
  92.1 0.6 collective-permute-done.13.refs_7_
  92.7 0.0 copy-done.5
  92.7 3.5 %gates.1 = bf16[64,8192]{1,0:T(8,128)(2,1)} custom-call(bf16[2,64,1024]{2,1,0:T(8,128)(2,1)S(1)} %copy-done.2, bf16[2,64,1024]{2,1,0:T(8,128)(2,1)S(1)} %collective-permute-done.7.refs_1_, bf16[2,64,1024]{2,1,0:T(8,128)(2,1)S(1)} %collective-permute-done.8.refs_2_, bf16[2,64,1024]{2,1,0:T(8,128)(2,1)} %collective-permute-done.9.refs_3_, ...), custom_call_target="tpu_custom_call" | custom-call | flops 10485760 | bytes 4194304 | tf_op jit(solution)/shard_map/gates/pallas_call | solution.py:490
  96.2 4.6 %all-to-all-done.4 = bf16[32,32,128]{2,1,0:T(8,128)(2,1)S(1)} async-done(((bf16[32,32,128]{2,1,0:T(8,128)(2,1)}), bf16[32,32,128]{2,1,0:T(8,128)(2,1)S(1)}, u32[]{:S(2)}, u32[]{:S(2)}) %all-to-all-start.4) | async-done | bytes 262176 | tf_op jit(solution)/shard_map/all_to_all | solution.py:398
  100.9 3.6 %last.1 = (bf16[512,1024]{1,0:T(8,128)(2,1)}, bf16[512,1024]{1,0:T(8,128)(2,1)}) custom-call(bf16[512,1024]{1,0:T(8,128)(2,1)} %get-tuple-element.37.refs_0_.ak_hbm, bf16[512,1024]{1,0:T(8,128)(2,1)} %get-tuple-element.38.av_hbm, bf16[512,1024]{1,0:T(8,128)(2,1)} %k_hbm.5, bf16[512,1024]{1,0:T(8,128)(2,1)} %v_hbm.5, bf16[8,128,128]{2,1,0:T(8,128)(2,1)S(1)} %bitcast.7), custom_call_target="tpu_custom_call" | custom-call | flops 268435456 | bytes 8388608 | tf_op jit(solution)/shard_map/last/pallas_call | solution.py:498
  (3 shorter events, 0.0 us)
Async XLA Ops:
  0.6 14.6 %copy-start.1 = (bf16[64,8192]{1,0:T(8,128)(2,1)S(1)}, bf16[64,8192]{1,0:T(8,128)(2,1)}, u32[]{:S(2)}) copy-start(bf16[64,8192]{1,0:T(8,128)(2,1)} %refs_9_.1) | copy-start | bytes 3145732
  0.6 14.6 %copy-start = (bf16[64,8192]{1,0:T(8,128)(2,1)S(1)}, bf16[64,8192]{1,0:T(8,128)(2,1)}, u32[]{:S(2)}) copy-start(bf16[64,8192]{1,0:T(8,128)(2,1)} %refs_8_.1) | copy-start | bytes 3145732
  3.8 24.4 %all-to-all-start = ((bf16[32,32,128]{2,1,0:T(8,128)(2,1)}), bf16[32,32,128]{2,1,0:T(8,128)(2,1)S(1)}, u32[]{:S(2)}, u32[]{:S(2)}) async-start(bf16[32,32,128]{2,1,0:T(8,128)(2,1)} %bitcast), calls=%async_computation | async-start | bytes 524288 | tf_op jit(solution)/shard_map/all_to_all | solution.py:398
  15.2 0.8 copy-start.4
  16.5 22.3 %copy-start.3 = (bf16[2,64,1024]{2,1,0:T(8,128)(2,1)}, bf16[2,64,1024]{2,1,0:T(8,128)(2,1)S(1)}, u32[]{:S(2)}) copy-start(bf16[2,64,1024]{2,1,0:T(8,128)(2,1)S(1)} %get-tuple-element.26.refs_3_) | copy-start | bytes 786436
  16.5 22.4 %collective-permute-start = (bf16[2,64,1024]{2,1,0:T(8,128)(2,1)S(1)}, bf16[2,64,1024]{2,1,0:T(8,128)(2,1)}, u32[]{:S(2)}, u32[]{:S(2)}) collective-permute-start(bf16[2,64,1024]{2,1,0:T(8,128)(2,1)S(1)} %get-tuple-element.27), channel_id=1, source_target_pairs={{0,2},{1,3},{2,4},{3,5},{4,6},{5,7},{6,0},{7,1},{8,10},{9,11},{10,... | collective-permute-start | bytes 786440 | tf_op jit(solution)/shard_map/ppermute | solution.py:56
  18.1 21.3 %collective-permute-start.1 = (bf16[2,64,1024]{2,1,0:T(8,128)(2,1)S(1)}, bf16[2,64,1024]{2,1,0:T(8,128)(2,1)}, u32[]{:S(2)}, u32[]{:S(2)}) collective-permute-start(bf16[2,64,1024]{2,1,0:T(8,128)(2,1)S(1)} %get-tuple-element.28), channel_id=1, source_target_pairs={{0,4},{1,5},{2,6},{3,7},{4,0},{5,1},{6,2},{7,3},{8,12},{9,13},{10,... | collective-permute-start | bytes 786440 | tf_op jit(solution)/shard_map/ppermute | solution.py:56
  20.8 18.7 %collective-permute-start.2 = (bf16[2,64,1024]{2,1,0:T(8,128)(2,1)S(1)}, bf16[2,64,1024]{2,1,0:T(8,128)(2,1)}, u32[]{:S(2)}, u32[]{:S(2)}) collective-permute-start(bf16[2,64,1024]{2,1,0:T(8,128)(2,1)S(1)} %get-tuple-element.29), channel_id=1, source_target_pairs={{0,6},{1,7},{2,0},{3,1},{4,2},{5,3},{6,4},{7,5},{8,14},{9,15},{10,... | collective-permute-start | bytes 786440 | tf_op jit(solution)/shard_map/ppermute | solution.py:56
  29.0 20.9 %all-to-all-start.1 = ((bf16[32,32,128]{2,1,0:T(8,128)(2,1)}), bf16[32,32,128]{2,1,0:T(8,128)(2,1)S(1)}, u32[]{:S(2)}, u32[]{:S(2)}) async-start(bf16[32,32,128]{2,1,0:T(8,128)(2,1)} %running.2), calls=%async_computation.1 | async-start | bytes 524288 | tf_op jit(solution)/shard_map/all_to_all | solution.py:398
  38.8 1.6 %collective-permute-start.3 = (bf16[2,64,1024]{2,1,0:T(8,128)(2,1)S(1)}, bf16[2,64,1024]{2,1,0:T(8,128)(2,1)S(1)}, u32[]{:S(2)}, u32[]{:S(2)}) collective-permute-start(bf16[2,64,1024]{2,1,0:T(8,128)(2,1)S(1)} %get-tuple-element.26.refs_3_), channel_id=1, source_target_pairs={{0,1},{1,0},{2,3},{3,2},{4,5},{5,4},{6,7},{7,6},{8,9},{9,8},{10,11... | collective-permute-start | bytes 786440 | tf_op jit(solution)/shard_map/ppermute | solution.py:57
  38.9 2.1 %collective-permute-start.4 = (bf16[2,64,1024]{2,1,0:T(8,128)(2,1)}, bf16[2,64,1024]{2,1,0:T(8,128)(2,1)S(1)}, u32[]{:S(2)}, u32[]{:S(2)}) collective-permute-start(bf16[2,64,1024]{2,1,0:T(8,128)(2,1)} %collective-permute-done.refs_4_), channel_id=1, source_target_pairs={{0,1},{1,0},{2,3},{3,2},{4,5},{5,4},{6,7},{7,6},{8,9},{9,8},{10,11... | collective-permute-start | bytes 786440 | tf_op jit(solution)/shard_map/ppermute | solution.py:57
  39.4 2.0 %collective-permute-start.5 = (bf16[2,64,1024]{2,1,0:T(8,128)(2,1)}, bf16[2,64,1024]{2,1,0:T(8,128)(2,1)S(1)}, u32[]{:S(2)}, u32[]{:S(2)}) collective-permute-start(bf16[2,64,1024]{2,1,0:T(8,128)(2,1)} %collective-permute-done.1.refs_5_), channel_id=1, source_target_pairs={{0,1},{1,0},{2,3},{3,2},{4,5},{5,4},{6,7},{7,6},{8,9},{9,8},{10,11... | collective-permute-start | bytes 786440 | tf_op jit(solution)/shard_map/ppermute | solution.py:57
  39.5 2.2 %collective-permute-start.6 = (bf16[2,64,1024]{2,1,0:T(8,128)(2,1)}, bf16[2,64,1024]{2,1,0:T(8,128)(2,1)S(1)}, u32[]{:S(2)}, u32[]{:S(2)}) collective-permute-start(bf16[2,64,1024]{2,1,0:T(8,128)(2,1)} %collective-permute-done.2.refs_6_), channel_id=1, source_target_pairs={{0,1},{1,0},{2,3},{3,2},{4,5},{5,4},{6,7},{7,6},{8,9},{9,8},{10,11... | collective-permute-start | bytes 786440 | tf_op jit(solution)/shard_map/ppermute | solution.py:57
  40.4 1.0 copy-start.6
  41.0 8.9 %copy-start.7 = (bf16[2,64,1024]{2,1,0:T(8,128)(2,1)}, bf16[2,64,1024]{2,1,0:T(8,128)(2,1)S(1)}, u32[]{:S(2)}) copy-start(bf16[2,64,1024]{2,1,0:T(8,128)(2,1)S(1)} %collective-permute-done.4.refs_8_) | copy-start | bytes 786436
  41.4 8.5 %copy-start.8 = (bf16[2,64,1024]{2,1,0:T(8,128)(2,1)}, bf16[2,64,1024]{2,1,0:T(8,128)(2,1)S(1)}, u32[]{:S(2)}) copy-start(bf16[2,64,1024]{2,1,0:T(8,128)(2,1)S(1)} %collective-permute-done.5.refs_9_) | copy-start | bytes 786436
  41.8 8.2 %copy-start.9 = (bf16[2,64,1024]{2,1,0:T(8,128)(2,1)}, bf16[2,64,1024]{2,1,0:T(8,128)(2,1)S(1)}, u32[]{:S(2)}) copy-start(bf16[2,64,1024]{2,1,0:T(8,128)(2,1)S(1)} %collective-permute-done.6.refs_10_) | copy-start | bytes 786436
  63.3 16.6 %all-to-all-start.3 = ((bf16[32,32,128]{2,1,0:T(8,128)(2,1)}), bf16[32,32,128]{2,1,0:T(8,128)(2,1)S(1)}, u32[]{:S(2)}, u32[]{:S(2)}) async-start(bf16[32,32,128]{2,1,0:T(8,128)(2,1)} %bitcast.3), calls=%async_computation.3 | async-start | bytes 524288 | tf_op jit(solution)/shard_map/all_to_all | solution.py:398
  67.7 22.2 %collective-permute-start.7 = (bf16[2,64,1024]{2,1,0:T(8,128)(2,1)}, bf16[2,64,1024]{2,1,0:T(8,128)(2,1)S(1)}, u32[]{:S(2)}, u32[]{:S(2)}) collective-permute-start(bf16[2,64,1024]{2,1,0:T(8,128)(2,1)} %get-tuple-element.43), channel_id=1, source_target_pairs={{0,2},{1,3},{2,4},{3,5},{4,6},{5,7},{6,0},{7,1},{8,10},{9,11},{10,... | collective-permute-start | bytes 786440 | tf_op jit(solution)/shard_map/ppermute | solution.py:56
  68.3 22.0 %collective-permute-start.8 = (bf16[2,64,1024]{2,1,0:T(8,128)(2,1)}, bf16[2,64,1024]{2,1,0:T(8,128)(2,1)S(1)}, u32[]{:S(2)}, u32[]{:S(2)}) collective-permute-start(bf16[2,64,1024]{2,1,0:T(8,128)(2,1)} %get-tuple-element.44), channel_id=1, source_target_pairs={{0,4},{1,5},{2,6},{3,7},{4,0},{5,1},{6,2},{7,3},{8,12},{9,13},{10,... | collective-permute-start | bytes 786440 | tf_op jit(solution)/shard_map/ppermute | solution.py:56
  70.4 20.1 %collective-permute-start.9 = (bf16[2,64,1024]{2,1,0:T(8,128)(2,1)}, bf16[2,64,1024]{2,1,0:T(8,128)(2,1)}, u32[]{:S(2)}, u32[]{:S(2)}) collective-permute-start(bf16[2,64,1024]{2,1,0:T(8,128)(2,1)} %get-tuple-element.45), channel_id=1, source_target_pairs={{0,6},{1,7},{2,0},{3,1},{4,2},{5,3},{6,4},{7,5},{8,14},{9,15},{10,... | collective-permute-start | bytes 786440 | tf_op jit(solution)/shard_map/ppermute | solution.py:56
  71.5 18.3 %copy-start.2 = (bf16[2,64,1024]{2,1,0:T(8,128)(2,1)S(1)}, bf16[2,64,1024]{2,1,0:T(8,128)(2,1)}, u32[]{:S(2)}) copy-start(bf16[2,64,1024]{2,1,0:T(8,128)(2,1)} %get-tuple-element.42.refs_0_) | copy-start | bytes 786436
  71.5 21.2 %copy-start.5 = (f32[8192]{0:T(1024)S(1)}, f32[8192]{0:T(1024)}, u32[]{:S(2)}) copy-start(f32[8192]{0:T(1024)} %param.10) | copy-start | bytes 98308
  80.7 20.2 %all-to-all-start.4 = ((bf16[32,32,128]{2,1,0:T(8,128)(2,1)}), bf16[32,32,128]{2,1,0:T(8,128)(2,1)S(1)}, u32[]{:S(2)}, u32[]{:S(2)}) async-start(bf16[32,32,128]{2,1,0:T(8,128)(2,1)} %running.3), calls=%async_computation.4 | async-start | bytes 524288 | tf_op jit(solution)/shard_map/all_to_all | solution.py:398
  89.7 1.6 %collective-permute-start.10 = (bf16[2,64,1024]{2,1,0:T(8,128)(2,1)S(1)}, bf16[2,64,1024]{2,1,0:T(8,128)(2,1)S(1)}, u32[]{:S(2)}, u32[]{:S(2)}) collective-permute-start(bf16[2,64,1024]{2,1,0:T(8,128)(2,1)S(1)} %copy-done.2), channel_id=1, source_target_pairs={{0,1},{1,0},{2,3},{3,2},{4,5},{5,4},{6,7},{7,6},{8,9},{9,8},{10,11... | collective-permute-start | bytes 786440 | tf_op jit(solution)/shard_map/ppermute | solution.py:57
  89.9 1.9 %collective-permute-start.11 = (bf16[2,64,1024]{2,1,0:T(8,128)(2,1)S(1)}, bf16[2,64,1024]{2,1,0:T(8,128)(2,1)S(1)}, u32[]{:S(2)}, u32[]{:S(2)}) collective-permute-start(bf16[2,64,1024]{2,1,0:T(8,128)(2,1)S(1)} %collective-permute-done.7.refs_1_), channel_id=1, source_target_pairs={{0,1},{1,0},{2,3},{3,2},{4,5},{5,4},{6,7},{7,6},{8,9},{9,8},{10,11... | collective-permute-start | bytes 786440 | tf_op jit(solution)/shard_map/ppermute | solution.py:57
  90.3 1.8 %collective-permute-start.12 = (bf16[2,64,1024]{2,1,0:T(8,128)(2,1)S(1)}, bf16[2,64,1024]{2,1,0:T(8,128)(2,1)S(1)}, u32[]{:S(2)}, u32[]{:S(2)}) collective-permute-start(bf16[2,64,1024]{2,1,0:T(8,128)(2,1)S(1)} %collective-permute-done.8.refs_2_), channel_id=1, source_target_pairs={{0,1},{1,0},{2,3},{3,2},{4,5},{5,4},{6,7},{7,6},{8,9},{9,8},{10,11... | collective-permute-start | bytes 786440 | tf_op jit(solution)/shard_map/ppermute | solution.py:57
  90.5 2.2 %collective-permute-start.13 = (bf16[2,64,1024]{2,1,0:T(8,128)(2,1)}, bf16[2,64,1024]{2,1,0:T(8,128)(2,1)S(1)}, u32[]{:S(2)}, u32[]{:S(2)}) collective-permute-start(bf16[2,64,1024]{2,1,0:T(8,128)(2,1)} %collective-permute-done.9.refs_3_), channel_id=1, source_target_pairs={{0,1},{1,0},{2,3},{3,2},{4,5},{5,4},{6,7},{7,6},{8,9},{9,8},{10,11... | collective-permute-start | bytes 786440 | tf_op jit(solution)/shard_map/ppermute | solution.py:57

commit v4 on v3

--- a/solution.py
+++ b/solution.py
@@ -142,11 +142,14 @@
     return lax.broadcasted_iota(jnp.int32, (n, n), 0) <= lax.broadcasted_iota(jnp.int32, (n, n), 1)
 
 
-def intra_kernel(q_hbm, k_hbm, v_hbm, _, i_hbm, s_hbm, *refs):
-    q_ref, k_ref, v_ref, i_ref, s_ref, sems, out_sems = refs
+def intra_kernel(first, q_hbm, k_hbm, v_hbm, *refs):
+    i_hbm, s_hbm, q_ref, k_ref, v_ref, i_ref, s_ref, sems, out_sems = refs[-9:]
     t, own = q_ref.shape
     half = t // 2
     n = own // (2 * HEAD_DIM)
+    q_hbm, k_hbm, v_hbm = [
+        x.at[:, pl.ds(first * HEAD_DIM, own)] for x in (q_hbm, k_hbm, v_hbm)
+    ]
     ins = [
         by_pairs(src, dst, sems, n * j)
         for j, (src, dst) in enumerate(((q_hbm, q_ref), (k_hbm, k_ref), (v_hbm, v_ref)))
@@ -164,14 +167,18 @@
     for i in range(n):
         for c in ins:
             c[i].wait()
+        pair = []
         for h in range(2 * i, 2 * i + 2):
             cols = slice(h * HEAD_DIM, (h + 1) * HEAD_DIM)
-            q, k, v = q_ref[:, cols], k_ref[:, cols], v_ref[:, cols]
+            q, k = q_ref[:, cols], k_ref[:, cols]
             s0 = jnp.where(keep, mm_bt(q[one], k[one]), 0.0).astype(BF16)
-            i_ref[one, cols] = mm(s0, v[one])
             s2 = mm_bt(q[two], k[one]).astype(BF16)
             s1 = jnp.where(keep, mm_bt(q[two], k[two]), 0.0).astype(BF16)
-            i_ref[two, cols] = mm(s2, v[one]) + mm(s1, v[two])
+            pair.append((h, cols, s0, s1, s2))
+        for h, cols, s0, s1, s2 in pair:
+            v = v_ref[:, cols]
+            i_ref[one, cols] = mm(s0, v[one])
+            i_ref[two, cols] = mm(jnp.concatenate([s2, s1], axis=1), v)
             s_ref[h, 0], s_ref[h, 1], s_ref[h, 2] = s0, s1, s2
         outs[i].start()
         more[i].start()
@@ -179,7 +186,8 @@
 
 
 def out_kernel(n_head, *refs):
-    i_hbm, q_hbm, p_ref = refs[:3]
+    i0_hbm, i1_hbm, q_hbm, p_ref = refs[:4]
+    refs = refs[1:]
     w_any = refs[3 : 3 + n_head]
     sums_ref, o_ref, w_ref, q_ref = refs[3 + n_head : 7 + n_head]
     *bundles, i_ref, sems, out_sems = refs[7 + n_head :]
@@ -191,20 +199,24 @@
         pltpu.make_async_copy(q_hbm.at[pl.ds(r * d, d), :], q_ref.at[pl.ds(r * d, d), :], sems.at[r])
         for r in range(blocks)
     ]
+    some = i0_hbm.shape[1]
     ci = [
         pltpu.make_async_copy(
-            i_hbm.at[pl.ds(r * d, d), :], i_ref.at[pl.ds(r * d, d), :], sems.at[blocks + r]
+            src.at[pl.ds(r * d, d), :],
+            i_ref.at[pl.ds(r * d, d), pl.ds(j * some, some)],
+            sems.at[(1 + j) * blocks + r],
         )
         for r in range(blocks)
+        for j, src in enumerate((i0_hbm, i1_hbm))
     ]
     for r in range(blocks):
         cq[r].start()
-        ci[r].start()
-    cw = start_all(assemble(n_head, w_any, w_ref, sems, 2 * blocks))
+        start_all(ci[2 * r : 2 * r + 2])
+    cw = start_all(assemble(n_head, w_any, w_ref, sems, 3 * blocks))
     for r in range(blocks):
         at = slice(r * d, (r + 1) * d)
         cq[r].wait()
-        ci[r].wait()
+        wait_all(ci[2 * r : 2 * r + 2])
         for h in range(own // d):
             cols = slice(h * d, (h + 1) * d)
             o_ref[at, cols] = (i_ref[at, cols] + mm(q_ref[at, cols], p_ref[h])).astype(BF16)
@@ -267,9 +279,10 @@
 
 
 def back_kernel(
-    q_hbm, k_hbm, v_hbm, do_hbm, t_hbm, p_ref, ak_hbm, av_hbm, gq_hbm,
-    q_ref, k_ref, v_ref, do_ref, t_ref, ak_ref, av_ref, gq_ref, sems, out_sems,
+    q_hbm, k_hbm, v_hbm, do_hbm, t0_hbm, t1_hbm, p_ref, *refs
 ):
+    ak_hbm, av_hbm, gq_hbm, q_ref, k_ref, v_ref, do_ref, t_ref = refs[-13:-5]
+    ak_ref, av_ref, gq_ref, sems, out_sems = refs[-5:]
     t, own = q_ref.shape
     half = t // 2
     n = own // (2 * HEAD_DIM)
@@ -282,9 +295,10 @@
     ins.append(
         [
             pltpu.make_async_copy(
-                t_hbm.at[pl.ds(2 * i, 2)], t_ref.at[pl.ds(2 * i, 2)], sems.at[4 * n + i]
+                src.at[pl.ds(2 * i, 2)], t_ref.at[pl.ds(j * n + 2 * i, 2)], sems.at[4 * n + j * n // 2 + i]
             )
-            for i in range(n)
+            for j, src in enumerate((t0_hbm, t1_hbm))
+            for i in range(n // 2)
         ]
     )
     for i in range(n):
@@ -299,21 +313,29 @@
     for i in range(n):
         for c in ins:
             c[i].wait()
+        pair = []
         for h in range(2 * i, 2 * i + 2):
             cols = slice(h * HEAD_DIM, (h + 1) * HEAD_DIM)
-            q, k, v, do = q_ref[:, cols], k_ref[:, cols], v_ref[:, cols], do_ref[:, cols]
-            qt, dot = q.T, do.T
-            base = mm_bt(do, p_ref[h])
+            v, do = v_ref[:, cols], do_ref[:, cols]
             g0 = jnp.where(low, mm_bt(do[one], v[one]), 0.0).astype(BF16)
-            gq_ref[one, cols] = (mm(g0, k[one]) + base[one]).astype(BF16)
             g2 = mm_bt(do[two], v[one]).astype(BF16)
             g1 = jnp.where(low, mm_bt(do[two], v[two]), 0.0).astype(BF16)
-            gq_ref[two, cols] = (mm(g2, k[one]) + mm(g1, k[two]) + base[two]).astype(BF16)
-            ak_ref[one, cols] = (mm(qt[:, one], g0) + mm(qt[:, two], g2)).astype(BF16).T
+            pair.append((h, cols, g0, g1, g2))
+        for h, cols, _, _, _ in pair:
+            dot = do_ref[:, cols].T
+            s0, s1, s2 = t_ref[h, 0], t_ref[h, 1], t_ref[h, 2]
+            av = mm(dot, jnp.concatenate([s0, s2], axis=0))
+            av_ref[one, cols] = av.astype(BF16).T
+            av_ref[two, cols] = mm(dot[:, two], s1).astype(BF16).T
+        for h, cols, g0, g1, g2 in pair:
+            qt, kt, dot = q_ref[:, cols].T, k_ref[:, cols].T, do_ref[:, cols].T
+            base = mm(p_ref[h], dot)
+            gq_ref[one, cols] = (mm_bt(kt[:, one], g0) + base[:, one]).astype(BF16).T
+            gq = mm_bt(kt, jnp.concatenate([g2, g1], axis=1)) + base[:, two]
+            gq_ref[two, cols] = gq.astype(BF16).T
+            ak = mm(qt, jnp.concatenate([g0, g2], axis=0))
+            ak_ref[one, cols] = ak.astype(BF16).T
             ak_ref[two, cols] = mm(qt[:, two], g1).astype(BF16).T
-            s0, s1, s2 = t_ref[h, 0], t_ref[h, 1], t_ref[h, 2]
-            av_ref[one, cols] = (mm(dot[:, one], s0) + mm(dot[:, two], s2)).astype(BF16).T
-            av_ref[two, cols] = mm(dot[:, two], s1).astype(BF16).T
         for c in outs:
             c[i].start()
     for c in outs:
@@ -429,35 +451,44 @@
         cost_estimate=cost(20 * rows * width, 6 * rows * width),
         name="weigh",
     )(gate, grad_out, gain)
+    own_bundle = weighted[0]
     weighted = [in_hbm(w) for w in send_all(weighted)]
 
     tiles = (heads, 3, t // 2, t // 2)
-    intra, scores = pl.pallas_call(
-        intra_kernel,
-        out_shape=[pltpu.HBM((t, own), F32), pltpu.HBM(tiles, BF16)],
-        in_specs=[anywhere] * 4,
-        out_specs=[anywhere, anywhere],
-        scratch_shapes=[full] * 3
-        + [full32, pltpu.VMEM(tiles, BF16), dma(3 * pairs), dma(2 * pairs)],
-        compiler_params=params(),
-        cost_estimate=cost(2 * large, 16 * t * own),
-        name="intra",
-    )(query, key_in, value, states)
-    intra, scores = in_hbm(intra), in_hbm(scores)
-
-    prefix = exchange(running(received, False, intra)).reshape(heads, d, d)
+    some = heads // 2
+    tiles = (some, 3, t // 2, t // 2)
+
+    def intra(first, *after):
+        part = pltpu.VMEM((t, own // 2), BF16)
+        inner, scores = pl.pallas_call(
+            functools.partial(intra_kernel, first),
+            out_shape=[pltpu.HBM((t, own // 2), F32), pltpu.HBM(tiles, BF16)],
+            in_specs=[anywhere] * (3 + len(after)),
+            out_specs=[anywhere, anywhere],
+            scratch_shapes=[part] * 3
+            + [pltpu.VMEM((t, own // 2), F32), pltpu.VMEM(tiles, BF16), dma(3 * some), dma(2 * some)],
+            compiler_params=params(),
+            cost_estimate=cost(large, 8 * t * own),
+            name="intra",
+        )(query, key_in, value, *after)
+        return in_hbm(inner), in_hbm(scores)
+
+    inner0, scores0 = intra(0, states)
+    summed = running(received, False, own_bundle, inner0)
+    prefix = exchange(summed).reshape(heads, d, d)
+    inner1, scores1 = intra(some, in_hbm(summed), *weighted[1:chips])
 
     tile = (n_head, 2 * t // d, d)
     sums, out, weighted, queries, *bundles = pl.pallas_call(
         functools.partial(out_kernel, n_head),
         out_shape=[sds(tile, F32), full, full, full] + [pltpu.HBM(bundle, BF16)] * chips,
-        in_specs=[anywhere, anywhere, whole] + [anywhere] * n_head,
+        in_specs=[anywhere] * 3 + [whole] + [anywhere] * n_head,
         out_specs=[whole] * 4 + [anywhere] * chips,
-        scratch_shapes=[full32, dma(2 * t // d + n_head), dma(n_head)],
+        scratch_shapes=[full32, dma(3 * t // d + n_head), dma(n_head)],
         compiler_params=params(),
         cost_estimate=cost(small, 10 * t * own),
         name="outs",
-    )(intra, query, prefix, *weighted)
+    )(inner0, inner1, query, prefix, *weighted)
     sums = lax.all_to_all(sums, "head", 0, 0, tiled=True)
 
     states, grad_attn = pl.pallas_call(
@@ -475,14 +506,14 @@
     part_key, part_value, grad_query = pl.pallas_call(
         back_kernel,
         out_shape=[pltpu.HBM((t, own), BF16)] * 2 + [sds((t, own), BF16)],
-        in_specs=[anywhere] * 5 + [whole],
+        in_specs=[anywhere] * 6 + [whole],
         out_specs=[anywhere] * 3,
-        scratch_shapes=[full] * 4 + [pltpu.VMEM(tiles, BF16)] + [full] * 3
+        scratch_shapes=[full] * 4 + [pltpu.VMEM((heads,) + tiles[1:], BF16)] + [full] * 3
         + [dma(5 * pairs), dma(3 * pairs)],
         compiler_params=params(),
         cost_estimate=cost(3 * large, 20 * t * own),
         name="backs",
-    )(query, key_in, value, in_hbm(grad_attn), scores, prefix)
+    )(query, key_in, value, in_hbm(grad_attn), scores0, scores1, prefix)
     part_key, part_value = in_hbm(part_key), in_hbm(part_value)
     suffix = exchange(running(received, True, part_key)).reshape(heads, d, d)
 
@@ -493,7 +524,7 @@
         compiler_params=params(),
         cost_estimate=cost(20 * rows * width, 8 * rows * width),
         name="gates",
-    )(*token_rows, gate, grad_out, gain)
+    )(*token_rows, in_vmem(gate), in_vmem(grad_out), gain)
 
     grad_key, grad_value = pl.pallas_call(
         last_kernel,

time: 105 us -> 101 us (0.962)
  starting transfers between devices: 46.2 us -> 43.2 us
    all_to_all x4, starting transfers between devices: 34.5 us -> 31.3 us  [exchange(): return lax.all_to_all(states.reshape(piece), 'seq', 0, 0, tiled=True)]
    ppermute x8, waiting for transfers between devices: 3.66 us -> 1.85 us  [send_all(): lax.ppermute(b, 'head', [(i, i ^ 1) for i in range(n)])]
    all_to_all x4, waiting for transfers between devices: 13.6 us -> 14.9 us  [exchange(): return lax.all_to_all(states.reshape(piece), 'seq', 0, 0, tiled=True)]
    pallas_call x1, Pallas kernels: 7.71 us -> 6.6 us  [on_device(): pl.pallas_call(back_kernel, out_shape=[pltpu.HBM((t, own), BF16)] * 2 + [...]
    pallas_call x1 -> x2, Pallas kernels: 5.97 us -> 6.6 us  [intra(): pl.pallas_call(functools.partial(intra_kernel, first), out_shape=[pltpu.H...]
  transfers between devices with their start and end apart: 18 -> 18, of which waited for: 11 -> 8; matrix products, arithmetic and copies ran while one was open for 0% -> 0% of each run, Pallas kernels for 18% -> 19%
where the time goes in v4:
time: 101 us
  starting transfers between devices  43.2 us (43%)
  Pallas kernels  31.1 us (31%)
  waiting for transfers between devices  16.7 us (17%)
  blocking collectives  7.82 us (8%)
  between operations  1.05 us (1%)
    all_to_all x4, starting transfers between devices, exchange(): return lax.all_to_all(states.reshape(piece), 'seq', 0, 0, tiled=True)  31.3 us
    all_to_all x4, waiting for transfers between devices, exchange(): return lax.all_to_all(states.reshape(piece), 'seq', 0, 0, tiled=True)  14.9 us
    ppermute x6, starting transfers between devices, send_all(): same.append(lax.ppermute(bundles[dx], 'head', pairs))  9.71 us
    all_to_all x1, blocking collectives, on_device(): sums = lax.all_to_all(sums, 'head', 0, 0, tiled=True)  7.82 us
    pallas_call x2, Pallas kernels, intra(): pl.pallas_call(functools.partial(intra_kernel, first), out_shape=[pltpu.H...  6.6 us
    pallas_call x1, Pallas kernels, on_device(): pl.pallas_call(back_kernel, out_shape=[pltpu.HBM((t, own), BF16)] * 2 + [...  6.6 us
    pallas_call x1, Pallas kernels, on_device(): pl.pallas_call(last_kernel, out_shape=[sds((t, own), BF16), sds((t, own),...  3.6 us
    pallas_call x1, Pallas kernels, on_device(): pl.pallas_call(functools.partial(gate_kernel, n_head), out_shape=sds((row...  3.52 us
  transfers between devices with their start and end apart: 18, of which 8 were waited for; matrix products, arithmetic and copies ran while one was open for 0% of the time, Pallas kernels for 19%

profile of v4, /device:TPU:32, one launch (start us, length us, event | category | flops | bytes accessed | tf_op | source)
XLA Modules:
  0.0 100.6 jit_solution(16396497927058636892)
XLA Ops:
  0.6 0.0 copy-start.1
  0.6 0.0 copy-start
  0.7 0.0 copy-start.4
  0.7 3.2 %states.1.refs_0_ = bf16[8,128,128]{2,1,0:T(8,128)(2,1)} custom-call(bf16[512,1024]{1,0:T(8,128)(2,1)} %k_hbm.7, bf16[512,1024]{1,0:T(8,128)(2,1)} %v_hbm.7), custom_call_target="tpu_custom_call" | custom-call | flops 268435456 | bytes 2097152 | tf_op jit(solution)/shard_map/states/pallas_call | solution.py:434
  3.8 11.4 %all-to-all-start = ((bf16[32,32,128]{2,1,0:T(8,128)(2,1)}), bf16[32,32,128]{2,1,0:T(8,128)(2,1)S(1)}, u32[]{:S(2)}, u32[]{:S(2)}) async-start(bf16[32,32,128]{2,1,0:T(8,128)(2,1)} %bitcast), calls=%async_computation | async-start | bytes 524288 | tf_op jit(solution)/shard_map/all_to_all | solution.py:420
  15.2 0.0 copy-done.1
  15.2 0.0 copy-done
  15.2 0.0 copy-done.4
  15.3 0.5 weigh.1
  15.8 0.0 copy-start.2
  15.8 1.6 %collective-permute-start = (bf16[2,64,1024]{2,1,0:T(8,128)(2,1)S(1)}, bf16[2,64,1024]{2,1,0:T(8,128)(2,1)}, u32[]{:S(2)}, u32[]{:S(2)}) collective-permute-start(bf16[2,64,1024]{2,1,0:T(8,128)(2,1)S(1)} %get-tuple-element.29), channel_id=1, source_target_pairs={{0,2},{1,3},{2,4},{3,5},{4,6},{5,7},{6,0},{7,1},{8,10},{9,11},{10,... | collective-permute-start | bytes 786440 | tf_op jit(solution)/shard_map/ppermute | solution.py:56
  17.4 2.7 %collective-permute-start.1 = (bf16[2,64,1024]{2,1,0:T(8,128)(2,1)S(1)}, bf16[2,64,1024]{2,1,0:T(8,128)(2,1)}, u32[]{:S(2)}, u32[]{:S(2)}) collective-permute-start(bf16[2,64,1024]{2,1,0:T(8,128)(2,1)S(1)} %get-tuple-element.30), channel_id=1, source_target_pairs={{0,4},{1,5},{2,6},{3,7},{4,0},{5,1},{6,2},{7,3},{8,12},{9,13},{10,... | collective-permute-start | bytes 786440 | tf_op jit(solution)/shard_map/ppermute | solution.py:56
  20.1 1.4 %collective-permute-start.2 = (bf16[2,64,1024]{2,1,0:T(8,128)(2,1)S(1)}, bf16[2,64,1024]{2,1,0:T(8,128)(2,1)}, u32[]{:S(2)}, u32[]{:S(2)}) collective-permute-start(bf16[2,64,1024]{2,1,0:T(8,128)(2,1)S(1)} %get-tuple-element.31), channel_id=1, source_target_pairs={{0,6},{1,7},{2,0},{3,1},{4,2},{5,3},{6,4},{7,5},{8,14},{9,15},{10,... | collective-permute-start | bytes 786440 | tf_op jit(solution)/shard_map/ppermute | solution.py:56
  21.5 3.3 %intra.2 = (f32[512,512]{1,0:T(8,128)}, bf16[4,3,256,256]{3,2,1,0:T(8,128)(2,1)}) custom-call(bf16[512,1024]{1,0:T(8,128)(2,1)} %q_hbm.5, bf16[512,1024]{1,0:T(8,128)(2,1)} %k_hbm.7, bf16[512,1024]{1,0:T(8,128)(2,1)} %v_hbm.7, bf16[8,128,128]{2,1,0:T(8,128)(2,1)} %states.1.refs_0_), custom_call_target="tpu_custom_call" | custom-call | flops 536870912 | bytes 4194304 | tf_op jit(solution)/shard_map/intra/pallas_call | solution.py:463
  24.8 2.7 %all-to-all-done.x_ref = bf16[32,32,128]{2,1,0:T(8,128)(2,1)S(1)} async-done(((bf16[32,32,128]{2,1,0:T(8,128)(2,1)}), bf16[32,32,128]{2,1,0:T(8,128)(2,1)S(1)}, u32[]{:S(2)}, u32[]{:S(2)}) %all-to-all-start) | async-done | bytes 262176 | tf_op jit(solution)/shard_map/all_to_all | solution.py:420
  27.5 0.7 running.2.refs_0_
  28.3 7.1 %all-to-all-start.1 = ((bf16[32,32,128]{2,1,0:T(8,128)(2,1)}), bf16[32,32,128]{2,1,0:T(8,128)(2,1)S(1)}, u32[]{:S(2)}, u32[]{:S(2)}) async-start(bf16[32,32,128]{2,1,0:T(8,128)(2,1)} %running.2.refs_0_), calls=%async_computation.1 | async-start | bytes 524288 | tf_op jit(solution)/shard_map/all_to_all | solution.py:420
  35.4 0.0 copy-done.2
  35.4 0.1 collective-permute-start.3
  35.5 0.0 collective-permute-done.refs_1_.refs_5_
  35.5 0.5 collective-permute-start.4
  36.0 0.0 collective-permute-done.1.refs_2_.refs_6_
  36.0 0.1 collective-permute-start.5
  36.1 0.0 collective-permute-done.2.refs_3_.refs_7_
  36.1 0.4 collective-permute-start.6
  36.5 3.3 %intra.3 = (f32[512,512]{1,0:T(8,128)}, bf16[4,3,256,256]{3,2,1,0:T(8,128)(2,1)}) custom-call(bf16[512,1024]{1,0:T(8,128)(2,1)} %q_hbm.5, bf16[512,1024]{1,0:T(8,128)(2,1)} %k_hbm.7, bf16[512,1024]{1,0:T(8,128)(2,1)} %v_hbm.7, bf16[32,32,128]{2,1,0:T(8,128)(2,1)} %running.2.refs_0_, bf16[2,64,1024]{2,1,0:T(8,128)(2,1)} %collective-permute-done.refs_1_.refs_5_, ...), custom_call_target="tpu_custom_call" | custom-call | flops 536870912 | bytes 4194304 | tf_op jit(solution)/shard_map/intra/pallas_call | solution.py:463
  39.8 0.0 collective-permute-done.3.refs_8_
  39.8 0.0 copy-start.5
  39.9 0.0 collective-permute-done.4.refs_9_
  39.9 0.0 copy-start.6
  39.9 0.0 collective-permute-done.5.refs_10_
  39.9 0.7 copy-done.5
  40.6 0.0 collective-permute-done.6.refs_11_
  40.6 6.0 %all-to-all-done.1 = bf16[32,32,128]{2,1,0:T(8,128)(2,1)S(1)} async-done(((bf16[32,32,128]{2,1,0:T(8,128)(2,1)}), bf16[32,32,128]{2,1,0:T(8,128)(2,1)S(1)}, u32[]{:S(2)}, u32[]{:S(2)}) %all-to-all-start.1) | async-done | bytes 262176 | tf_op jit(solution)/shard_map/all_to_all | solution.py:420
  46.5 0.0 copy-done.6
  46.5 0.0 copy-done.7
  46.5 0.0 copy-done.8
  46.5 3.3 %outs.1 = (f32[8,8,128]{2,1,0:T(8,128)S(1)}, bf16[512,1024]{1,0:T(8,128)(2,1)S(1)}, bf16[512,1024]{1,0:T(8,128)(2,1)S(1)}, bf16[512,1024]{1,0:T(8,128)(2,1)S(1)}...) custom-call(f32[512,512]{1,0:T(8,128)} %get-tuple-element.27.refs_1_, ...), custom_call_target="tpu_custom_call" | custom-call | flops 134217728 | bytes 5242880 | tf_op jit(solution)/shard_map/outs/pallas_call | solution.py:482
  49.8 7.8 %all_to_all.25.sums_ref = f32[8,8,128]{2,1,0:T(8,128)S(1)} all-to-all(f32[8,8,128]{2,1,0:T(8,128)S(1)} %get-tuple-element.33), channel_id=1, replica_groups=mesh['seq'=32,'head'=8] {'head'}, dimensions={0} | all-to-all | bytes 65536 | tf_op jit(solution)/shard_map/all_to_all | solution.py:492
  57.6 2.3 %grads.1 = (bf16[8,128,128]{2,1,0:T(8,128)(2,1)}, bf16[512,1024]{1,0:T(8,128)(2,1)}) custom-call(f32[8,8,128]{2,1,0:T(8,128)S(1)} %all_to_all.25.sums_ref, bf16[512,1024]{1,0:T(8,128)(2,1)S(1)} %get-tuple-element.34.q_ref, bf16[512,1024]{1,0:T(8,128)(2,1)S(1)} %get-tuple-element.35.w_ref, bf16[512,1024]{1,0:T(8,128)(2,1)S(1)} %get-tuple-element.36.o_ref), custom_call_target="tpu_custom_call" | custom-call | flops 134217728 | bytes 4194304 | tf_op jit(solution)/shard_map/grads/pallas_call | solution.py:494
  59.9 4.6 %all-to-all-start.3 = ((bf16[32,32,128]{2,1,0:T(8,128)(2,1)}), bf16[32,32,128]{2,1,0:T(8,128)(2,1)S(1)}, u32[]{:S(2)}, u32[]{:S(2)}) async-start(bf16[32,32,128]{2,1,0:T(8,128)(2,1)} %bitcast.3), calls=%async_computation.3 | async-start | bytes 524288 | tf_op jit(solution)/shard_map/all_to_all | solution.py:420
  64.5 0.8 collective-permute-start.7
  65.3 2.1 %collective-permute-start.8 = (bf16[2,64,1024]{2,1,0:T(8,128)(2,1)}, bf16[2,64,1024]{2,1,0:T(8,128)(2,1)S(1)}, u32[]{:S(2)}, u32[]{:S(2)}) collective-permute-start(bf16[2,64,1024]{2,1,0:T(8,128)(2,1)} %get-tuple-element.48), channel_id=1, source_target_pairs={{0,4},{1,5},{2,6},{3,7},{4,0},{5,1},{6,2},{7,3},{8,12},{9,13},{10,... | collective-permute-start | bytes 786440 | tf_op jit(solution)/shard_map/ppermute | solution.py:56
  67.4 1.1 %collective-permute-start.9 = (bf16[2,64,1024]{2,1,0:T(8,128)(2,1)S(1)}, bf16[2,64,1024]{2,1,0:T(8,128)(2,1)}, u32[]{:S(2)}, u32[]{:S(2)}) collective-permute-start(bf16[2,64,1024]{2,1,0:T(8,128)(2,1)S(1)} %copy-done.9), channel_id=1, source_target_pairs={{0,6},{1,7},{2,0},{3,1},{4,2},{5,3},{6,4},{7,5},{8,14},{9,15},{10,... | collective-permute-start | bytes 786440 | tf_op jit(solution)/shard_map/ppermute | solution.py:56
  68.5 6.6 %backs.1 = (bf16[512,1024]{1,0:T(8,128)(2,1)}, bf16[512,1024]{1,0:T(8,128)(2,1)}, bf16[512,1024]{1,0:T(8,128)(2,1)}) custom-call(bf16[512,1024]{1,0:T(8,128)(2,1)} %q_hbm.5, bf16[512,1024]{1,0:T(8,128)(2,1)} %k_hbm.7, bf16[512,1024]{1,0:T(8,128)(2,1)} %v_hbm.7, bf16[512,1024]{1,0:T(8,128)(2,1)} %get-tuple-element.37.do_hbm, ...), custom_call_target="tpu_custom_call" | custom-call | flops 1610612736 | bytes 10485760 | tf_op jit(solution)/shard_map/backs/pallas_call | solution.py:506
  75.1 0.0 copy-start.3
  75.1 1.6 %all-to-all-done.3.x_ref = bf16[32,32,128]{2,1,0:T(8,128)(2,1)S(1)} async-done(((bf16[32,32,128]{2,1,0:T(8,128)(2,1)}), bf16[32,32,128]{2,1,0:T(8,128)(2,1)S(1)}, u32[]{:S(2)}, u32[]{:S(2)}) %all-to-all-start.3) | async-done | bytes 262176 | tf_op jit(solution)/shard_map/all_to_all | solution.py:420
  76.8 0.7 running.3
  77.5 8.2 %all-to-all-start.4 = ((bf16[32,32,128]{2,1,0:T(8,128)(2,1)}), bf16[32,32,128]{2,1,0:T(8,128)(2,1)S(1)}, u32[]{:S(2)}, u32[]{:S(2)}) async-start(bf16[32,32,128]{2,1,0:T(8,128)(2,1)} %running.3), calls=%async_computation.4 | async-start | bytes 524288 | tf_op jit(solution)/shard_map/all_to_all | solution.py:420
  85.7 0.0 copy-done.3
  85.7 0.1 collective-permute-start.10
  85.8 0.0 collective-permute-done.7.refs_1_
  85.8 0.5 collective-permute-start.11
  86.3 0.0 collective-permute-done.8.refs_2_
  86.3 0.1 collective-permute-start.12
  86.4 0.0 collective-permute-done.9.refs_3_
  86.4 0.4 collective-permute-start.13
  86.8 0.5 collective-permute-done.10.refs_4_
  87.3 0.4 collective-permute-done.11.refs_5_
  87.7 0.7 collective-permute-done.12.refs_6_
  88.4 0.2 collective-permute-done.13.refs_7_
  88.6 3.5 %gates.1 = bf16[64,8192]{1,0:T(8,128)(2,1)} custom-call(bf16[2,64,1024]{2,1,0:T(8,128)(2,1)S(1)} %copy-done.3, bf16[2,64,1024]{2,1,0:T(8,128)(2,1)S(1)} %collective-permute-done.7.refs_1_, bf16[2,64,1024]{2,1,0:T(8,128)(2,1)S(1)} %collective-permute-done.8.refs_2_, bf16[2,64,1024]{2,1,0:T(8,128)(2,1)} %collective-permute-done.9.refs_3_, ...), custom_call_target="tpu_custom_call" | custom-call | flops 10485760 | bytes 4194304 | tf_op jit(solution)/shard_map/gates/pallas_call | solution.py:521
  92.2 4.6 %all-to-all-done.4 = bf16[32,32,128]{2,1,0:T(8,128)(2,1)S(1)} async-done(((bf16[32,32,128]{2,1,0:T(8,128)(2,1)}), bf16[32,32,128]{2,1,0:T(8,128)(2,1)S(1)}, u32[]{:S(2)}, u32[]{:S(2)}) %all-to-all-start.4) | async-done | bytes 262176 | tf_op jit(solution)/shard_map/all_to_all | solution.py:420
  96.8 3.6 %last.1 = (bf16[512,1024]{1,0:T(8,128)(2,1)}, bf16[512,1024]{1,0:T(8,128)(2,1)}) custom-call(bf16[512,1024]{1,0:T(8,128)(2,1)} %get-tuple-element.41.refs_0_.ak_hbm, bf16[512,1024]{1,0:T(8,128)(2,1)} %get-tuple-element.42.av_hbm, bf16[512,1024]{1,0:T(8,128)(2,1)} %k_hbm.7, bf16[512,1024]{1,0:T(8,128)(2,1)} %v_hbm.7, bf16[8,128,128]{2,1,0:T(8,128)(2,1)S(1)} %bitcast.7), custom_call_target="tpu_custom_call" | custom-call | flops 268435456 | bytes 8388608 | tf_op jit(solution)/shard_map/last/pallas_call | solution.py:529
  (4 shorter events, 0.0 us)
Async XLA Ops:
  0.6 14.6 %copy-start.1 = (bf16[64,8192]{1,0:T(8,128)(2,1)S(1)}, bf16[64,8192]{1,0:T(8,128)(2,1)}, u32[]{:S(2)}) copy-start(bf16[64,8192]{1,0:T(8,128)(2,1)} %refs_9_.1) | copy-start | bytes 3145732
  0.6 14.6 %copy-start = (bf16[64,8192]{1,0:T(8,128)(2,1)S(1)}, bf16[64,8192]{1,0:T(8,128)(2,1)}, u32[]{:S(2)}) copy-start(bf16[64,8192]{1,0:T(8,128)(2,1)} %refs_8_.1) | copy-start | bytes 3145732
  0.7 14.6 %copy-start.4 = (f32[8192]{0:T(1024)S(1)}, f32[8192]{0:T(1024)}, u32[]{:S(2)}) copy-start(f32[8192]{0:T(1024)} %param.10) | copy-start | bytes 98308
  3.8 23.7 %all-to-all-start = ((bf16[32,32,128]{2,1,0:T(8,128)(2,1)}), bf16[32,32,128]{2,1,0:T(8,128)(2,1)S(1)}, u32[]{:S(2)}, u32[]{:S(2)}) async-start(bf16[32,32,128]{2,1,0:T(8,128)(2,1)} %bitcast), calls=%async_computation | async-start | bytes 524288 | tf_op jit(solution)/shard_map/all_to_all | solution.py:420
  15.8 19.6 %copy-start.2 = (bf16[2,64,1024]{2,1,0:T(8,128)(2,1)}, bf16[2,64,1024]{2,1,0:T(8,128)(2,1)S(1)}, u32[]{:S(2)}) copy-start(bf16[2,64,1024]{2,1,0:T(8,128)(2,1)S(1)} %get-tuple-element.28.refs_0_.refs_4_) | copy-start | bytes 786436
  15.8 19.7 %collective-permute-start = (bf16[2,64,1024]{2,1,0:T(8,128)(2,1)S(1)}, bf16[2,64,1024]{2,1,0:T(8,128)(2,1)}, u32[]{:S(2)}, u32[]{:S(2)}) collective-permute-start(bf16[2,64,1024]{2,1,0:T(8,128)(2,1)S(1)} %get-tuple-element.29), channel_id=1, source_target_pairs={{0,2},{1,3},{2,4},{3,5},{4,6},{5,7},{6,0},{7,1},{8,10},{9,11},{10,... | collective-permute-start | bytes 786440 | tf_op jit(solution)/shard_map/ppermute | solution.py:56
  17.4 18.6 %collective-permute-start.1 = (bf16[2,64,1024]{2,1,0:T(8,128)(2,1)S(1)}, bf16[2,64,1024]{2,1,0:T(8,128)(2,1)}, u32[]{:S(2)}, u32[]{:S(2)}) collective-permute-start(bf16[2,64,1024]{2,1,0:T(8,128)(2,1)S(1)} %get-tuple-element.30), channel_id=1, source_target_pairs={{0,4},{1,5},{2,6},{3,7},{4,0},{5,1},{6,2},{7,3},{8,12},{9,13},{10,... | collective-permute-start | bytes 786440 | tf_op jit(solution)/shard_map/ppermute | solution.py:56
  20.1 16.0 %collective-permute-start.2 = (bf16[2,64,1024]{2,1,0:T(8,128)(2,1)S(1)}, bf16[2,64,1024]{2,1,0:T(8,128)(2,1)}, u32[]{:S(2)}, u32[]{:S(2)}) collective-permute-start(bf16[2,64,1024]{2,1,0:T(8,128)(2,1)S(1)} %get-tuple-element.31), channel_id=1, source_target_pairs={{0,6},{1,7},{2,0},{3,1},{4,2},{5,3},{6,4},{7,5},{8,14},{9,15},{10,... | collective-permute-start | bytes 786440 | tf_op jit(solution)/shard_map/ppermute | solution.py:56
  28.3 18.3 %all-to-all-start.1 = ((bf16[32,32,128]{2,1,0:T(8,128)(2,1)}), bf16[32,32,128]{2,1,0:T(8,128)(2,1)S(1)}, u32[]{:S(2)}, u32[]{:S(2)}) async-start(bf16[32,32,128]{2,1,0:T(8,128)(2,1)} %running.2.refs_0_), calls=%async_computation.1 | async-start | bytes 524288 | tf_op jit(solution)/shard_map/all_to_all | solution.py:420
  35.4 4.4 %collective-permute-start.3 = (bf16[2,64,1024]{2,1,0:T(8,128)(2,1)S(1)}, bf16[2,64,1024]{2,1,0:T(8,128)(2,1)S(1)}, u32[]{:S(2)}, u32[]{:S(2)}) collective-permute-start(bf16[2,64,1024]{2,1,0:T(8,128)(2,1)S(1)} %get-tuple-element.28.refs_0_.refs_4_), channel_id=1, source_target_pairs={{0,1},{1,0},{2,3},{3,2},{4,5},{5,4},{6,7},{7,6},{8,9},{9,8},{10,11... | collective-permute-start | bytes 786440 | tf_op jit(solution)/shard_map/ppermute | solution.py:57
  35.5 4.3 %collective-permute-start.4 = (bf16[2,64,1024]{2,1,0:T(8,128)(2,1)}, bf16[2,64,1024]{2,1,0:T(8,128)(2,1)S(1)}, u32[]{:S(2)}, u32[]{:S(2)}) collective-permute-start(bf16[2,64,1024]{2,1,0:T(8,128)(2,1)} %collective-permute-done.refs_1_.refs_5_), channel_id=1, source_target_pairs={{0,1},{1,0},{2,3},{3,2},{4,5},{5,4},{6,7},{7,6},{8,9},{9,8},{10,11... | collective-permute-start | bytes 786440 | tf_op jit(solution)/shard_map/ppermute | solution.py:57
  36.0 3.9 %collective-permute-start.5 = (bf16[2,64,1024]{2,1,0:T(8,128)(2,1)}, bf16[2,64,1024]{2,1,0:T(8,128)(2,1)S(1)}, u32[]{:S(2)}, u32[]{:S(2)}) collective-permute-start(bf16[2,64,1024]{2,1,0:T(8,128)(2,1)} %collective-permute-done.1.refs_2_.refs_6_), channel_id=1, source_target_pairs={{0,1},{1,0},{2,3},{3,2},{4,5},{5,4},{6,7},{7,6},{8,9},{9,8},{10,11... | collective-permute-start | bytes 786440 | tf_op jit(solution)/shard_map/ppermute | solution.py:57
  36.1 4.5 %collective-permute-start.6 = (bf16[2,64,1024]{2,1,0:T(8,128)(2,1)}, bf16[2,64,1024]{2,1,0:T(8,128)(2,1)S(1)}, u32[]{:S(2)}, u32[]{:S(2)}) collective-permute-start(bf16[2,64,1024]{2,1,0:T(8,128)(2,1)} %collective-permute-done.2.refs_3_.refs_7_), channel_id=1, source_target_pairs={{0,1},{1,0},{2,3},{3,2},{4,5},{5,4},{6,7},{7,6},{8,9},{9,8},{10,11... | collective-permute-start | bytes 786440 | tf_op jit(solution)/shard_map/ppermute | solution.py:57
  39.8 0.7 copy-start.5
  39.9 6.7 %copy-start.6 = (bf16[2,64,1024]{2,1,0:T(8,128)(2,1)}, bf16[2,64,1024]{2,1,0:T(8,128)(2,1)S(1)}, u32[]{:S(2)}) copy-start(bf16[2,64,1024]{2,1,0:T(8,128)(2,1)S(1)} %collective-permute-done.4.refs_9_) | copy-start | bytes 786436
  40.6 6.0 %copy-start.7 = (bf16[2,64,1024]{2,1,0:T(8,128)(2,1)}, bf16[2,64,1024]{2,1,0:T(8,128)(2,1)S(1)}, u32[]{:S(2)}) copy-start(bf16[2,64,1024]{2,1,0:T(8,128)(2,1)S(1)} %collective-permute-done.5.refs_10_) | copy-start | bytes 786436
  40.6 6.0 %copy-start.8 = (bf16[2,64,1024]{2,1,0:T(8,128)(2,1)}, bf16[2,64,1024]{2,1,0:T(8,128)(2,1)S(1)}, u32[]{:S(2)}) copy-start(bf16[2,64,1024]{2,1,0:T(8,128)(2,1)S(1)} %collective-permute-done.6.refs_11_) | copy-start | bytes 786436
  57.6 9.8 %copy-start.9 = (bf16[2,64,1024]{2,1,0:T(8,128)(2,1)S(1)}, bf16[2,64,1024]{2,1,0:T(8,128)(2,1)}, u32[]{:S(2)}) copy-start(bf16[2,64,1024]{2,1,0:T(8,128)(2,1)} %get-tuple-element.49) | copy-start | bytes 786436
  59.9 16.8 %all-to-all-start.3 = ((bf16[32,32,128]{2,1,0:T(8,128)(2,1)}), bf16[32,32,128]{2,1,0:T(8,128)(2,1)S(1)}, u32[]{:S(2)}, u32[]{:S(2)}) async-start(bf16[32,32,128]{2,1,0:T(8,128)(2,1)} %bitcast.3), calls=%async_computation.3 | async-start | bytes 524288 | tf_op jit(solution)/shard_map/all_to_all | solution.py:420
  64.5 21.3 %collective-permute-start.7 = (bf16[2,64,1024]{2,1,0:T(8,128)(2,1)}, bf16[2,64,1024]{2,1,0:T(8,128)(2,1)S(1)}, u32[]{:S(2)}, u32[]{:S(2)}) collective-permute-start(bf16[2,64,1024]{2,1,0:T(8,128)(2,1)} %get-tuple-element.47), channel_id=1, source_target_pairs={{0,2},{1,3},{2,4},{3,5},{4,6},{5,7},{6,0},{7,1},{8,10},{9,11},{10,... | collective-permute-start | bytes 786440 | tf_op jit(solution)/shard_map/ppermute | solution.py:56
  65.3 20.9 %collective-permute-start.8 = (bf16[2,64,1024]{2,1,0:T(8,128)(2,1)}, bf16[2,64,1024]{2,1,0:T(8,128)(2,1)S(1)}, u32[]{:S(2)}, u32[]{:S(2)}) collective-permute-start(bf16[2,64,1024]{2,1,0:T(8,128)(2,1)} %get-tuple-element.48), channel_id=1, source_target_pairs={{0,4},{1,5},{2,6},{3,7},{4,0},{5,1},{6,2},{7,3},{8,12},{9,13},{10,... | collective-permute-start | bytes 786440 | tf_op jit(solution)/shard_map/ppermute | solution.py:56
  67.4 19.0 %collective-permute-start.9 = (bf16[2,64,1024]{2,1,0:T(8,128)(2,1)S(1)}, bf16[2,64,1024]{2,1,0:T(8,128)(2,1)}, u32[]{:S(2)}, u32[]{:S(2)}) collective-permute-start(bf16[2,64,1024]{2,1,0:T(8,128)(2,1)S(1)} %copy-done.9), channel_id=1, source_target_pairs={{0,6},{1,7},{2,0},{3,1},{4,2},{5,3},{6,4},{7,5},{8,14},{9,15},{10,... | collective-permute-start | bytes 786440 | tf_op jit(solution)/shard_map/ppermute | solution.py:56
  75.1 10.6 %copy-start.3 = (bf16[2,64,1024]{2,1,0:T(8,128)(2,1)S(1)}, bf16[2,64,1024]{2,1,0:T(8,128)(2,1)}, u32[]{:S(2)}) copy-start(bf16[2,64,1024]{2,1,0:T(8,128)(2,1)} %get-tuple-element.46.refs_0_) | copy-start | bytes 786436
  77.5 19.3 %all-to-all-start.4 = ((bf16[32,32,128]{2,1,0:T(8,128)(2,1)}), bf16[32,32,128]{2,1,0:T(8,128)(2,1)S(1)}, u32[]{:S(2)}, u32[]{:S(2)}) async-start(bf16[32,32,128]{2,1,0:T(8,128)(2,1)} %running.3), calls=%async_computation.4 | async-start | bytes 524288 | tf_op jit(solution)/shard_map/all_to_all | solution.py:420
  85.7 1.6 %collective-permute-start.10 = (bf16[2,64,1024]{2,1,0:T(8,128)(2,1)S(1)}, bf16[2,64,1024]{2,1,0:T(8,128)(2,1)S(1)}, u32[]{:S(2)}, u32[]{:S(2)}) collective-permute-start(bf16[2,64,1024]{2,1,0:T(8,128)(2,1)S(1)} %copy-done.3), channel_id=1, source_target_pairs={{0,1},{1,0},{2,3},{3,2},{4,5},{5,4},{6,7},{7,6},{8,9},{9,8},{10,11... | collective-permute-start | bytes 786440 | tf_op jit(solution)/shard_map/ppermute | solution.py:57
  85.8 1.9 %collective-permute-start.11 = (bf16[2,64,1024]{2,1,0:T(8,128)(2,1)S(1)}, bf16[2,64,1024]{2,1,0:T(8,128)(2,1)S(1)}, u32[]{:S(2)}, u32[]{:S(2)}) collective-permute-start(bf16[2,64,1024]{2,1,0:T(8,128)(2,1)S(1)} %collective-permute-done.7.refs_1_), channel_id=1, source_target_pairs={{0,1},{1,0},{2,3},{3,2},{4,5},{5,4},{6,7},{7,6},{8,9},{9,8},{10,11... | collective-permute-start | bytes 786440 | tf_op jit(solution)/shard_map/ppermute | solution.py:57
  86.3 2.1 %collective-permute-start.12 = (bf16[2,64,1024]{2,1,0:T(8,128)(2,1)S(1)}, bf16[2,64,1024]{2,1,0:T(8,128)(2,1)S(1)}, u32[]{:S(2)}, u32[]{:S(2)}) collective-permute-start(bf16[2,64,1024]{2,1,0:T(8,128)(2,1)S(1)} %collective-permute-done.8.refs_2_), channel_id=1, source_target_pairs={{0,1},{1,0},{2,3},{3,2},{4,5},{5,4},{6,7},{7,6},{8,9},{9,8},{10,11... | collective-permute-start | bytes 786440 | tf_op jit(solution)/shard_map/ppermute | solution.py:57
  86.4 2.2 %collective-permute-start.13 = (bf16[2,64,1024]{2,1,0:T(8,128)(2,1)}, bf16[2,64,1024]{2,1,0:T(8,128)(2,1)S(1)}, u32[]{:S(2)}, u32[]{:S(2)}) collective-permute-start(bf16[2,64,1024]{2,1,0:T(8,128)(2,1)} %collective-permute-done.9.refs_3_), channel_id=1, source_target_pairs={{0,1},{1,0},{2,3},{3,2},{4,5},{5,4},{6,7},{7,6},{8,9},{9,8},{10,11... | collective-permute-start | bytes 786440 | tf_op jit(solution)/shard_map/ppermute | solution.py:57

commit v5 on v4

--- a/solution.py
+++ b/solution.py
@@ -48,14 +48,18 @@
     return lax.rem(chip + sign * dx + n // 2, n // 2) * 2 + flip
 
 
+def across(bundles):
+    n = 2 * len(bundles)
+    return [bundles[0]] + [
+        lax.ppermute(bundles[dx], "head", [(i, (i + 2 * dx) % n) for i in range(n)])
+        for dx in range(1, n // 2)
+    ]
+
+
 def send_all(bundles):
     n = 2 * len(bundles)
-    same = [bundles[0]]
-    for dx in range(1, n // 2):
-        pairs = [(i, (i + 2 * dx) % n) for i in range(n)]
-        same.append(lax.ppermute(bundles[dx], "head", pairs))
-    other = [lax.ppermute(b, "head", [(i, i ^ 1) for i in range(n)]) for b in same]
-    return same + other
+    same = across(bundles)
+    return same + [lax.ppermute(b, "head", [(i, i ^ 1) for i in range(n)]) for b in same]
 
 
 def parts(n):
@@ -190,7 +194,7 @@
     refs = refs[1:]
     w_any = refs[3 : 3 + n_head]
     sums_ref, o_ref, w_ref, q_ref = refs[3 + n_head : 7 + n_head]
-    *bundles, i_ref, sems, out_sems = refs[7 + n_head :]
+    give_hbm, i_ref, sems, out_sems = refs[7 + n_head :]
     d = HEAD_DIM
     t, own = q_ref.shape
     rows = t // n_head
@@ -223,12 +227,9 @@
     co = start_all(
         [
             pltpu.make_async_copy(
-                o_ref.at[rows_of(n_head, dx, dc, 1, rows), :],
-                bundles[dx].at[dc],
-                out_sems.at[2 * dx + dc],
+                o_ref.at[rows_of(n_head, dx, 1, 1, rows), :], give_hbm.at[dx], out_sems.at[dx]
             )
             for dx in range(n_head // 2)
-            for dc in range(2)
         ]
     )
     wait_all(cw)
@@ -249,7 +250,14 @@
     wait_all(co)
 
 
-def grad_kernel(width, sums_ref, q_ref, w_ref, o_ref, z_ref, do_hbm, do_ref, sems):
+def grad_kernel(n_head, width, sums_ref, q_ref, w_ref, o_ref, got_any, z_ref, do_hbm, *refs):
+    *bundles, do_ref, sems, out_sems = refs
+    rows = got_any.shape[1]
+    ready = []
+    for dx, bundle in enumerate(bundles):
+        own_rows = o_ref.at[rows_of(n_head, dx, 0, 1, rows), :]
+        ready.append(pltpu.make_async_copy(own_rows, bundle.at[0], out_sems.at[2 * dx]))
+        ready.append(pltpu.make_async_copy(got_any.at[dx], bundle.at[1], out_sems.at[2 * dx + 1]))
     d = HEAD_DIM
     t, own = q_ref.shape
     tile = jnp.sum(sums_ref[...], axis=0)
@@ -272,10 +280,11 @@
             )
         )
         copies[r].start()
+        start_all(ready[r * len(ready) // blocks : (r + 1) * len(ready) // blocks])
     for h in range(own // d):
         cols = slice(h * d, (h + 1) * d)
         z_ref[h] = mm_at(q_ref[:, cols], do_ref[:, cols]).astype(z_ref.dtype)
-    wait_all(copies)
+    wait_all(copies + ready)
 
 
 def back_kernel(
@@ -343,8 +352,8 @@
 
 
 def last_kernel(
-    ak_hbm, av_hbm, k_hbm, v_hbm, s_ref, gk_hbm, gv_hbm,
-    ak_ref, av_ref, k_ref, v_ref, gk_ref, gv_ref, sems, out_sems,
+    ak_hbm, av_hbm, k_ref, v_ref, s_ref, gk_hbm, gv_hbm,
+    ak_ref, av_ref, gk_ref, gv_ref, sems, out_sems,
 ):
     d = HEAD_DIM
     t, own = k_ref.shape
@@ -352,7 +361,7 @@
     ins = [
         by_pairs(src, dst, sems, n * j)
         for j, (src, dst) in enumerate(
-            ((k_hbm, k_ref), (av_hbm, av_ref), (v_hbm, v_ref), (ak_hbm, ak_ref))
+            ((av_hbm, av_ref), (ak_hbm, ak_ref))
         )
     ]
     for i in range(n):
@@ -376,21 +385,38 @@
 
 
 def gate_kernel(n, *refs):
-    *o_refs, gate_ref, grad_ref, gain_ref, gg_ref = refs
+    chips = n // 2
+    srcs, gain_ref, gg_hbm = refs[: chips + 2], refs[chips + 2], refs[chips + 3]
+    dsts, (gg_ref, sems, out_sems) = refs[chips + 4 : 2 * chips + 6], refs[2 * chips + 6 :]
+    loads = start_all(
+        [pltpu.make_async_copy(x, y, sems.at[j]) for j, (x, y) in enumerate(zip(srcs, dsts))]
+    )
+    *o_refs, gate_ref, grad_ref = dsts
     wide = o_refs[0].shape[2]
     total = None
-    for k, _, dc in parts(n):
-        o = o_refs[k][dc].astype(F32)
-        s = o * o
-        total = s if total is None else total + s
-    inv = lax.rsqrt(jnp.sum(total, axis=1, keepdims=True) / (n * wide) + EPS)
-    for k, dx, dc in parts(n):
-        cols = pl.ds(pl.multiple_of(place(n, dx, dc, -1) * wide, wide), wide)
-        g = gate_ref[:, cols].astype(F32)
-        s = jax.nn.sigmoid(g)
-        scaled = grad_ref[:, cols].astype(F32) * gain_ref[:, cols]
-        normed = o_refs[k][dc].astype(F32) * inv
-        gg_ref[:, cols] = (scaled * normed * s * (1.0 + g * (1.0 - s))).astype(BF16)
+    for dx in range(chips):
+        loads[dx].wait()
+        for dc in range(2):
+            o = o_refs[dx][dc].astype(F32)
+            o = jnp.sum(o * o, axis=1, keepdims=True)
+            total = o if total is None else total + o
+    inv = lax.rsqrt(total / (n * wide) + EPS)
+    wait_all(loads[chips:])
+    stores = []
+    for dx in range(chips):
+        for dc in range(2):
+            cols = pl.ds(pl.multiple_of(place(n, dx, dc, -1) * wide, wide), wide)
+            g = gate_ref[:, cols].astype(F32)
+            s = jax.nn.sigmoid(g)
+            scaled = grad_ref[:, cols].astype(F32) * gain_ref[:, cols]
+            normed = o_refs[dx][dc].astype(F32) * inv
+            gg_ref[:, cols] = (scaled * normed * s * (1.0 + g * (1.0 - s))).astype(BF16)
+            store = pltpu.make_async_copy(
+                gg_ref.at[:, cols], gg_hbm.at[:, cols], out_sems.at[2 * dx + dc]
+            )
+            store.start()
+            stores.append(store)
+    wait_all(stores)
 
 
 def on_device(query, key_in, value, gate, gain, grad_out):
@@ -430,6 +456,7 @@
             name="running",
         )(states, *after)
 
+    keys, values = in_vmem(key_in), in_vmem(value)
     query, key_in, value = in_hbm(query), in_hbm(key_in), in_hbm(value)
     states = pl.pallas_call(
         state_kernel,
@@ -479,28 +506,30 @@
     inner1, scores1 = intra(some, in_hbm(summed), *weighted[1:chips])
 
     tile = (n_head, 2 * t // d, d)
-    sums, out, weighted, queries, *bundles = pl.pallas_call(
+    sums, out, weighted, queries, given = pl.pallas_call(
         functools.partial(out_kernel, n_head),
-        out_shape=[sds(tile, F32), full, full, full] + [pltpu.HBM(bundle, BF16)] * chips,
+        out_shape=[sds(tile, F32), full, full, full, pltpu.HBM((chips, rows, own), BF16)],
         in_specs=[anywhere] * 3 + [whole] + [anywhere] * n_head,
-        out_specs=[whole] * 4 + [anywhere] * chips,
-        scratch_shapes=[full32, dma(3 * t // d + n_head), dma(n_head)],
+        out_specs=[whole] * 4 + [anywhere],
+        scratch_shapes=[full32, dma(3 * t // d + n_head), dma(chips)],
         compiler_params=params(),
         cost_estimate=cost(small, 10 * t * own),
         name="outs",
     )(inner0, inner1, query, prefix, *weighted)
     sums = lax.all_to_all(sums, "head", 0, 0, tiled=True)
 
-    states, grad_attn = pl.pallas_call(
-        functools.partial(grad_kernel, float(width)),
-        out_shape=[sds((heads, d, d), BF16), pltpu.HBM((t, own), BF16)],
-        in_specs=[whole] * 4,
-        out_specs=[whole, anywhere],
-        scratch_shapes=[full, dma(t // d)],
+    got = lax.ppermute(given, "head", [(i, i ^ 1) for i in range(n_head)])
+    states, grad_attn, *bundles = pl.pallas_call(
+        functools.partial(grad_kernel, n_head, float(width)),
+        out_shape=[sds((heads, d, d), BF16), pltpu.HBM((t, own), BF16)]
+        + [pltpu.HBM(bundle, BF16)] * chips,
+        in_specs=[whole] * 4 + [anywhere],
+        out_specs=[whole] + [anywhere] * (1 + chips),
+        scratch_shapes=[full, dma(t // d), dma(n_head)],
         compiler_params=params(),
         cost_estimate=cost(small, 8 * t * own),
         name="grads",
-    )(sums, in_vmem(queries), in_vmem(weighted), in_vmem(out))
+    )(sums, in_vmem(queries), in_vmem(weighted), in_vmem(out), got)
     received = exchange(states)
 
     part_key, part_value, grad_query = pl.pallas_call(
@@ -517,25 +546,30 @@
     part_key, part_value = in_hbm(part_key), in_hbm(part_value)
     suffix = exchange(running(received, True, part_key)).reshape(heads, d, d)
 
-    token_rows = send_all(bundles)
+    token_rows = across(bundles)
+    strip = pltpu.VMEM((rows, width), BF16)
     grad_gate = pl.pallas_call(
         functools.partial(gate_kernel, n_head),
         out_shape=sds((rows, width), BF16),
-        compiler_params=params(),
-        cost_estimate=cost(20 * rows * width, 8 * rows * width),
+        in_specs=[anywhere] * (chips + 2) + [whole],
+        out_specs=anywhere,
+        scratch_shapes=[pltpu.VMEM(bundle, BF16)] * chips
+        + [strip, strip, strip, dma(chips + 2), dma(n_head)],
+        compiler_params=params(),
+        cost_estimate=cost(30 * large, 200 * t * own),
         name="gates",
-    )(*token_rows, in_vmem(gate), in_vmem(grad_out), gain)
+    )(in_hbm(token_rows[0]), *token_rows[1:], in_hbm(gate), in_hbm(grad_out), gain)
 
     grad_key, grad_value = pl.pallas_call(
         last_kernel,
         out_shape=[sds((t, own), BF16), sds((t, own), BF16)],
-        in_specs=[anywhere] * 4 + [whole],
+        in_specs=[anywhere] * 2 + [whole] * 3,
         out_specs=[anywhere] * 2,
-        scratch_shapes=[full] * 6 + [dma(4 * pairs), dma(2 * pairs)],
+        scratch_shapes=[full] * 4 + [dma(2 * pairs), dma(2 * pairs)],
         compiler_params=params(),
         cost_estimate=cost(2 * small, 16 * t * own),
         name="last",
-    )(part_key, part_value, key_in, value, suffix)
+    )(part_key, part_value, keys, values, suffix)
     return grad_query, grad_key, grad_value, grad_gate
 
 

time: 101 us -> 101 us (level)
  starting transfers between devices: 43.2 us -> 41.9 us
    all_to_all x4, waiting for transfers between devices: 14.9 us -> 17.7 us  [exchange(): return lax.all_to_all(states.reshape(piece), 'seq', 0, 0, tiled=True)]
    ppermute x8 -> x4, waiting for transfers between devices: 1.85 us -> 0.01 us  [send_all(): lax.ppermute(b, 'head', [(i, i ^ 1) for i in range(n)])]
    ppermute x8 -> x4, starting transfers between devices: 2.19 us -> 1.08 us  [send_all(): lax.ppermute(b, 'head', [(i, i ^ 1) for i in range(n)])]
    ppermute x6 -> x7, starting transfers between devices: 9.71 us -> 9.61 us  [the longest x6 9.52 us: across(): lax.ppermute(bundles[dx], 'head', [(i, (i + 2 * dx) % n) for i in range(n)])]
  transfers between devices with their start and end apart: 18 -> 15, of which waited for: 8 -> 4; matrix products, arithmetic and copies ran while one was open for 0% -> 0% of each run, Pallas kernels for 19% -> 19%
where the time goes in v5:
time: 101 us
  starting transfers between devices  41.9 us (41%)
  Pallas kernels  31.7 us (31%)
  waiting for transfers between devices  17.7 us (18%)
  blocking collectives  7.82 us (8%)
  between operations  1.1 us (1%)
    all_to_all x4, starting transfers between devices, exchange(): return lax.all_to_all(states.reshape(piece), 'seq', 0, 0, tiled=True)  31.2 us
    all_to_all x4, waiting for transfers between devices, exchange(): return lax.all_to_all(states.reshape(piece), 'seq', 0, 0, tiled=True)  17.7 us
    ppermute x6, starting transfers between devices, across(): lax.ppermute(bundles[dx], 'head', [(i, (i + 2 * dx) % n) for i in range(n)])  9.52 us
    all_to_all x1, blocking collectives, on_device(): sums = lax.all_to_all(sums, 'head', 0, 0, tiled=True)  7.82 us
    pallas_call x2, Pallas kernels, intra(): pl.pallas_call(functools.partial(intra_kernel, first), out_shape=[pltpu.H...  6.61 us
    pallas_call x1, Pallas kernels, on_device(): pl.pallas_call(back_kernel, out_shape=[pltpu.HBM((t, own), BF16)] * 2 + [...  6.59 us
    pallas_call x1, Pallas kernels, on_device(): pl.pallas_call(functools.partial(gate_kernel, n_head), out_shape=sds((row...  4.14 us
    pallas_call x1, Pallas kernels, on_device(): pl.pallas_call(last_kernel, out_shape=[sds((t, own), BF16), sds((t, own),...  3.35 us
  transfers between devices with their start and end apart: 15, of which 4 were waited for; matrix products, arithmetic and copies ran while one was open for 0% of the time, Pallas kernels for 19%

profile of v5, /device:TPU:32, one launch (start us, length us, event | category | flops | bytes accessed | tf_op | source)
XLA Modules:
  0.0 100.6 jit_solution(10579748754059548401)
XLA Ops:
  0.6 0.0 copy-start.3
  0.6 0.0 copy-start.2
  0.7 0.0 copy-start.5
  0.7 3.2 %states.1.refs_0_ = bf16[8,128,128]{2,1,0:T(8,128)(2,1)} custom-call(bf16[512,1024]{1,0:T(8,128)(2,1)} %k_ref.1, bf16[512,1024]{1,0:T(8,128)(2,1)} %v_ref.1), custom_call_target="tpu_custom_call" | custom-call | flops 268435456 | bytes 2097152 | tf_op jit(solution)/shard_map/states/pallas_call | solution.py:461
  3.8 11.4 %all-to-all-start = ((bf16[32,32,128]{2,1,0:T(8,128)(2,1)}), bf16[32,32,128]{2,1,0:T(8,128)(2,1)S(1)}, u32[]{:S(2)}, u32[]{:S(2)}) async-start(bf16[32,32,128]{2,1,0:T(8,128)(2,1)} %bitcast), calls=%async_computation | async-start | bytes 524288 | tf_op jit(solution)/shard_map/all_to_all | solution.py:446
  15.2 0.0 copy-done.3
  15.2 0.0 copy-done.2
  15.2 0.0 copy-done.5
  15.3 0.5 weigh.1
  15.8 0.0 copy-start.4
  15.8 1.6 %collective-permute-start = (bf16[2,64,1024]{2,1,0:T(8,128)(2,1)S(1)}, bf16[2,64,1024]{2,1,0:T(8,128)(2,1)S(1)}, u32[]{:S(2)}, u32[]{:S(2)}) collective-permute-start(bf16[2,64,1024]{2,1,0:T(8,128)(2,1)S(1)} %get-tuple-element.30), channel_id=1, source_target_pairs={{0,2},{1,3},{2,4},{3,5},{4,6},{5,7},{6,0},{7,1},{8,10},{9,11},{10,... | collective-permute-start | bytes 786440 | tf_op jit(solution)/shard_map/ppermute | solution.py:54
  17.4 2.7 %collective-permute-start.1 = (bf16[2,64,1024]{2,1,0:T(8,128)(2,1)S(1)}, bf16[2,64,1024]{2,1,0:T(8,128)(2,1)S(1)}, u32[]{:S(2)}, u32[]{:S(2)}) collective-permute-start(bf16[2,64,1024]{2,1,0:T(8,128)(2,1)S(1)} %get-tuple-element.31), channel_id=1, source_target_pairs={{0,4},{1,5},{2,6},{3,7},{4,0},{5,1},{6,2},{7,3},{8,12},{9,13},{10,... | collective-permute-start | bytes 786440 | tf_op jit(solution)/shard_map/ppermute | solution.py:54
  20.1 1.4 %collective-permute-start.2 = (bf16[2,64,1024]{2,1,0:T(8,128)(2,1)S(1)}, bf16[2,64,1024]{2,1,0:T(8,128)(2,1)S(1)}, u32[]{:S(2)}, u32[]{:S(2)}) collective-permute-start(bf16[2,64,1024]{2,1,0:T(8,128)(2,1)S(1)} %get-tuple-element.32), channel_id=1, source_target_pairs={{0,6},{1,7},{2,0},{3,1},{4,2},{5,3},{6,4},{7,5},{8,14},{9,15},{10,... | collective-permute-start | bytes 786440 | tf_op jit(solution)/shard_map/ppermute | solution.py:54
  21.5 3.3 %intra.2 = (f32[512,512]{1,0:T(8,128)}, bf16[4,3,256,256]{3,2,1,0:T(8,128)(2,1)}) custom-call(bf16[512,1024]{1,0:T(8,128)(2,1)} %q_hbm.5, bf16[512,1024]{1,0:T(8,128)(2,1)} %k_ref.1, bf16[512,1024]{1,0:T(8,128)(2,1)} %v_ref.1, bf16[8,128,128]{2,1,0:T(8,128)(2,1)} %states.1.refs_0_), custom_call_target="tpu_custom_call" | custom-call | flops 536870912 | bytes 4194304 | tf_op jit(solution)/shard_map/intra/pallas_call | solution.py:490
  24.9 2.7 %all-to-all-done.x_ref = bf16[32,32,128]{2,1,0:T(8,128)(2,1)S(1)} async-done(((bf16[32,32,128]{2,1,0:T(8,128)(2,1)}), bf16[32,32,128]{2,1,0:T(8,128)(2,1)S(1)}, u32[]{:S(2)}, u32[]{:S(2)}) %all-to-all-start) | async-done | bytes 262176 | tf_op jit(solution)/shard_map/all_to_all | solution.py:446
  27.5 0.7 running.2.refs_0_
  28.3 7.1 %all-to-all-start.1 = ((bf16[32,32,128]{2,1,0:T(8,128)(2,1)}), bf16[32,32,128]{2,1,0:T(8,128)(2,1)S(1)}, u32[]{:S(2)}, u32[]{:S(2)}) async-start(bf16[32,32,128]{2,1,0:T(8,128)(2,1)} %running.2.refs_0_), calls=%async_computation.1 | async-start | bytes 524288 | tf_op jit(solution)/shard_map/all_to_all | solution.py:446
  35.4 0.0 copy-done.4
  35.4 0.1 collective-permute-start.3
  35.5 0.0 collective-permute-done.refs_1_.refs_5_
  35.5 0.0 copy-start.6
  35.5 0.5 collective-permute-start.4
  36.0 0.0 collective-permute-done.1.refs_2_.refs_6_
  36.0 0.1 collective-permute-start.5
  36.1 0.0 collective-permute-done.2.refs_3_.refs_7_
  36.1 0.4 collective-permute-start.6
  36.5 0.0 copy-done.6
  36.5 0.2 copy-done.7
  36.7 0.1 copy-done.8
  36.8 3.3 %intra.3 = (f32[512,512]{1,0:T(8,128)}, bf16[4,3,256,256]{3,2,1,0:T(8,128)(2,1)}) custom-call(bf16[512,1024]{1,0:T(8,128)(2,1)} %q_hbm.5, bf16[512,1024]{1,0:T(8,128)(2,1)} %k_ref.1, bf16[512,1024]{1,0:T(8,128)(2,1)} %v_ref.1, bf16[32,32,128]{2,1,0:T(8,128)(2,1)} %running.2.refs_0_, bf16[2,64,1024]{2,1,0:T(8,128)(2,1)} %copy-done.6, ...), custom_call_target="tpu_custom_call" | custom-call | flops 536870912 | bytes 4194304 | tf_op jit(solution)/shard_map/intra/pallas_call | solution.py:490
  40.2 0.0 collective-permute-done.3.refs_8_
  40.2 0.0 copy-start.9
  40.2 0.0 collective-permute-done.4.refs_9_
  40.2 0.0 copy-start.10
  40.2 0.0 collective-permute-done.5.refs_10_
  40.2 0.0 copy-start.11
  40.2 0.0 collective-permute-done.6.refs_11_
  40.2 0.0 copy-start.12
  40.2 6.3 %all-to-all-done.1 = bf16[32,32,128]{2,1,0:T(8,128)(2,1)S(1)} async-done(((bf16[32,32,128]{2,1,0:T(8,128)(2,1)}), bf16[32,32,128]{2,1,0:T(8,128)(2,1)S(1)}, u32[]{:S(2)}, u32[]{:S(2)}) %all-to-all-start.1) | async-done | bytes 262176 | tf_op jit(solution)/shard_map/all_to_all | solution.py:446
  46.5 0.0 copy-done.9
  46.5 0.0 copy-done.10
  46.5 0.0 copy-done.11
  46.5 3.0 %outs.1 = (f32[8,8,128]{2,1,0:T(8,128)S(1)}, bf16[512,1024]{1,0:T(8,128)(2,1)S(1)}, bf16[512,1024]{1,0:T(8,128)(2,1)S(1)}, bf16[512,1024]{1,0:T(8,128)(2,1)S(1)}, bf16[4,64,1024]{2,1,0:T(8,128)(2,1)}) custom-call(f32[512,512]{1,0:T(8,128)} %get-tuple-element.28.refs_1_.refs_0_, f32[512,512]{1,0:T(8,128)} %get-tuple-element.33.refs_1_, ...), custom_call_target="tpu_custom_call" | custom-call | flops 134217728 | bytes 5242880 | tf_op jit(solution)/shard_map/outs/pallas_call | solution.py:509
  49.6 0.1 collective-permute-start.7
  49.7 7.8 %all_to_all.25.sums_ref = f32[8,8,128]{2,1,0:T(8,128)S(1)} all-to-all(f32[8,8,128]{2,1,0:T(8,128)S(1)} %get-tuple-element.34), channel_id=1, replica_groups=mesh['seq'=32,'head'=8] {'head'}, dimensions={0} | all-to-all | bytes 65536 | tf_op jit(solution)/shard_map/all_to_all | solution.py:519
  57.5 0.0 collective-permute-done.7.got_any
  57.5 2.8 %grads.1 = (bf16[8,128,128]{2,1,0:T(8,128)(2,1)}, bf16[512,1024]{1,0:T(8,128)(2,1)}, bf16[2,64,1024]{2,1,0:T(8,128)(2,1)}, bf16[2,64,1024]{2,1,0:T(8,128)(2,1)},...) custom-call(f32[8,8,128]{2,1,0:T(8,128)S(1)} %all_to_all.25.sums_ref, ...), custom_call_target="tpu_custom_call" | custom-call | flops 134217728 | bytes 4194304 | tf_op jit(solution)/shard_map/grads/pallas_call | solution.py:522
  60.3 4.8 %all-to-all-start.3 = ((bf16[32,32,128]{2,1,0:T(8,128)(2,1)}), bf16[32,32,128]{2,1,0:T(8,128)(2,1)S(1)}, u32[]{:S(2)}, u32[]{:S(2)}) async-start(bf16[32,32,128]{2,1,0:T(8,128)(2,1)} %bitcast.3), calls=%async_computation.3 | async-start | bytes 524288 | tf_op jit(solution)/shard_map/all_to_all | solution.py:446
  65.1 0.6 collective-permute-start.8
  65.7 2.1 %collective-permute-start.9 = (bf16[2,64,1024]{2,1,0:T(8,128)(2,1)}, bf16[2,64,1024]{2,1,0:T(8,128)(2,1)S(1)}, u32[]{:S(2)}, u32[]{:S(2)}) collective-permute-start(bf16[2,64,1024]{2,1,0:T(8,128)(2,1)} %get-tuple-element.50), channel_id=1, source_target_pairs={{0,4},{1,5},{2,6},{3,7},{4,0},{5,1},{6,2},{7,3},{8,12},{9,13},{10,... | collective-permute-start | bytes 786440 | tf_op jit(solution)/shard_map/ppermute | solution.py:54
  67.8 1.1 %collective-permute-start.10 = (bf16[2,64,1024]{2,1,0:T(8,128)(2,1)}, bf16[2,64,1024]{2,1,0:T(8,128)(2,1)S(1)}, u32[]{:S(2)}, u32[]{:S(2)}) collective-permute-start(bf16[2,64,1024]{2,1,0:T(8,128)(2,1)} %get-tuple-element.51), channel_id=1, source_target_pairs={{0,6},{1,7},{2,0},{3,1},{4,2},{5,3},{6,4},{7,5},{8,14},{9,15},{10,... | collective-permute-start | bytes 786440 | tf_op jit(solution)/shard_map/ppermute | solution.py:54
  68.9 6.6 %backs.1 = (bf16[512,1024]{1,0:T(8,128)(2,1)}, bf16[512,1024]{1,0:T(8,128)(2,1)}, bf16[512,1024]{1,0:T(8,128)(2,1)}) custom-call(bf16[512,1024]{1,0:T(8,128)(2,1)} %q_hbm.5, bf16[512,1024]{1,0:T(8,128)(2,1)} %k_ref.1, bf16[512,1024]{1,0:T(8,128)(2,1)} %v_ref.1, bf16[512,1024]{1,0:T(8,128)(2,1)} %get-tuple-element.39.do_hbm, ...), custom_call_target="tpu_custom_call" | custom-call | flops 1610612736 | bytes 10485760 | tf_op jit(solution)/shard_map/backs/pallas_call | solution.py:535
  75.5 1.8 %all-to-all-done.3.x_ref = bf16[32,32,128]{2,1,0:T(8,128)(2,1)S(1)} async-done(((bf16[32,32,128]{2,1,0:T(8,128)(2,1)}), bf16[32,32,128]{2,1,0:T(8,128)(2,1)S(1)}, u32[]{:S(2)}, u32[]{:S(2)}) %all-to-all-start.3) | async-done | bytes 262176 | tf_op jit(solution)/shard_map/all_to_all | solution.py:446
  77.3 0.7 running.3
  78.0 8.0 %all-to-all-start.4 = ((bf16[32,32,128]{2,1,0:T(8,128)(2,1)}), bf16[32,32,128]{2,1,0:T(8,128)(2,1)S(1)}, u32[]{:S(2)}, u32[]{:S(2)}) async-start(bf16[32,32,128]{2,1,0:T(8,128)(2,1)} %running.3), calls=%async_computation.4 | async-start | bytes 524288 | tf_op jit(solution)/shard_map/all_to_all | solution.py:446
  86.0 0.0 collective-permute-done.8.refs_1_
  86.0 0.0 collective-permute-done.9.refs_2_
  86.0 0.0 collective-permute-done.10.refs_3_
  86.0 0.0 copy-start
  86.1 0.0 copy-start.1
  86.1 4.1 %gates.1 = bf16[64,8192]{1,0:T(8,128)(2,1)} custom-call(bf16[2,64,1024]{2,1,0:T(8,128)(2,1)} %get-tuple-element.48.refs_0_, bf16[2,64,1024]{2,1,0:T(8,128)(2,1)S(1)} %collective-permute-done.8.refs_1_, bf16[2,64,1024]{2,1,0:T(8,128)(2,1)S(1)} %collective-permute-done.9.refs_2_, bf16[2,64,1024]{2,1,0:T(8,128)(2,1)S(1)} %collective-permute-done.10.refs_3_, ...), custom_call_target="tpu_custom_call" | custom-call | flops 16106127360 | bytes 104857600 | tf_op jit(solution)/shard_map/gates/pallas_call | solution.py:551
  90.2 6.9 %all-to-all-done.4 = bf16[32,32,128]{2,1,0:T(8,128)(2,1)S(1)} async-done(((bf16[32,32,128]{2,1,0:T(8,128)(2,1)}), bf16[32,32,128]{2,1,0:T(8,128)(2,1)S(1)}, u32[]{:S(2)}, u32[]{:S(2)}) %all-to-all-start.4) | async-done | bytes 262176 | tf_op jit(solution)/shard_map/all_to_all | solution.py:446
  97.1 0.0 copy-done
  97.1 3.3 %last.1 = (bf16[512,1024]{1,0:T(8,128)(2,1)}, bf16[512,1024]{1,0:T(8,128)(2,1)}) custom-call(bf16[512,1024]{1,0:T(8,128)(2,1)} %get-tuple-element.43.refs_0_.ak_hbm, bf16[512,1024]{1,0:T(8,128)(2,1)} %get-tuple-element.44.av_hbm, bf16[512,1024]{1,0:T(8,128)(2,1)S(1)} %copy-done, bf16[512,1024]{1,0:T(8,128)(2,1)S(1)} %copy-done.1, ...), custom_call_target="tpu_custom_call" | custom-call | flops 268435456 | bytes 8388608 | tf_op jit(solution)/shard_map/last/pallas_call | solution.py:563
  (4 shorter events, 0.0 us)
Async XLA Ops:
  0.6 14.6 %copy-start.3 = (bf16[64,8192]{1,0:T(8,128)(2,1)S(1)}, bf16[64,8192]{1,0:T(8,128)(2,1)}, u32[]{:S(2)}) copy-start(bf16[64,8192]{1,0:T(8,128)(2,1)} %refs_5_.1) | copy-start | bytes 3145732
  0.6 14.6 %copy-start.2 = (bf16[64,8192]{1,0:T(8,128)(2,1)S(1)}, bf16[64,8192]{1,0:T(8,128)(2,1)}, u32[]{:S(2)}) copy-start(bf16[64,8192]{1,0:T(8,128)(2,1)} %refs_4_.1) | copy-start | bytes 3145732
  0.7 14.6 %copy-start.5 = (f32[8192]{0:T(1024)S(1)}, f32[8192]{0:T(1024)}, u32[]{:S(2)}) copy-start(f32[8192]{0:T(1024)} %param.10) | copy-start | bytes 98308
  3.8 23.7 %all-to-all-start = ((bf16[32,32,128]{2,1,0:T(8,128)(2,1)}), bf16[32,32,128]{2,1,0:T(8,128)(2,1)S(1)}, u32[]{:S(2)}, u32[]{:S(2)}) async-start(bf16[32,32,128]{2,1,0:T(8,128)(2,1)} %bitcast), calls=%async_computation | async-start | bytes 524288 | tf_op jit(solution)/shard_map/all_to_all | solution.py:446
  15.8 19.6 %copy-start.4 = (bf16[2,64,1024]{2,1,0:T(8,128)(2,1)}, bf16[2,64,1024]{2,1,0:T(8,128)(2,1)S(1)}, u32[]{:S(2)}) copy-start(bf16[2,64,1024]{2,1,0:T(8,128)(2,1)S(1)} %get-tuple-element.29.refs_0_.refs_4_) | copy-start | bytes 786436
  15.8 19.7 %collective-permute-start = (bf16[2,64,1024]{2,1,0:T(8,128)(2,1)S(1)}, bf16[2,64,1024]{2,1,0:T(8,128)(2,1)S(1)}, u32[]{:S(2)}, u32[]{:S(2)}) collective-permute-start(bf16[2,64,1024]{2,1,0:T(8,128)(2,1)S(1)} %get-tuple-element.30), channel_id=1, source_target_pairs={{0,2},{1,3},{2,4},{3,5},{4,6},{5,7},{6,0},{7,1},{8,10},{9,11},{10,... | collective-permute-start | bytes 786440 | tf_op jit(solution)/shard_map/ppermute | solution.py:54
  17.4 18.6 %collective-permute-start.1 = (bf16[2,64,1024]{2,1,0:T(8,128)(2,1)S(1)}, bf16[2,64,1024]{2,1,0:T(8,128)(2,1)S(1)}, u32[]{:S(2)}, u32[]{:S(2)}) collective-permute-start(bf16[2,64,1024]{2,1,0:T(8,128)(2,1)S(1)} %get-tuple-element.31), channel_id=1, source_target_pairs={{0,4},{1,5},{2,6},{3,7},{4,0},{5,1},{6,2},{7,3},{8,12},{9,13},{10,... | collective-permute-start | bytes 786440 | tf_op jit(solution)/shard_map/ppermute | solution.py:54
  20.1 16.0 %collective-permute-start.2 = (bf16[2,64,1024]{2,1,0:T(8,128)(2,1)S(1)}, bf16[2,64,1024]{2,1,0:T(8,128)(2,1)S(1)}, u32[]{:S(2)}, u32[]{:S(2)}) collective-permute-start(bf16[2,64,1024]{2,1,0:T(8,128)(2,1)S(1)} %get-tuple-element.32), channel_id=1, source_target_pairs={{0,6},{1,7},{2,0},{3,1},{4,2},{5,3},{6,4},{7,5},{8,14},{9,15},{10,... | collective-permute-start | bytes 786440 | tf_op jit(solution)/shard_map/ppermute | solution.py:54
  28.3 18.3 %all-to-all-start.1 = ((bf16[32,32,128]{2,1,0:T(8,128)(2,1)}), bf16[32,32,128]{2,1,0:T(8,128)(2,1)S(1)}, u32[]{:S(2)}, u32[]{:S(2)}) async-start(bf16[32,32,128]{2,1,0:T(8,128)(2,1)} %running.2.refs_0_), calls=%async_computation.1 | async-start | bytes 524288 | tf_op jit(solution)/shard_map/all_to_all | solution.py:446
  35.4 4.8 %collective-permute-start.3 = (bf16[2,64,1024]{2,1,0:T(8,128)(2,1)S(1)}, bf16[2,64,1024]{2,1,0:T(8,128)(2,1)S(1)}, u32[]{:S(2)}, u32[]{:S(2)}) collective-permute-start(bf16[2,64,1024]{2,1,0:T(8,128)(2,1)S(1)} %get-tuple-element.29.refs_0_.refs_4_), channel_id=1, source_target_pairs={{0,1},{1,0},{2,3},{3,2},{4,5},{5,4},{6,7},{7,6},{8,9},{9,8},{10,11... | collective-permute-start | bytes 786440 | tf_op jit(solution)/shard_map/ppermute | solution.py:62
  35.5 1.0 %copy-start.6 = (bf16[2,64,1024]{2,1,0:T(8,128)(2,1)}, bf16[2,64,1024]{2,1,0:T(8,128)(2,1)S(1)}, u32[]{:S(2)}) copy-start(bf16[2,64,1024]{2,1,0:T(8,128)(2,1)S(1)} %collective-permute-done.refs_1_.refs_5_) | copy-start | bytes 786436
  35.5 4.7 %collective-permute-start.4 = (bf16[2,64,1024]{2,1,0:T(8,128)(2,1)S(1)}, bf16[2,64,1024]{2,1,0:T(8,128)(2,1)S(1)}, u32[]{:S(2)}, u32[]{:S(2)}) collective-permute-start(bf16[2,64,1024]{2,1,0:T(8,128)(2,1)S(1)} %collective-permute-done.refs_1_.refs_5_), channel_id=1, source_target_pairs={{0,1},{1,0},{2,3},{3,2},{4,5},{5,4},{6,7},{7,6},{8,9},{9,8},{10,11... | collective-permute-start | bytes 786440 | tf_op jit(solution)/shard_map/ppermute | solution.py:62
  36.0 0.7 copy-start.7
  36.0 4.2 %collective-permute-start.5 = (bf16[2,64,1024]{2,1,0:T(8,128)(2,1)S(1)}, bf16[2,64,1024]{2,1,0:T(8,128)(2,1)S(1)}, u32[]{:S(2)}, u32[]{:S(2)}) collective-permute-start(bf16[2,64,1024]{2,1,0:T(8,128)(2,1)S(1)} %collective-permute-done.1.refs_2_.refs_6_), channel_id=1, source_target_pairs={{0,1},{1,0},{2,3},{3,2},{4,5},{5,4},{6,7},{7,6},{8,9},{9,8},{10,11... | collective-permute-start | bytes 786440 | tf_op jit(solution)/shard_map/ppermute | solution.py:62
  36.1 0.7 copy-start.8
  36.1 4.1 %collective-permute-start.6 = (bf16[2,64,1024]{2,1,0:T(8,128)(2,1)S(1)}, bf16[2,64,1024]{2,1,0:T(8,128)(2,1)S(1)}, u32[]{:S(2)}, u32[]{:S(2)}) collective-permute-start(bf16[2,64,1024]{2,1,0:T(8,128)(2,1)S(1)} %collective-permute-done.2.refs_3_.refs_7_), channel_id=1, source_target_pairs={{0,1},{1,0},{2,3},{3,2},{4,5},{5,4},{6,7},{7,6},{8,9},{9,8},{10,11... | collective-permute-start | bytes 786440 | tf_op jit(solution)/shard_map/ppermute | solution.py:62
  40.2 6.4 %copy-start.9 = (bf16[2,64,1024]{2,1,0:T(8,128)(2,1)}, bf16[2,64,1024]{2,1,0:T(8,128)(2,1)S(1)}, u32[]{:S(2)}) copy-start(bf16[2,64,1024]{2,1,0:T(8,128)(2,1)S(1)} %collective-permute-done.3.refs_8_) | copy-start | bytes 786436
  40.2 6.3 %copy-start.10 = (bf16[2,64,1024]{2,1,0:T(8,128)(2,1)}, bf16[2,64,1024]{2,1,0:T(8,128)(2,1)S(1)}, u32[]{:S(2)}) copy-start(bf16[2,64,1024]{2,1,0:T(8,128)(2,1)S(1)} %collective-permute-done.4.refs_9_) | copy-start | bytes 786436
  40.2 6.3 %copy-start.11 = (bf16[2,64,1024]{2,1,0:T(8,128)(2,1)}, bf16[2,64,1024]{2,1,0:T(8,128)(2,1)S(1)}, u32[]{:S(2)}) copy-start(bf16[2,64,1024]{2,1,0:T(8,128)(2,1)S(1)} %collective-permute-done.5.refs_10_) | copy-start | bytes 786436
  40.2 6.3 %copy-start.12 = (bf16[2,64,1024]{2,1,0:T(8,128)(2,1)}, bf16[2,64,1024]{2,1,0:T(8,128)(2,1)S(1)}, u32[]{:S(2)}) copy-start(bf16[2,64,1024]{2,1,0:T(8,128)(2,1)S(1)} %collective-permute-done.6.refs_11_) | copy-start | bytes 786436
  49.6 7.9 %collective-permute-start.7 = (bf16[4,64,1024]{2,1,0:T(8,128)(2,1)}, bf16[4,64,1024]{2,1,0:T(8,128)(2,1)S(1)}, u32[]{:S(2)}, u32[]{:S(2)}) collective-permute-start(bf16[4,64,1024]{2,1,0:T(8,128)(2,1)} %get-tuple-element.38), channel_id=1, source_target_pairs={{0,1},{1,0},{2,3},{3,2},{4,5},{5,4},{6,7},{7,6},{8,9},{9,8},{10,11... | collective-permute-start | bytes 1572872 | tf_op jit(solution)/shard_map/ppermute | solution.py:521
  60.3 17.0 %all-to-all-start.3 = ((bf16[32,32,128]{2,1,0:T(8,128)(2,1)}), bf16[32,32,128]{2,1,0:T(8,128)(2,1)S(1)}, u32[]{:S(2)}, u32[]{:S(2)}) async-start(bf16[32,32,128]{2,1,0:T(8,128)(2,1)} %bitcast.3), calls=%async_computation.3 | async-start | bytes 524288 | tf_op jit(solution)/shard_map/all_to_all | solution.py:446
  65.1 20.9 %collective-permute-start.8 = (bf16[2,64,1024]{2,1,0:T(8,128)(2,1)}, bf16[2,64,1024]{2,1,0:T(8,128)(2,1)S(1)}, u32[]{:S(2)}, u32[]{:S(2)}) collective-permute-start(bf16[2,64,1024]{2,1,0:T(8,128)(2,1)} %get-tuple-element.49), channel_id=1, source_target_pairs={{0,2},{1,3},{2,4},{3,5},{4,6},{5,7},{6,0},{7,1},{8,10},{9,11},{10,... | collective-permute-start | bytes 786440 | tf_op jit(solution)/shard_map/ppermute | solution.py:54
  65.7 20.3 %collective-permute-start.9 = (bf16[2,64,1024]{2,1,0:T(8,128)(2,1)}, bf16[2,64,1024]{2,1,0:T(8,128)(2,1)S(1)}, u32[]{:S(2)}, u32[]{:S(2)}) collective-permute-start(bf16[2,64,1024]{2,1,0:T(8,128)(2,1)} %get-tuple-element.50), channel_id=1, source_target_pairs={{0,4},{1,5},{2,6},{3,7},{4,0},{5,1},{6,2},{7,3},{8,12},{9,13},{10,... | collective-permute-start | bytes 786440 | tf_op jit(solution)/shard_map/ppermute | solution.py:54
  67.8 18.3 %collective-permute-start.10 = (bf16[2,64,1024]{2,1,0:T(8,128)(2,1)}, bf16[2,64,1024]{2,1,0:T(8,128)(2,1)S(1)}, u32[]{:S(2)}, u32[]{:S(2)}) collective-permute-start(bf16[2,64,1024]{2,1,0:T(8,128)(2,1)} %get-tuple-element.51), channel_id=1, source_target_pairs={{0,6},{1,7},{2,0},{3,1},{4,2},{5,3},{6,4},{7,5},{8,14},{9,15},{10,... | collective-permute-start | bytes 786440 | tf_op jit(solution)/shard_map/ppermute | solution.py:54
  78.0 19.1 %all-to-all-start.4 = ((bf16[32,32,128]{2,1,0:T(8,128)(2,1)}), bf16[32,32,128]{2,1,0:T(8,128)(2,1)S(1)}, u32[]{:S(2)}, u32[]{:S(2)}) async-start(bf16[32,32,128]{2,1,0:T(8,128)(2,1)} %running.3), calls=%async_computation.4 | async-start | bytes 524288 | tf_op jit(solution)/shard_map/all_to_all | solution.py:446
  86.0 11.1 %copy-start = (bf16[512,1024]{1,0:T(8,128)(2,1)S(1)}, bf16[512,1024]{1,0:T(8,128)(2,1)}, u32[]{:S(2)}) copy-start(bf16[512,1024]{1,0:T(8,128)(2,1)} %k_ref.1) | copy-start | bytes 3145732
  86.1 11.1 %copy-start.1 = (bf16[512,1024]{1,0:T(8,128)(2,1)S(1)}, bf16[512,1024]{1,0:T(8,128)(2,1)}, u32[]{:S(2)}) copy-start(bf16[512,1024]{1,0:T(8,128)(2,1)} %v_ref.1) | copy-start | bytes 3145732

commit v6 on v5

--- a/solution.py
+++ b/solution.py
@@ -287,14 +287,15 @@
     wait_all(copies + ready)
 
 
-def back_kernel(
-    q_hbm, k_hbm, v_hbm, do_hbm, t0_hbm, t1_hbm, p_ref, *refs
-):
+def back_kernel(first, q_hbm, k_hbm, v_hbm, do_hbm, t_hbm, p_ref, *refs):
     ak_hbm, av_hbm, gq_hbm, q_ref, k_ref, v_ref, do_ref, t_ref = refs[-13:-5]
     ak_ref, av_ref, gq_ref, sems, out_sems = refs[-5:]
     t, own = q_ref.shape
     half = t // 2
     n = own // (2 * HEAD_DIM)
+    q_hbm, k_hbm, v_hbm, do_hbm, gq_hbm = [
+        x.at[:, pl.ds(first * HEAD_DIM, own)] for x in (q_hbm, k_hbm, v_hbm, do_hbm, gq_hbm)
+    ]
     ins = [
         by_pairs(src, dst, sems, n * j)
         for j, (src, dst) in enumerate(
@@ -304,10 +305,9 @@
     ins.append(
         [
             pltpu.make_async_copy(
-                src.at[pl.ds(2 * i, 2)], t_ref.at[pl.ds(j * n + 2 * i, 2)], sems.at[4 * n + j * n // 2 + i]
+                t_hbm.at[pl.ds(2 * i, 2)], t_ref.at[pl.ds(2 * i, 2)], sems.at[4 * n + i]
             )
-            for j, src in enumerate((t0_hbm, t1_hbm))
-            for i in range(n // 2)
+            for i in range(n)
         ]
     )
     for i in range(n):
@@ -338,7 +338,7 @@
             av_ref[two, cols] = mm(dot[:, two], s1).astype(BF16).T
         for h, cols, g0, g1, g2 in pair:
             qt, kt, dot = q_ref[:, cols].T, k_ref[:, cols].T, do_ref[:, cols].T
-            base = mm(p_ref[h], dot)
+            base = mm(p_ref[first + h], dot)
             gq_ref[one, cols] = (mm_bt(kt[:, one], g0) + base[:, one]).astype(BF16).T
             gq = mm_bt(kt, jnp.concatenate([g2, g1], axis=1)) + base[:, two]
             gq_ref[two, cols] = gq.astype(BF16).T
@@ -352,18 +352,19 @@
 
 
 def last_kernel(
-    ak_hbm, av_hbm, k_ref, v_ref, s_ref, gk_hbm, gv_hbm,
+    ak0_hbm, ak1_hbm, av0_hbm, av1_hbm, k_ref, v_ref, s_ref, gk_hbm, gv_hbm,
     ak_ref, av_ref, gk_ref, gv_ref, sems, out_sems,
 ):
     d = HEAD_DIM
     t, own = k_ref.shape
     n = own // (2 * d)
-    ins = [
-        by_pairs(src, dst, sems, n * j)
-        for j, (src, dst) in enumerate(
-            ((av_hbm, av_ref), (ak_hbm, ak_ref))
-        )
-    ]
+    ins = []
+    for j, (dst, srcs) in enumerate(((av_ref, (av0_hbm, av1_hbm)), (ak_ref, (ak0_hbm, ak1_hbm)))):
+        parts_of = []
+        for m, src in enumerate(srcs):
+            part = dst.at[:, pl.ds(m * own // 2, own // 2)]
+            parts_of += by_pairs(src, part, sems, n * j + m * n // 2)
+        ins.append(parts_of)
     for i in range(n):
         for c in ins:
             c[i].start()
@@ -532,19 +533,29 @@
     )(sums, in_vmem(queries), in_vmem(weighted), in_vmem(out), got)
     received = exchange(states)
 
-    part_key, part_value, grad_query = pl.pallas_call(
-        back_kernel,
-        out_shape=[pltpu.HBM((t, own), BF16)] * 2 + [sds((t, own), BF16)],
-        in_specs=[anywhere] * 6 + [whole],
-        out_specs=[anywhere] * 3,
-        scratch_shapes=[full] * 4 + [pltpu.VMEM((heads,) + tiles[1:], BF16)] + [full] * 3
-        + [dma(5 * pairs), dma(3 * pairs)],
-        compiler_params=params(),
-        cost_estimate=cost(3 * large, 20 * t * own),
-        name="backs",
-    )(query, key_in, value, in_hbm(grad_attn), scores0, scores1, prefix)
-    part_key, part_value = in_hbm(part_key), in_hbm(part_value)
-    suffix = exchange(running(received, True, part_key)).reshape(heads, d, d)
+    grad_attn = in_hbm(grad_attn)
+
+    def back(first, scores, into, *after):
+        part = pltpu.VMEM((t, own // 2), BF16)
+        return pl.pallas_call(
+            functools.partial(back_kernel, first),
+            out_shape=[pltpu.HBM((t, own // 2), BF16)] * 2 + [sds((t, own), BF16)],
+            in_specs=[anywhere] * 5 + [whole] + [anywhere] * (len(into) + len(after)),
+            out_specs=[anywhere] * 3,
+            scratch_shapes=[part] * 4 + [pltpu.VMEM(tiles, BF16)] + [part] * 3
+            + [dma(5 * pairs // 2), dma(3 * pairs // 2)],
+            input_output_aliases={6: 2} if into else {},
+            compiler_params=params(),
+            cost_estimate=cost(2 * large, 10 * t * own),
+            name="backs",
+        )(query, key_in, value, grad_attn, scores, prefix, *into, *after)
+
+    key0, value0, grad_query = back(0, scores0, [])
+    key0, value0 = in_hbm(key0), in_hbm(value0)
+    summed = running(received, True, key0)
+    suffix = exchange(summed).reshape(heads, d, d)
+    key1, value1, grad_query = back(some, scores1, [grad_query], in_hbm(summed))
+    key1, value1 = in_hbm(key1), in_hbm(value1)
 
     token_rows = across(bundles)
     strip = pltpu.VMEM((rows, width), BF16)
@@ -563,13 +574,13 @@
     grad_key, grad_value = pl.pallas_call(
         last_kernel,
         out_shape=[sds((t, own), BF16), sds((t, own), BF16)],
-        in_specs=[anywhere] * 2 + [whole] * 3,
+        in_specs=[anywhere] * 4 + [whole] * 3,
         out_specs=[anywhere] * 2,
         scratch_shapes=[full] * 4 + [dma(2 * pairs), dma(2 * pairs)],
         compiler_params=params(),
         cost_estimate=cost(2 * small, 16 * t * own),
         name="last",
-    )(part_key, part_value, keys, values, suffix)
+    )(key0, key1, value0, value1, keys, values, suffix)
     return grad_query, grad_key, grad_value, grad_gate
 
 

time: 101 us -> 99 us (0.980)
  Pallas kernels: 31.7 us -> 33.9 us
  waiting for transfers between devices: 17.7 us -> 15.5 us
  starting transfers between devices: 41.9 us -> 39.7 us
    pallas_call x1 -> x2, Pallas kernels: 6.59 us -> 8.93 us  [back(): pl.pallas_call(functools.partial(back_kernel, first), out_shape=[pltpu.HB...]
    all_to_all x4, waiting for transfers between devices: 17.7 us -> 15.5 us  [exchange(): return lax.all_to_all(states.reshape(piece), 'seq', 0, 0, tiled=True)]
    all_to_all x4, starting transfers between devices: 31.2 us -> 29 us  [exchange(): return lax.all_to_all(states.reshape(piece), 'seq', 0, 0, tiled=True)]
  transfers between devices with their start and end apart: 15 -> 15, of which waited for: 4 -> 4; matrix products, arithmetic and copies ran while one was open for 0% -> 0% of each run, Pallas kernels for 19% -> 22%
where the time goes in v6:
time: 99 us; the launch traced here: 98.5 us
  starting transfers between devices  39.7 us (40%)
  Pallas kernels  33.9 us (34%)
  waiting for transfers between devices  15.5 us (16%)
  blocking collectives  7.82 us (8%)
  between operations  1.11 us (1%)
    all_to_all x4, starting transfers between devices, exchange(): return lax.all_to_all(states.reshape(piece), 'seq', 0, 0, tiled=True)  29 us
    all_to_all x4, waiting for transfers between devices, exchange(): return lax.all_to_all(states.reshape(piece), 'seq', 0, 0, tiled=True)  15.5 us
    ppermute x6, starting transfers between devices, across(): lax.ppermute(bundles[dx], 'head', [(i, (i + 2 * dx) % n) for i in range(n)])  9.53 us
    pallas_call x2, Pallas kernels, back(): pl.pallas_call(functools.partial(back_kernel, first), out_shape=[pltpu.HB...  8.93 us
    all_to_all x1, blocking collectives, on_device(): sums = lax.all_to_all(sums, 'head', 0, 0, tiled=True)  7.82 us
    pallas_call x2, Pallas kernels, intra(): pl.pallas_call(functools.partial(intra_kernel, first), out_shape=[pltpu.H...  6.61 us
    pallas_call x1, Pallas kernels, on_device(): pl.pallas_call(functools.partial(gate_kernel, n_head), out_shape=sds((row...  4.01 us
    pallas_call x1, Pallas kernels, on_device(): pl.pallas_call(last_kernel, out_shape=[sds((t, own), BF16), sds((t, own),...  3.34 us
  transfers between devices with their start and end apart: 15, of which 4 were waited for; matrix products, arithmetic and copies ran while one was open for 0% of the time, Pallas kernels for 22%

profile of v6, /device:TPU:32, one launch (start us, length us, event | category | flops | bytes accessed | tf_op | source)
XLA Modules:
  0.0 98.5 jit_solution(14911268921273110354)
XLA Ops:
  0.6 0.0 copy-start.3
  0.6 0.0 copy-start.2
  0.7 0.0 copy-start.5
  0.7 3.2 %states.1.refs_0_ = bf16[8,128,128]{2,1,0:T(8,128)(2,1)} custom-call(bf16[512,1024]{1,0:T(8,128)(2,1)} %k_ref.1, bf16[512,1024]{1,0:T(8,128)(2,1)} %v_ref.1), custom_call_target="tpu_custom_call" | custom-call | flops 268435456 | bytes 2097152 | tf_op jit(solution)/shard_map/states/pallas_call | solution.py:462
  3.8 11.4 %all-to-all-start = ((bf16[32,32,128]{2,1,0:T(8,128)(2,1)}), bf16[32,32,128]{2,1,0:T(8,128)(2,1)S(1)}, u32[]{:S(2)}, u32[]{:S(2)}) async-start(bf16[32,32,128]{2,1,0:T(8,128)(2,1)} %bitcast), calls=%async_computation | async-start | bytes 524288 | tf_op jit(solution)/shard_map/all_to_all | solution.py:447
  15.2 0.0 copy-done.3
  15.2 0.0 copy-done.2
  15.2 0.0 copy-done.5
  15.3 0.5 weigh.1
  15.8 0.0 copy-start.4
  15.8 1.6 %collective-permute-start = (bf16[2,64,1024]{2,1,0:T(8,128)(2,1)S(1)}, bf16[2,64,1024]{2,1,0:T(8,128)(2,1)S(1)}, u32[]{:S(2)}, u32[]{:S(2)}) collective-permute-start(bf16[2,64,1024]{2,1,0:T(8,128)(2,1)S(1)} %get-tuple-element.33), channel_id=1, source_target_pairs={{0,2},{1,3},{2,4},{3,5},{4,6},{5,7},{6,0},{7,1},{8,10},{9,11},{10,... | collective-permute-start | bytes 786440 | tf_op jit(solution)/shard_map/ppermute | solution.py:54
  17.4 2.7 %collective-permute-start.1 = (bf16[2,64,1024]{2,1,0:T(8,128)(2,1)S(1)}, bf16[2,64,1024]{2,1,0:T(8,128)(2,1)S(1)}, u32[]{:S(2)}, u32[]{:S(2)}) collective-permute-start(bf16[2,64,1024]{2,1,0:T(8,128)(2,1)S(1)} %get-tuple-element.34), channel_id=1, source_target_pairs={{0,4},{1,5},{2,6},{3,7},{4,0},{5,1},{6,2},{7,3},{8,12},{9,13},{10,... | collective-permute-start | bytes 786440 | tf_op jit(solution)/shard_map/ppermute | solution.py:54
  20.1 1.4 %collective-permute-start.2 = (bf16[2,64,1024]{2,1,0:T(8,128)(2,1)S(1)}, bf16[2,64,1024]{2,1,0:T(8,128)(2,1)S(1)}, u32[]{:S(2)}, u32[]{:S(2)}) collective-permute-start(bf16[2,64,1024]{2,1,0:T(8,128)(2,1)S(1)} %get-tuple-element.35), channel_id=1, source_target_pairs={{0,6},{1,7},{2,0},{3,1},{4,2},{5,3},{6,4},{7,5},{8,14},{9,15},{10,... | collective-permute-start | bytes 786440 | tf_op jit(solution)/shard_map/ppermute | solution.py:54
  21.5 3.3 %intra.2 = (f32[512,512]{1,0:T(8,128)}, bf16[4,3,256,256]{3,2,1,0:T(8,128)(2,1)}) custom-call(bf16[512,1024]{1,0:T(8,128)(2,1)} %q_hbm.7, bf16[512,1024]{1,0:T(8,128)(2,1)} %k_ref.1, bf16[512,1024]{1,0:T(8,128)(2,1)} %v_ref.1, bf16[8,128,128]{2,1,0:T(8,128)(2,1)} %states.1.refs_0_), custom_call_target="tpu_custom_call" | custom-call | flops 536870912 | bytes 4194304 | tf_op jit(solution)/shard_map/intra/pallas_call | solution.py:491
  24.9 2.7 %all-to-all-done.x_ref = bf16[32,32,128]{2,1,0:T(8,128)(2,1)S(1)} async-done(((bf16[32,32,128]{2,1,0:T(8,128)(2,1)}), bf16[32,32,128]{2,1,0:T(8,128)(2,1)S(1)}, u32[]{:S(2)}, u32[]{:S(2)}) %all-to-all-start) | async-done | bytes 262176 | tf_op jit(solution)/shard_map/all_to_all | solution.py:447
  27.5 0.7 running.2.refs_0_
  28.3 7.1 %all-to-all-start.1 = ((bf16[32,32,128]{2,1,0:T(8,128)(2,1)}), bf16[32,32,128]{2,1,0:T(8,128)(2,1)S(1)}, u32[]{:S(2)}, u32[]{:S(2)}) async-start(bf16[32,32,128]{2,1,0:T(8,128)(2,1)} %running.2.refs_0_), calls=%async_computation.1 | async-start | bytes 524288 | tf_op jit(solution)/shard_map/all_to_all | solution.py:447
  35.4 0.0 copy-done.4
  35.4 0.1 collective-permute-start.3
  35.5 0.0 collective-permute-done.refs_1_.refs_5_
  35.5 0.0 copy-start.6
  35.5 0.5 collective-permute-start.4
  36.0 0.0 collective-permute-done.1.refs_2_.refs_6_
  36.0 0.1 collective-permute-start.5
  36.1 0.0 collective-permute-done.2.refs_3_.refs_7_
  36.1 0.4 collective-permute-start.6
  36.5 0.0 copy-done.6
  36.5 0.2 copy-done.7
  36.7 0.1 copy-done.8
  36.8 3.3 %intra.3 = (f32[512,512]{1,0:T(8,128)}, bf16[4,3,256,256]{3,2,1,0:T(8,128)(2,1)}) custom-call(bf16[512,1024]{1,0:T(8,128)(2,1)} %q_hbm.7, bf16[512,1024]{1,0:T(8,128)(2,1)} %k_ref.1, bf16[512,1024]{1,0:T(8,128)(2,1)} %v_ref.1, bf16[32,32,128]{2,1,0:T(8,128)(2,1)} %running.2.refs_0_, bf16[2,64,1024]{2,1,0:T(8,128)(2,1)} %copy-done.6, ...), custom_call_target="tpu_custom_call" | custom-call | flops 536870912 | bytes 4194304 | tf_op jit(solution)/shard_map/intra/pallas_call | solution.py:491
  40.2 0.0 collective-permute-done.3.refs_8_
  40.2 0.0 copy-start.9
  40.2 0.0 collective-permute-done.4.refs_9_
  40.2 0.0 copy-start.10
  40.2 0.0 collective-permute-done.5.refs_10_
  40.2 0.0 copy-start.11
  40.2 0.0 collective-permute-done.6.refs_11_
  40.2 0.0 copy-start.12
  40.2 6.3 %all-to-all-done.1 = bf16[32,32,128]{2,1,0:T(8,128)(2,1)S(1)} async-done(((bf16[32,32,128]{2,1,0:T(8,128)(2,1)}), bf16[32,32,128]{2,1,0:T(8,128)(2,1)S(1)}, u32[]{:S(2)}, u32[]{:S(2)}) %all-to-all-start.1) | async-done | bytes 262176 | tf_op jit(solution)/shard_map/all_to_all | solution.py:447
  46.5 0.0 copy-done.9
  46.5 0.0 copy-done.11
  46.5 3.0 %outs.1 = (f32[8,8,128]{2,1,0:T(8,128)S(1)}, bf16[512,1024]{1,0:T(8,128)(2,1)S(1)}, bf16[512,1024]{1,0:T(8,128)(2,1)S(1)}, bf16[512,1024]{1,0:T(8,128)(2,1)S(1)}, bf16[4,64,1024]{2,1,0:T(8,128)(2,1)}) custom-call(f32[512,512]{1,0:T(8,128)} %get-tuple-element.31.refs_1_.refs_0_, f32[512,512]{1,0:T(8,128)} %get-tuple-element.36.refs_1_, ...), custom_call_target="tpu_custom_call" | custom-call | flops 134217728 | bytes 5242880 | tf_op jit(solution)/shard_map/outs/pallas_call | solution.py:510
  49.6 0.1 collective-permute-start.7
  49.7 7.8 %all_to_all.25.sums_ref = f32[8,8,128]{2,1,0:T(8,128)S(1)} all-to-all(f32[8,8,128]{2,1,0:T(8,128)S(1)} %get-tuple-element.37), channel_id=1, replica_groups=mesh['seq'=32,'head'=8] {'head'}, dimensions={0} | all-to-all | bytes 65536 | tf_op jit(solution)/shard_map/all_to_all | solution.py:520
  57.5 0.0 collective-permute-done.7.got_any
  57.5 2.8 %grads.1 = (bf16[8,128,128]{2,1,0:T(8,128)(2,1)}, bf16[512,1024]{1,0:T(8,128)(2,1)}, bf16[2,64,1024]{2,1,0:T(8,128)(2,1)}, bf16[2,64,1024]{2,1,0:T(8,128)(2,1)},...) custom-call(f32[8,8,128]{2,1,0:T(8,128)S(1)} %all_to_all.25.sums_ref, ...), custom_call_target="tpu_custom_call" | custom-call | flops 134217728 | bytes 4194304 | tf_op jit(solution)/shard_map/grads/pallas_call | solution.py:523
  60.3 4.8 %all-to-all-start.3 = ((bf16[32,32,128]{2,1,0:T(8,128)(2,1)}), bf16[32,32,128]{2,1,0:T(8,128)(2,1)S(1)}, u32[]{:S(2)}, u32[]{:S(2)}) async-start(bf16[32,32,128]{2,1,0:T(8,128)(2,1)} %bitcast.3), calls=%async_computation.3 | async-start | bytes 524288 | tf_op jit(solution)/shard_map/all_to_all | solution.py:447
  65.1 0.6 collective-permute-start.8
  65.7 2.1 %collective-permute-start.9 = (bf16[2,64,1024]{2,1,0:T(8,128)(2,1)}, bf16[2,64,1024]{2,1,0:T(8,128)(2,1)S(1)}, u32[]{:S(2)}, u32[]{:S(2)}) collective-permute-start(bf16[2,64,1024]{2,1,0:T(8,128)(2,1)} %get-tuple-element.56), channel_id=1, source_target_pairs={{0,4},{1,5},{2,6},{3,7},{4,0},{5,1},{6,2},{7,3},{8,12},{9,13},{10,... | collective-permute-start | bytes 786440 | tf_op jit(solution)/shard_map/ppermute | solution.py:54
  67.8 1.1 %collective-permute-start.10 = (bf16[2,64,1024]{2,1,0:T(8,128)(2,1)}, bf16[2,64,1024]{2,1,0:T(8,128)(2,1)S(1)}, u32[]{:S(2)}, u32[]{:S(2)}) collective-permute-start(bf16[2,64,1024]{2,1,0:T(8,128)(2,1)} %get-tuple-element.57), channel_id=1, source_target_pairs={{0,6},{1,7},{2,0},{3,1},{4,2},{5,3},{6,4},{7,5},{8,14},{9,15},{10,... | collective-permute-start | bytes 786440 | tf_op jit(solution)/shard_map/ppermute | solution.py:54
  68.9 4.4 %backs.2 = (bf16[512,512]{1,0:T(8,128)(2,1)}, bf16[512,512]{1,0:T(8,128)(2,1)}, bf16[512,1024]{1,0:T(8,128)(2,1)}) custom-call(bf16[512,1024]{1,0:T(8,128)(2,1)} %q_hbm.7, bf16[512,1024]{1,0:T(8,128)(2,1)} %k_ref.1, bf16[512,1024]{1,0:T(8,128)(2,1)} %v_ref.1, bf16[512,1024]{1,0:T(8,128)(2,1)} %get-tuple-element.42.do_hbm, ...), custom_call_target="tpu_custom_call" | custom-call | flops 1073741824 | bytes 5242880 | tf_op jit(solution)/shard_map/backs/pallas_call | solution.py:540
  73.3 4.0 %all-to-all-done.3.x_ref = bf16[32,32,128]{2,1,0:T(8,128)(2,1)S(1)} async-done(((bf16[32,32,128]{2,1,0:T(8,128)(2,1)}), bf16[32,32,128]{2,1,0:T(8,128)(2,1)S(1)}, u32[]{:S(2)}, u32[]{:S(2)}) %all-to-all-start.3) | async-done | bytes 262176 | tf_op jit(solution)/shard_map/all_to_all | solution.py:447
  77.3 0.7 running.3.refs_1_
  78.1 5.8 %all-to-all-start.4 = ((bf16[32,32,128]{2,1,0:T(8,128)(2,1)}), bf16[32,32,128]{2,1,0:T(8,128)(2,1)S(1)}, u32[]{:S(2)}, u32[]{:S(2)}) async-start(bf16[32,32,128]{2,1,0:T(8,128)(2,1)} %running.3.refs_1_), calls=%async_computation.4 | async-start | bytes 524288 | tf_op jit(solution)/shard_map/all_to_all | solution.py:447
  83.8 0.0 collective-permute-done.8.refs_1_
  83.8 0.0 collective-permute-done.9.refs_2_
  83.8 0.0 collective-permute-done.10.refs_3_
  83.9 4.0 %gates.1 = bf16[64,8192]{1,0:T(8,128)(2,1)} custom-call(bf16[2,64,1024]{2,1,0:T(8,128)(2,1)} %get-tuple-element.54.refs_0_, bf16[2,64,1024]{2,1,0:T(8,128)(2,1)S(1)} %collective-permute-done.8.refs_1_, bf16[2,64,1024]{2,1,0:T(8,128)(2,1)S(1)} %collective-permute-done.9.refs_2_, bf16[2,64,1024]{2,1,0:T(8,128)(2,1)S(1)} %collective-permute-done.10.refs_3_, ...), custom_call_target="tpu_custom_call" | custom-call | flops 16106127360 | bytes 104857600 | tf_op jit(solution)/shard_map/gates/pallas_call | solution.py:562
  87.9 0.0 copy-start
  87.9 0.0 copy-start.1
  87.9 4.5 %backs.3 = (bf16[512,512]{1,0:T(8,128)(2,1)}, bf16[512,512]{1,0:T(8,128)(2,1)}, bf16[512,1024]{1,0:T(8,128)(2,1)}) custom-call(bf16[512,1024]{1,0:T(8,128)(2,1)} %q_hbm.7, bf16[512,1024]{1,0:T(8,128)(2,1)} %k_ref.1, bf16[512,1024]{1,0:T(8,128)(2,1)} %v_ref.1, bf16[512,1024]{1,0:T(8,128)(2,1)} %get-tuple-element.42.do_hbm, ...), custom_call_target="tpu_custom_call", output_to_operand_aliasing={{2}: (6, {})} | custom-call | flops 1073741824 | bytes 5242880 | tf_op jit(solution)/shard_map/backs/pallas_call | solution.py:540
  92.5 2.5 %all-to-all-done.4 = bf16[32,32,128]{2,1,0:T(8,128)(2,1)S(1)} async-done(((bf16[32,32,128]{2,1,0:T(8,128)(2,1)}), bf16[32,32,128]{2,1,0:T(8,128)(2,1)S(1)}, u32[]{:S(2)}, u32[]{:S(2)}) %all-to-all-start.4) | async-done | bytes 262176 | tf_op jit(solution)/shard_map/all_to_all | solution.py:447
  95.0 0.0 copy-done.1
  95.0 3.3 %last.1 = (bf16[512,1024]{1,0:T(8,128)(2,1)}, bf16[512,1024]{1,0:T(8,128)(2,1)}) custom-call(bf16[512,512]{1,0:T(8,128)(2,1)} %get-tuple-element.47.refs_0_.ak0_hbm, bf16[512,512]{1,0:T(8,128)(2,1)} %get-tuple-element.49.ak1_hbm, bf16[512,512]{1,0:T(8,128)(2,1)} %get-tuple-element.50.av0_hbm, bf16[512,512]{1,0:T(8,128)(2,1)} %get-tuple-element.51.av1_hbm, ...), custom_call_target="tpu_custom_call" | custom-call | flops 268435456 | bytes 8388608 | tf_op jit(solution)/shard_map/last/pallas_call | solution.py:574
  (5 shorter events, 0.0 us)
Async XLA Ops:
  0.6 14.6 %copy-start.3 = (bf16[64,8192]{1,0:T(8,128)(2,1)S(1)}, bf16[64,8192]{1,0:T(8,128)(2,1)}, u32[]{:S(2)}) copy-start(bf16[64,8192]{1,0:T(8,128)(2,1)} %refs_5_.1) | copy-start | bytes 3145732
  0.6 14.6 %copy-start.2 = (bf16[64,8192]{1,0:T(8,128)(2,1)S(1)}, bf16[64,8192]{1,0:T(8,128)(2,1)}, u32[]{:S(2)}) copy-start(bf16[64,8192]{1,0:T(8,128)(2,1)} %refs_4_.1) | copy-start | bytes 3145732
  0.7 14.6 %copy-start.5 = (f32[8192]{0:T(1024)S(1)}, f32[8192]{0:T(1024)}, u32[]{:S(2)}) copy-start(f32[8192]{0:T(1024)} %param.10) | copy-start | bytes 98308
  3.8 23.7 %all-to-all-start = ((bf16[32,32,128]{2,1,0:T(8,128)(2,1)}), bf16[32,32,128]{2,1,0:T(8,128)(2,1)S(1)}, u32[]{:S(2)}, u32[]{:S(2)}) async-start(bf16[32,32,128]{2,1,0:T(8,128)(2,1)} %bitcast), calls=%async_computation | async-start | bytes 524288 | tf_op jit(solution)/shard_map/all_to_all | solution.py:447
  15.8 19.6 %copy-start.4 = (bf16[2,64,1024]{2,1,0:T(8,128)(2,1)}, bf16[2,64,1024]{2,1,0:T(8,128)(2,1)S(1)}, u32[]{:S(2)}) copy-start(bf16[2,64,1024]{2,1,0:T(8,128)(2,1)S(1)} %get-tuple-element.32.refs_0_.refs_4_) | copy-start | bytes 786436
  15.8 19.7 %collective-permute-start = (bf16[2,64,1024]{2,1,0:T(8,128)(2,1)S(1)}, bf16[2,64,1024]{2,1,0:T(8,128)(2,1)S(1)}, u32[]{:S(2)}, u32[]{:S(2)}) collective-permute-start(bf16[2,64,1024]{2,1,0:T(8,128)(2,1)S(1)} %get-tuple-element.33), channel_id=1, source_target_pairs={{0,2},{1,3},{2,4},{3,5},{4,6},{5,7},{6,0},{7,1},{8,10},{9,11},{10,... | collective-permute-start | bytes 786440 | tf_op jit(solution)/shard_map/ppermute | solution.py:54
  17.4 18.6 %collective-permute-start.1 = (bf16[2,64,1024]{2,1,0:T(8,128)(2,1)S(1)}, bf16[2,64,1024]{2,1,0:T(8,128)(2,1)S(1)}, u32[]{:S(2)}, u32[]{:S(2)}) collective-permute-start(bf16[2,64,1024]{2,1,0:T(8,128)(2,1)S(1)} %get-tuple-element.34), channel_id=1, source_target_pairs={{0,4},{1,5},{2,6},{3,7},{4,0},{5,1},{6,2},{7,3},{8,12},{9,13},{10,... | collective-permute-start | bytes 786440 | tf_op jit(solution)/shard_map/ppermute | solution.py:54
  20.1 16.0 %collective-permute-start.2 = (bf16[2,64,1024]{2,1,0:T(8,128)(2,1)S(1)}, bf16[2,64,1024]{2,1,0:T(8,128)(2,1)S(1)}, u32[]{:S(2)}, u32[]{:S(2)}) collective-permute-start(bf16[2,64,1024]{2,1,0:T(8,128)(2,1)S(1)} %get-tuple-element.35), channel_id=1, source_target_pairs={{0,6},{1,7},{2,0},{3,1},{4,2},{5,3},{6,4},{7,5},{8,14},{9,15},{10,... | collective-permute-start | bytes 786440 | tf_op jit(solution)/shard_map/ppermute | solution.py:54
  28.3 18.3 %all-to-all-start.1 = ((bf16[32,32,128]{2,1,0:T(8,128)(2,1)}), bf16[32,32,128]{2,1,0:T(8,128)(2,1)S(1)}, u32[]{:S(2)}, u32[]{:S(2)}) async-start(bf16[32,32,128]{2,1,0:T(8,128)(2,1)} %running.2.refs_0_), calls=%async_computation.1 | async-start | bytes 524288 | tf_op jit(solution)/shard_map/all_to_all | solution.py:447
  35.4 4.7 %collective-permute-start.3 = (bf16[2,64,1024]{2,1,0:T(8,128)(2,1)S(1)}, bf16[2,64,1024]{2,1,0:T(8,128)(2,1)S(1)}, u32[]{:S(2)}, u32[]{:S(2)}) collective-permute-start(bf16[2,64,1024]{2,1,0:T(8,128)(2,1)S(1)} %get-tuple-element.32.refs_0_.refs_4_), channel_id=1, source_target_pairs={{0,1},{1,0},{2,3},{3,2},{4,5},{5,4},{6,7},{7,6},{8,9},{9,8},{10,11... | collective-permute-start | bytes 786440 | tf_op jit(solution)/shard_map/ppermute | solution.py:62
  35.5 1.0 %copy-start.6 = (bf16[2,64,1024]{2,1,0:T(8,128)(2,1)}, bf16[2,64,1024]{2,1,0:T(8,128)(2,1)S(1)}, u32[]{:S(2)}) copy-start(bf16[2,64,1024]{2,1,0:T(8,128)(2,1)S(1)} %collective-permute-done.refs_1_.refs_5_) | copy-start | bytes 786436
  35.5 4.6 %collective-permute-start.4 = (bf16[2,64,1024]{2,1,0:T(8,128)(2,1)S(1)}, bf16[2,64,1024]{2,1,0:T(8,128)(2,1)S(1)}, u32[]{:S(2)}, u32[]{:S(2)}) collective-permute-start(bf16[2,64,1024]{2,1,0:T(8,128)(2,1)S(1)} %collective-permute-done.refs_1_.refs_5_), channel_id=1, source_target_pairs={{0,1},{1,0},{2,3},{3,2},{4,5},{5,4},{6,7},{7,6},{8,9},{9,8},{10,11... | collective-permute-start | bytes 786440 | tf_op jit(solution)/shard_map/ppermute | solution.py:62
  36.0 0.7 copy-start.7
  36.0 4.2 %collective-permute-start.5 = (bf16[2,64,1024]{2,1,0:T(8,128)(2,1)S(1)}, bf16[2,64,1024]{2,1,0:T(8,128)(2,1)S(1)}, u32[]{:S(2)}, u32[]{:S(2)}) collective-permute-start(bf16[2,64,1024]{2,1,0:T(8,128)(2,1)S(1)} %collective-permute-done.1.refs_2_.refs_6_), channel_id=1, source_target_pairs={{0,1},{1,0},{2,3},{3,2},{4,5},{5,4},{6,7},{7,6},{8,9},{9,8},{10,11... | collective-permute-start | bytes 786440 | tf_op jit(solution)/shard_map/ppermute | solution.py:62
  36.1 0.7 copy-start.8
  36.1 4.1 %collective-permute-start.6 = (bf16[2,64,1024]{2,1,0:T(8,128)(2,1)S(1)}, bf16[2,64,1024]{2,1,0:T(8,128)(2,1)S(1)}, u32[]{:S(2)}, u32[]{:S(2)}) collective-permute-start(bf16[2,64,1024]{2,1,0:T(8,128)(2,1)S(1)} %collective-permute-done.2.refs_3_.refs_7_), channel_id=1, source_target_pairs={{0,1},{1,0},{2,3},{3,2},{4,5},{5,4},{6,7},{7,6},{8,9},{9,8},{10,11... | collective-permute-start | bytes 786440 | tf_op jit(solution)/shard_map/ppermute | solution.py:62
  40.2 6.4 %copy-start.9 = (bf16[2,64,1024]{2,1,0:T(8,128)(2,1)}, bf16[2,64,1024]{2,1,0:T(8,128)(2,1)S(1)}, u32[]{:S(2)}) copy-start(bf16[2,64,1024]{2,1,0:T(8,128)(2,1)S(1)} %collective-permute-done.3.refs_8_) | copy-start | bytes 786436
  40.2 6.3 %copy-start.10 = (bf16[2,64,1024]{2,1,0:T(8,128)(2,1)}, bf16[2,64,1024]{2,1,0:T(8,128)(2,1)S(1)}, u32[]{:S(2)}) copy-start(bf16[2,64,1024]{2,1,0:T(8,128)(2,1)S(1)} %collective-permute-done.4.refs_9_) | copy-start | bytes 786436
  40.2 6.3 %copy-start.11 = (bf16[2,64,1024]{2,1,0:T(8,128)(2,1)}, bf16[2,64,1024]{2,1,0:T(8,128)(2,1)S(1)}, u32[]{:S(2)}) copy-start(bf16[2,64,1024]{2,1,0:T(8,128)(2,1)S(1)} %collective-permute-done.5.refs_10_) | copy-start | bytes 786436
  40.2 6.3 %copy-start.12 = (bf16[2,64,1024]{2,1,0:T(8,128)(2,1)}, bf16[2,64,1024]{2,1,0:T(8,128)(2,1)S(1)}, u32[]{:S(2)}) copy-start(bf16[2,64,1024]{2,1,0:T(8,128)(2,1)S(1)} %collective-permute-done.6.refs_11_) | copy-start | bytes 786436
  49.6 7.9 %collective-permute-start.7 = (bf16[4,64,1024]{2,1,0:T(8,128)(2,1)}, bf16[4,64,1024]{2,1,0:T(8,128)(2,1)S(1)}, u32[]{:S(2)}, u32[]{:S(2)}) collective-permute-start(bf16[4,64,1024]{2,1,0:T(8,128)(2,1)} %get-tuple-element.41), channel_id=1, source_target_pairs={{0,1},{1,0},{2,3},{3,2},{4,5},{5,4},{6,7},{7,6},{8,9},{9,8},{10,11... | collective-permute-start | bytes 1572872 | tf_op jit(solution)/shard_map/ppermute | solution.py:522
  60.3 17.0 %all-to-all-start.3 = ((bf16[32,32,128]{2,1,0:T(8,128)(2,1)}), bf16[32,32,128]{2,1,0:T(8,128)(2,1)S(1)}, u32[]{:S(2)}, u32[]{:S(2)}) async-start(bf16[32,32,128]{2,1,0:T(8,128)(2,1)} %bitcast.3), calls=%async_computation.3 | async-start | bytes 524288 | tf_op jit(solution)/shard_map/all_to_all | solution.py:447
  65.1 18.7 %collective-permute-start.8 = (bf16[2,64,1024]{2,1,0:T(8,128)(2,1)}, bf16[2,64,1024]{2,1,0:T(8,128)(2,1)S(1)}, u32[]{:S(2)}, u32[]{:S(2)}) collective-permute-start(bf16[2,64,1024]{2,1,0:T(8,128)(2,1)} %get-tuple-element.55), channel_id=1, source_target_pairs={{0,2},{1,3},{2,4},{3,5},{4,6},{5,7},{6,0},{7,1},{8,10},{9,11},{10,... | collective-permute-start | bytes 786440 | tf_op jit(solution)/shard_map/ppermute | solution.py:54
  65.7 18.1 %collective-permute-start.9 = (bf16[2,64,1024]{2,1,0:T(8,128)(2,1)}, bf16[2,64,1024]{2,1,0:T(8,128)(2,1)S(1)}, u32[]{:S(2)}, u32[]{:S(2)}) collective-permute-start(bf16[2,64,1024]{2,1,0:T(8,128)(2,1)} %get-tuple-element.56), channel_id=1, source_target_pairs={{0,4},{1,5},{2,6},{3,7},{4,0},{5,1},{6,2},{7,3},{8,12},{9,13},{10,... | collective-permute-start | bytes 786440 | tf_op jit(solution)/shard_map/ppermute | solution.py:54
  67.8 16.1 %collective-permute-start.10 = (bf16[2,64,1024]{2,1,0:T(8,128)(2,1)}, bf16[2,64,1024]{2,1,0:T(8,128)(2,1)S(1)}, u32[]{:S(2)}, u32[]{:S(2)}) collective-permute-start(bf16[2,64,1024]{2,1,0:T(8,128)(2,1)} %get-tuple-element.57), channel_id=1, source_target_pairs={{0,6},{1,7},{2,0},{3,1},{4,2},{5,3},{6,4},{7,5},{8,14},{9,15},{10,... | collective-permute-start | bytes 786440 | tf_op jit(solution)/shard_map/ppermute | solution.py:54
  78.1 16.9 %all-to-all-start.4 = ((bf16[32,32,128]{2,1,0:T(8,128)(2,1)}), bf16[32,32,128]{2,1,0:T(8,128)(2,1)S(1)}, u32[]{:S(2)}, u32[]{:S(2)}) async-start(bf16[32,32,128]{2,1,0:T(8,128)(2,1)} %running.3.refs_1_), calls=%async_computation.4 | async-start | bytes 524288 | tf_op jit(solution)/shard_map/all_to_all | solution.py:447
  87.9 7.1 %copy-start = (bf16[512,1024]{1,0:T(8,128)(2,1)S(1)}, bf16[512,1024]{1,0:T(8,128)(2,1)}, u32[]{:S(2)}) copy-start(bf16[512,1024]{1,0:T(8,128)(2,1)} %k_ref.1) | copy-start | bytes 3145732
  87.9 7.1 %copy-start.1 = (bf16[512,1024]{1,0:T(8,128)(2,1)S(1)}, bf16[512,1024]{1,0:T(8,128)(2,1)}, u32[]{:S(2)}) copy-start(bf16[512,1024]{1,0:T(8,128)(2,1)} %v_ref.1) | copy-start | bytes 3145732
